TPU v7x, 32 devices: a whole 2x2x4 slice. The times are simulated.
32 devices in a mesh: dp: 2 (over core), seq: 4 (over y, x), fsdp: 4 (over z).
Axes of the slice: x: 2, y: 2, z: 4, core: 2. Of those that a mesh axis runs over, the one named last changes fastest.
Arguments:
- image_tokens: bfloat16 [4, 16, 196, 768], P('dp', 'fsdp', 'seq'), may hold values from -6 to 6
- slot_window: int32 [16], P('fsdp'), may hold values from 0 to 15, as said below
- first_gain: float32 [768], replicated, may hold values from 0.5 to 1.5
- first_bias: float32 [768], replicated, may hold values from -1.2 to 1.2
- qkv_weight: bfloat16 [768, 2304], P('fsdp'), may hold values from -0.21875 to 0.21875
- qkv_bias: float32 [2304], replicated, may hold values from -1.2 to 1.2
- rel_height: bfloat16 [27, 64], replicated, may hold values from -0.75 to 0.75
- rel_width: bfloat16 [27, 64], replicated, may hold values from -0.75 to 0.75
- proj_weight: bfloat16 [768, 768], P('fsdp'), may hold values from -0.875 to 0.875
- proj_bias: float32 [768], replicated, may hold values from -1.2 to 1.2
- second_gain: float32 [768], replicated, may hold values from 0.5 to 1.5
- second_bias: float32 [768], replicated, may hold values from -1.2 to 1.2
- hidden_weight: bfloat16 [768, 3072], P('fsdp'), may hold values from -0.21875 to 0.21875
- hidden_bias: float32 [3072], replicated, may hold values from -1.2 to 1.2
- output_weight: bfloat16 [3072, 768], P('fsdp'), may hold values from -0.109375 to 0.109375
- output_bias: float32 [768], replicated, may hold values from -1.2 to 1.2
- cotangent: bfloat16 [4, 16, 196, 768], P('dp', 'fsdp', 'seq'), may hold values from -6 to 6
Outputs:
- block_out: bfloat16 [4, 16, 196, 768], P('dp', 'fsdp', 'seq')
- input_grad: bfloat16 [4, 16, 196, 768], P('dp', 'fsdp', 'seq')
- first_gain_grad: float32 [768], replicated
- first_bias_grad: float32 [768], replicated
- qkv_weight_grad: float32 [768, 2304], P(('dp', 'seq', 'fsdp'))
- qkv_bias_grad: float32 [2304], replicated
- rel_height_grad: float32 [27, 64], replicated
- rel_width_grad: float32 [27, 64], replicated
- proj_weight_grad: float32 [768, 768], P(('dp', 'seq', 'fsdp'))
- proj_bias_grad: float32 [768], replicated
- second_gain_grad: float32 [768], replicated
- second_bias_grad: float32 [768], replicated
- hidden_weight_grad: float32 [768, 3072], P(('dp', 'seq', 'fsdp'))
- hidden_bias_grad: float32 [3072], replicated
- output_weight_grad: float32 [3072, 768], P(None, ('dp', 'seq', 'fsdp'))
- output_bias_grad: float32 [768], replicated
Inputs may be any that keep to these rules, and one draw needn't show every extreme that they name: `slot_window`: each window number 0 to 15 stands in exactly one slot; any other slots hold -1.
All inputs are finite; a program needn't handle non-finite values.
Results may differ from a plain program's by a relative error of at most 0.012.
Values may be sent and summed in bfloat16 or wider, within the bound.
No kernel may reach another device: no remote copies, remote signals or barrier semaphores. Data moves between devices by JAX's collectives and lax.ppermute only.
A program may use at most 256 MiB of HBM per device.

v0:
```python
import jax
import jax.numpy as jnp
from jax import lax
from jax.sharding import PartitionSpec as P

HEADS = 12
HD = 64
WIN = 14
GRID = 48
NWS = 4


def exact_einsum(form, left, right):
    return jnp.einsum(
        form, left, right, preferred_element_type=jnp.float32, precision=lax.Precision.HIGHEST
    )


def layer_norm(values, gain, shift):
    centre = values - jnp.mean(values, axis=-1, keepdims=True)
    spread = jnp.mean(centre * centre, axis=-1, keepdims=True)
    return centre * lax.rsqrt(spread + 1e-06) * gain + shift


def exact_gelu(values):
    return jax.nn.gelu(values, approximate=False)


def offset_table():
    offsets = jnp.arange(WIN)[:, None] - jnp.arange(WIN)[None, :] + WIN - 1
    return (offsets[:, :, None] == jnp.arange(2 * WIN - 1)[None, None, :]).astype(jnp.float32)


def scores_of(query_part, key_part, height_table, width_table):
    count, _, heads_here, head_size = query_part.shape
    grid_query = query_part.reshape(count, WIN, WIN, heads_here, head_size)
    height_terms = jnp.einsum(
        "nrchd,rkd->nhrck", grid_query, height_table, preferred_element_type=jnp.float32
    )
    width_terms = jnp.einsum(
        "nrchd,ckd->nhrck", grid_query, width_table, preferred_element_type=jnp.float32
    )
    rel_terms = (height_terms[..., :, None] + width_terms[..., None, :]).reshape(
        count, heads_here, WIN * WIN, WIN * WIN
    )
    dots = jnp.einsum("nqhd,nkhd->nhqk", query_part, key_part, preferred_element_type=jnp.float32)
    return head_size ** (-0.5) * dots + rel_terms


def attend_back(received, log_total, grad_heads, height_table, width_table, positions_table):
    query_part = received[:, :, 0]
    key_part = received[:, :, 1]
    value_part = received[:, :, 2]
    count, _, heads_here, head_size = query_part.shape
    scale_factor = head_size ** (-0.5)
    scores = scores_of(query_part, key_part, height_table, width_table)
    soft_exact = jnp.exp(scores - log_total[..., None])
    soft_low = soft_exact.astype(jnp.bfloat16)
    grad_value = jnp.einsum(
        "nhqk,nqhd->nkhd", soft_low, grad_heads, preferred_element_type=jnp.float32
    )
    grad_soft = jnp.einsum(
        "nqhd,nkhd->nhqk", grad_heads, value_part, preferred_element_type=jnp.float32
    )
    grad_scores = (
        soft_exact * (grad_soft - jnp.sum(grad_soft * soft_exact, axis=-1, keepdims=True))
    ).astype(jnp.bfloat16)
    grad_query = scale_factor * jnp.einsum(
        "nhqk,nkhd->nqhd", grad_scores, key_part, preferred_element_type=jnp.float32
    )
    grad_key = scale_factor * jnp.einsum(
        "nhqk,nqhd->nkhd", grad_scores, query_part, preferred_element_type=jnp.float32
    )
    grid_grads = grad_scores.reshape(count, heads_here, WIN, WIN, WIN, WIN)
    height_grads = jnp.sum(grid_grads, axis=5, dtype=jnp.float32)
    width_grads = jnp.sum(grid_grads, axis=4, dtype=jnp.float32)
    grid_query = query_part.astype(jnp.float32).reshape(count, WIN, WIN, heads_here, head_size)
    rel_query = exact_einsum("nhrck,rkd->nrchd", height_grads, height_table.astype(jnp.float32))
    rel_query = rel_query + exact_einsum(
        "nhrck,ckd->nrchd", width_grads, width_table.astype(jnp.float32)
    )
    grad_query = grad_query + rel_query.reshape(count, WIN * WIN, heads_here, head_size)
    height_pairs = exact_einsum("nhrck,nrchd->rkd", height_grads, grid_query)
    width_pairs = exact_einsum("nhrck,nrchd->ckd", width_grads, grid_query)
    grad_height = exact_einsum("abk,abd->kd", positions_table, height_pairs)
    grad_width = exact_einsum("abk,abd->kd", positions_table, width_pairs)
    grad_packed = jnp.stack([grad_query, grad_key, grad_value], axis=2).astype(jnp.bfloat16)
    return (grad_packed, grad_height, grad_width)


def per_device(
    image_tokens,
    slot_window,
    first_gain,
    first_bias,
    qkv_weight,
    qkv_bias,
    rel_height,
    rel_width,
    proj_weight,
    proj_bias,
    second_gain,
    second_bias,
    hidden_weight,
    hidden_bias,
    output_weight,
    output_bias,
    cotangent,
):
    micro_count, slots_here, tok_here, features = image_tokens.shape
    total_rows = slots_here * tok_here
    positions = lax.axis_index("seq") * tok_here + jnp.arange(tok_here)
    window_ids = slot_window[:, None]
    row_ok = window_ids // NWS * WIN + positions[None, :] // WIN < GRID
    col_ok = window_ids % NWS * WIN + positions[None, :] % WIN < GRID
    valid_mask = ((window_ids >= 0) & row_ok & col_ok).astype(jnp.float32).reshape(total_rows, 1)
    positions_table = offset_table()
    height_table = exact_einsum(
        "abk,kd->abd", positions_table, rel_height.astype(jnp.float32)
    ).astype(jnp.bfloat16)
    width_table = exact_einsum(
        "abk,kd->abd", positions_table, rel_width.astype(jnp.float32)
    ).astype(jnp.bfloat16)
    outputs = []
    input_grads = []
    small_sums = None
    large_sums = None
    for index in range(micro_count):
        gathered = (
            lax.all_gather(qkv_weight, "fsdp", axis=0, tiled=True),
            lax.all_gather(proj_weight, "fsdp", axis=0, tiled=True),
            lax.all_gather(hidden_weight, "fsdp", axis=0, tiled=True),
            lax.all_gather(output_weight, "fsdp", axis=0, tiled=True),
        )
        w_qkv, w_proj, w_hidden, w_output = gathered
        tokens_f = image_tokens[index].reshape(total_rows, features).astype(jnp.float32)
        normed_f, first_back = jax.vjp(
            lambda values, gain, shift: layer_norm(values, gain, shift) * valid_mask,
            tokens_f,
            first_gain,
            first_bias,
        )
        normed = normed_f.astype(jnp.bfloat16)
        packed = (jnp.dot(normed, w_qkv, preferred_element_type=jnp.float32) + qkv_bias).astype(
            jnp.bfloat16
        )
        packed = packed.reshape(slots_here, tok_here, 3, HEADS, HD)
        received = lax.all_to_all(packed, "seq", split_axis=3, concat_axis=1, tiled=True)
        query_part = received[:, :, 0]
        key_part = received[:, :, 1]
        value_part = received[:, :, 2]
        scores = scores_of(query_part, key_part, height_table, width_table)
        row_max = jnp.max(scores, axis=-1, keepdims=True)
        exp_scores = jnp.exp(scores - row_max)
        row_total = jnp.sum(exp_scores, axis=-1, keepdims=True)
        soft_low = (exp_scores / row_total).astype(jnp.bfloat16)
        log_total = (row_max + jnp.log(row_total))[..., 0]
        attended_h = jnp.einsum(
            "nhqk,nkhd->nqhd", soft_low, value_part, preferred_element_type=jnp.float32
        ).astype(jnp.bfloat16)
        attended_h, log_total, received = (attended_h, log_total, received)
        attended = lax.all_to_all(
            attended_h, "seq", split_axis=1, concat_axis=2, tiled=True
        ).reshape(total_rows, features)
        middle = (
            tokens_f + jnp.dot(attended, w_proj, preferred_element_type=jnp.float32) + proj_bias
        )
        second_f, second_back = jax.vjp(layer_norm, middle, second_gain, second_bias)
        second = second_f.astype(jnp.bfloat16)
        pre_act = jnp.dot(second, w_hidden, preferred_element_type=jnp.float32) + hidden_bias
        active_f, gelu_back = jax.vjp(exact_gelu, pre_act)
        active = active_f.astype(jnp.bfloat16)
        feed_out = jnp.dot(active, w_output, preferred_element_type=jnp.float32) + output_bias
        outputs.append(
            ((middle + feed_out) * valid_mask)
            .astype(jnp.bfloat16)
            .reshape(slots_here, tok_here, features)
        )
        grad_out = cotangent[index].reshape(total_rows, features).astype(jnp.float32) * valid_mask
        grad_feed = grad_out.astype(jnp.bfloat16)
        grad_w_output = jnp.einsum(
            "rf,rd->fd", active, grad_feed, preferred_element_type=jnp.float32
        )
        grad_active = jnp.einsum(
            "rd,fd->rf", grad_feed, w_output, preferred_element_type=jnp.float32
        )
        grad_pre = gelu_back(grad_active)[0].astype(jnp.bfloat16)
        grad_w_hidden = jnp.einsum(
            "rd,rf->df", second, grad_pre, preferred_element_type=jnp.float32
        )
        grad_second = jnp.einsum(
            "rf,df->rd", grad_pre, w_hidden, preferred_element_type=jnp.float32
        )
        grad_mid_norm, grad_gain_two, grad_bias_two = second_back(grad_second)
        grad_middle = grad_out + grad_mid_norm
        grad_branch = grad_middle.astype(jnp.bfloat16)
        grad_w_proj = jnp.einsum(
            "rd,re->de", attended, grad_branch, preferred_element_type=jnp.float32
        )
        grad_attended = jnp.einsum(
            "re,de->rd", grad_branch, w_proj, preferred_element_type=jnp.float32
        ).astype(jnp.bfloat16)
        grad_attended = grad_attended.reshape(slots_here, tok_here, HEADS, HD)
        grad_heads = lax.all_to_all(grad_attended, "seq", split_axis=2, concat_axis=1, tiled=True)
        grad_packed_h, grad_height, grad_width = attend_back(
            received, log_total, grad_heads, height_table, width_table, positions_table
        )
        grad_packed = lax.all_to_all(
            grad_packed_h, "seq", split_axis=1, concat_axis=3, tiled=True
        ).reshape(total_rows, 3 * features)
        grad_w_qkv = jnp.einsum(
            "rd,re->de", normed, grad_packed, preferred_element_type=jnp.float32
        )
        grad_normed = jnp.einsum(
            "re,de->rd", grad_packed, w_qkv, preferred_element_type=jnp.float32
        )
        grad_tok_norm, grad_gain_one, grad_bias_one = first_back(grad_normed)
        input_grads.append(
            (grad_middle + grad_tok_norm)
            .astype(jnp.bfloat16)
            .reshape(slots_here, tok_here, features)
        )
        small_terms = (
            grad_gain_one,
            grad_bias_one,
            jnp.sum(grad_packed.astype(jnp.float32), axis=0),
            grad_height,
            grad_width,
            jnp.sum(grad_branch.astype(jnp.float32), axis=0),
            grad_gain_two,
            grad_bias_two,
            jnp.sum(grad_pre.astype(jnp.float32), axis=0),
            jnp.sum(grad_feed.astype(jnp.float32), axis=0),
        )
        small_sums = (
            small_terms
            if small_sums is None
            else jax.tree.map(lambda left, right: left + right, small_sums, small_terms)
        )
        large_terms = (grad_w_qkv, grad_w_proj, grad_w_hidden, grad_w_output)
        large_sums = (
            large_terms
            if large_sums is None
            else jax.tree.map(lambda left, right: left + right, large_sums, large_terms)
        )
    large_sums = (
        lax.psum_scatter(large_sums[0], ("dp", "seq", "fsdp"), scatter_dimension=0, tiled=True),
        lax.psum_scatter(large_sums[1], ("dp", "seq", "fsdp"), scatter_dimension=0, tiled=True),
        lax.psum_scatter(large_sums[2], ("dp", "seq", "fsdp"), scatter_dimension=0, tiled=True),
        lax.psum_scatter(large_sums[3], ("dp", "seq", "fsdp"), scatter_dimension=1, tiled=True),
    )
    small_sums = lax.psum(small_sums, ("dp", "seq", "fsdp"))
    block_out = jnp.stack(outputs, axis=0)
    input_grad = jnp.stack(input_grads, axis=0)
    return (
        block_out,
        input_grad,
        small_sums[0],
        small_sums[1],
        large_sums[0],
        small_sums[2],
        small_sums[3],
        small_sums[4],
        large_sums[1],
        small_sums[5],
        small_sums[6],
        small_sums[7],
        large_sums[2],
        small_sums[8],
        large_sums[3],
        small_sums[9],
    )


def solution(mesh):
    placed = (
        P("dp", "fsdp", "seq", None),
        P("fsdp"),
        P(),
        P(),
        P("fsdp", None),
        P(),
        P(),
        P(),
        P("fsdp", None),
        P(),
        P(),
        P(),
        P("fsdp", None),
        P(),
        P("fsdp", None),
        P(),
        P("dp", "fsdp", "seq", None),
    )
    return jax.shard_map(
        per_device,
        mesh=mesh,
        in_specs=placed,
        out_specs=(
            P("dp", "fsdp", "seq", None),
            P("dp", "fsdp", "seq", None),
            P(),
            P(),
            P(("dp", "seq", "fsdp"), None),
            P(),
            P(),
            P(),
            P(("dp", "seq", "fsdp"), None),
            P(),
            P(),
            P(),
            P(("dp", "seq", "fsdp"), None),
            P(),
            P(None, ("dp", "seq", "fsdp")),
            P(),
        ),
        check_vma=False,
    )
```

profile of v0, /device:TPU:0, one launch (start us, length us, event | category | flops | bytes accessed | tf_op | source)
XLA Modules:
  0.0 920.2 jit_solution(660363463687802984)
XLA Ops:
  15.1 67.2 %all-gather.5.cloned.1.call-done = bf16[768,2304]{1,0:T(8,128)(2,1)} async-done(((bf16[192,2304]{1,0:T(8,128)(2,1)}), bf16[768,2304]{1,0:T(8,128)(2,1)}) %all-gather.5.cloned.1.call-update) | async-done | bytes 3538960 | tf_op jit(solution)/shard_map/all_gather | solution.py:130
  88.8 5.0 reshape.519
  93.8 3.8 all-to-all-start
  99.4 4.1 fusion.1
  108.5 4.9 reshape.525
  113.4 4.6 all-to-all-start.2
  121.8 3.8 reshape.520
  125.6 5.9 copy.412
  141.3 4.1 reshape.526
  145.5 5.1 copy.414
  160.7 3.9 copy.308
  166.8 3.9 copy.328
  173.0 8.6 broadcast_add_fusion
  181.6 12.7 %add.447 = f32[4,3,196,196]{3,2,1,0:T(8,128)} reshape(f32[4,3,14,14,14,14]{5,4,3,2,1,0:T(8,128)} %broadcast_add_fusion) | data formatting | bytes 3687936 | tf_op jit(solution)/shard_map/add | solution.py:43
  207.5 4.2 all-to-all-start.3
  211.7 7.6 broadcast_add_fusion.1
  219.3 11.5 %add.427 = f32[4,3,196,196]{3,2,1,0:T(8,128)S(1)} reshape(f32[4,3,14,14,14,14]{5,4,3,2,1,0:T(8,128)} %broadcast_add_fusion.1) | data formatting | bytes 3687936 | tf_op jit(solution)/shard_map/add | solution.py:43
  241.1 4.2 all-to-all-start.1
  261.0 9.7 %multiply_convert_fusion.2 = (bf16[196,3072]{1,0:T(8,128)(2,1)}, f32[196,3072]{1,0:T(8,128)}, f32[196,3072]{1,0:T(8,128)}) fusion(f32[3072]{0:T(1024)S(1)} %copy-done.112, bf16[768,3072]{1,0:T(8,128)(2,1)} %all-gather.9.cloned.1.call-done, f32[196,768]{1,0:T(8,128)S(1)} %get-tuple-element.157, f32[196]{0:T(256)S(1)} %fusion.118, ...), kind=kOutput, calls=%fused_computation.27 | convolution fusion | flops 965336064 | bytes 11361824 | tf_op jit(solution)/shard_map/dot_general | solution.py:170
  270.7 21.8 %all-gather.11.cloned.1.call-done = bf16[3072,768]{1,0:T(8,128)(2,1)} async-done(((bf16[768,768]{1,0:T(8,128)(2,1)}), bf16[3072,768]{1,0:T(8,128)(2,1)}) %all-gather.11.cloned.1.call-update) | async-done | bytes 4718608 | tf_op jit(solution)/shard_map/all_gather | solution.py:133
  292.4 6.7 convert_reduce_fusion.2
  301.9 7.2 multiply_convert_fusion.3
  326.5 4.1 all-to-all-start.6
  345.6 4.1 all-to-all-start.4
  382.5 12.8 %reshape.502 = f32[4,3,14,14,14,14]{5,4,3,2,1,0:T(8,128)} reshape(f32[4,3,196,196]{3,2,1,0:T(8,128)} %copy.339) | data formatting | bytes 3687936 | tf_op jit(solution)/shard_map/convert_element_type | solution.py:75
  395.3 12.7 %reshape.504 = f32[4,3,14,14,14,14]{5,4,3,2,1,0:T(8,128)} reshape(f32[4,3,196,196]{3,2,1,0:T(8,128)} %copy.355) | data formatting | bytes 3687936 | tf_op jit(solution)/shard_map/convert_element_type | solution.py:75
  408.0 18.4 %fusion.137 = (f32[4,3,14,14,14]{4,3,2,1,0:T(8,128)}, f32[4,3,14,14,14]{4,3,2,1,0:T(8,128)}, f32[4,3,14,14,14]{4,3,2,1,0:T(8,128)S(1)}, f32[4,3,14,14,14]{4,3,2,1,0:T(8,128)S(1)}) fusion(f32[4,3,14,14,14,14]{5,4,3,2,1,0:T(8,128)} %reshape.502, f32[4,3,14,14,14,14]{5,4,3,2,1,0:T(8,128)} %reshape.504), kind=kLoop, calls=%fused_computation.278 | loop fusion | flops 1712256 | bytes 4214784 | tf_op jit(solution)/shard_map/reduce_sum | solution.py:75
  436.1 5.0 copy.363
  441.2 4.8 reshape.531
  446.0 4.3 all-to-all-start.7
  464.3 4.4 copy.347
  472.2 4.2 all-to-all-start.5
  479.1 4.3 reshape.532
  485.8 5.1 reshape.497
  491.0 5.1 reshape.534
  496.0 3.9 copy.349
  499.9 5.1 reshape.494
  507.4 4.1 convolution_add_fusion
  515.4 5.3 convolution_add_fusion.2
  524.5 5.3 convolution_add_fusion.1
  530.4 4.0 fusion.52
  534.6 4.2 fusion.53
  547.7 5.2 copy.408
  552.9 7.1 copy.405
  571.5 41.8 %all-reduce = (f32[768]{0:T(1024)}, f32[768]{0:T(1024)}, f32[2304]{0:T(1024)}, f32[27,64]{1,0:T(8,128)}, f32[27,64]{1,0:T(8,128)}, /*index=5*/f32[768]{0:T(1024)...) all-reduce(f32[768]{0:T(1024)S(1)} %add.466, ...), channel_id=1, replica_groups=mesh['dp'=2,'seq'=4,'fsdp'=4] {'dp','seq','fsdp'}, use_global_device_ids=true, to_apply=%region_28.29 | all-reduce | flops 13440 | bytes 107520 | tf_op jit(solution)/shard_map/psum | solution.py:252
  613.2 16.8 %reduce-scatter.5.cloned.1.call-done = f32[24,2304]{1,0:T(8,128)} async-done(((f32[768,2304]{1,0:T(8,128)}), f32[24,2304]{1,0:T(8,128)}) %reduce-scatter.5.cloned.1.call-update) | async-done | bytes 221200 | tf_op jit(solution)/shard_map/reduce_scatter | solution.py:247
  630.0 141.2 %reduce-scatter.9.cloned.1.call-done = f32[24,3072]{1,0:T(8,128)} async-done(((f32[768,3072]{1,0:T(8,128)}), f32[24,3072]{1,0:T(8,128)}) %reduce-scatter.9.cloned.1.call-update) | async-done | bytes 294928 | tf_op jit(solution)/shard_map/reduce_scatter | solution.py:249
  771.3 141.9 %reduce-scatter.11.cloned.1.call-done = f32[3072,24]{0,1:T(8,128)} async-done(((f32[3072,768]{0,1:T(8,128)}), f32[3072,24]{0,1:T(8,128)}) %reduce-scatter.11.cloned.1.call-update) | async-done | bytes 294928 | tf_op jit(solution)/shard_map/reduce_scatter | solution.py:250
  (441 shorter events, 218.4 us)
Async XLA Ops:
  7.2 110.8 %copy-start = (bf16[27,64]{1,0:T(8,128)(2,1)S(1)}, bf16[27,64]{1,0:T(8,128)(2,1)}, u32[]{:S(2)}) copy-start(bf16[27,64]{1,0:T(8,128)(2,1)} %param.24) | copy-start | bytes 10372
  7.2 75.1 %all-gather.5.cloned.1.call-start = ((), (), s32[]{:S(2)}) async-start(), calls=%async_computation.12 | async-start | bytes 4423680 | tf_op jit(solution)/shard_map/all_gather | solution.py:130
  8.0 247.8 %all-gather.7.cloned.1.call-start = ((), (), s32[]{:S(2)}) async-start(), calls=%async_computation.13 | async-start | bytes 1474560 | tf_op jit(solution)/shard_map/all_gather | solution.py:131
  8.7 252.2 %all-gather.9.cloned.1.call-start = ((), (), s32[]{:S(2)}) async-start(), calls=%async_computation.14 | async-start | bytes 5898240 | tf_op jit(solution)/shard_map/all_gather | solution.py:132
  9.4 283.0 %all-gather.11.cloned.1.call-start = ((), (), s32[]{:S(2)}) async-start(), calls=%async_computation.15 | async-start | bytes 5898240 | tf_op jit(solution)/shard_map/all_gather | solution.py:133
  10.4 71.9 %copy-start.80 = (f32[768]{0:T(1024)S(1)}, f32[768]{0:T(1024)}, u32[]{:S(2)}) copy-start(f32[768]{0:T(1024)} %param.19) | copy-start | bytes 9220
  10.4 71.9 %copy-start.95 = (f32[768]{0:T(1024)S(1)}, f32[768]{0:T(1024)}, u32[]{:S(2)}) copy-start(f32[768]{0:T(1024)} %param.20) | copy-start | bytes 9220
  10.4 71.9 %copy-start.111 = (f32[2304]{0:T(1024)S(1)}, f32[2304]{0:T(1024)}, u32[]{:S(2)}) copy-start(f32[2304]{0:T(1024)} %param.22) | copy-start | bytes 27652
  12.2 87.2 %copy-start.84 = (f32[196]{0:T(256)}, f32[196]{0:T(256)S(1)}, u32[]{:S(2)}) copy-start(f32[196]{0:T(256)S(1)} %reshape.499) | copy-start | bytes 2356
  12.3 70.0 %copy-start.97 = (f32[196]{0:T(256)}, f32[196]{0:T(256)S(1)}, u32[]{:S(2)}) copy-start(f32[196]{0:T(256)S(1)} %div.116) | copy-start | bytes 2356
  12.3 85.2 %copy-start.64 = (f32[4,49]{0,1:T(8,128)}, f32[4,49]{0,1:T(8,128)S(1)}, u32[]{:S(2)}) copy-start(f32[4,49]{0,1:T(8,128)S(1)} %broadcast_multiply_fusion) | copy-start | bytes 2356
  14.3 68.0 %copy-start.101 = (f32[196]{0:T(256)}, f32[196]{0:T(256)S(1)}, u32[]{:S(2)}) copy-start(f32[196]{0:T(256)S(1)} %rsqrt.46) | copy-start | bytes 2356
  15.1 67.2 %copy-start.34 = (f32[196,768]{1,0:T(8,128)}, f32[196,768]{1,0:T(8,128)S(1)}, u32[]{:S(2)}) copy-start(f32[196,768]{1,0:T(8,128)S(1)} %reshape.498) | copy-start | bytes 1806340
  88.8 9.0 copy-start.49
  93.8 19.7 %all-to-all-start = ((bf16[4,2,56448]{2,1,0:T(2,128)(2,1)}), bf16[4,2,56448]{2,1,0:T(2,128)(2,1)S(1)}, u32[]{:S(2)}, u32[]{:S(2)}) async-start(bf16[4,2,56448]{2,1,0:T(2,128)(2,1)} %reshape.519), calls=%async_computation | async-start | bytes 1806336 | tf_op jit(solution)/shard_map/all_to_all | solution.py:148
  97.6 23.4 %copy-start.69 = (s32[14,14]{1,0:T(8,128)}, s32[14,14]{1,0:T(8,128)S(1)}, u32[]{:S(2)}) copy-start(s32[14,14]{1,0:T(8,128)S(1)} %subtract_add_fusion) | copy-start | bytes 2356
  108.5 10.4 %copy-start.51 = (f32[1,4,49,768]{3,1,2,0:T(4,128)S(1)}, f32[1,4,49,768]{3,1,2,0:T(4,128)}, u32[]{:S(2)}) copy-start(f32[1,4,49,768]{3,1,2,0:T(4,128)} %get-tuple-element.130) | copy-start | bytes 1806340
  113.4 27.9 %all-to-all-start.2 = ((bf16[4,2,56448]{2,1,0:T(2,128)(2,1)}), bf16[4,2,56448]{2,1,0:T(2,128)(2,1)}, u32[]{:S(2)}, u32[]{:S(2)}) async-start(bf16[4,2,56448]{2,1,0:T(2,128)(2,1)} %reshape.525), calls=%async_computation.2 | async-start | bytes 1806336 | tf_op jit(solution)/shard_map/all_to_all | solution.py:148
  134.8 10.6 %copy-start.9 = (bf16[4,196,1,3,64]{4,0,3,1,2:T(4,128)(2,1)}, bf16[4,196,1,3,64]{4,0,3,1,2:T(4,128)(2,1)S(1)}, u32[]{:S(2)}) copy-start(bf16[4,196,1,3,64]{4,0,3,1,2:T(4,128)(2,1)S(1)} %copy.304) | copy-start | bytes 903172
  154.1 46.6 %copy-start.21 = (bf16[4,196,3,3,64]{1,4,3,0,2:T(8,128)(2,1)}, bf16[4,196,3,3,64]{1,4,3,0,2:T(8,128)(2,1)S(1)}, u32[]{:S(2)}) copy-start(bf16[4,196,3,3,64]{1,4,3,0,2:T(8,128)(2,1)S(1)} %reshape.518) | copy-start | bytes 2709508
  155.0 9.6 %copy-start.11 = (bf16[4,196,1,3,64]{4,0,3,1,2:T(4,128)(2,1)}, bf16[4,196,1,3,64]{4,0,3,1,2:T(4,128)(2,1)S(1)}, u32[]{:S(2)}) copy-start(bf16[4,196,1,3,64]{4,0,3,1,2:T(4,128)(2,1)S(1)} %copy.324) | copy-start | bytes 903172
  201.8 9.9 %copy-start.42 = (f32[4,3,14,14,14]{4,3,2,1,0:T(8,128)S(1)}, f32[4,3,14,14,14]{4,3,2,1,0:T(8,128)}, u32[]{:S(2)}) copy-start(f32[4,3,14,14,14]{4,3,2,1,0:T(8,128)} %copy.306) | copy-start | bytes 395140
  203.2 8.5 copy-start.41
  207.5 33.6 %all-to-all-start.3 = ((bf16[4,2,18816]{2,1,0:T(2,128)(2,1)}), bf16[4,2,18816]{2,1,0:T(2,128)(2,1)S(1)}, u32[]{:S(2)}, u32[]{:S(2)}) async-start(bf16[4,2,18816]{2,1,0:T(2,128)(2,1)} %reshape.527), calls=%async_computation.3 | async-start | bytes 602112 | tf_op jit(solution)/shard_map/all_to_all | solution.py:162
  241.1 9.8 %all-to-all-start.1 = ((bf16[4,2,18816]{2,1,0:T(2,128)(2,1)}), bf16[4,2,18816]{2,1,0:T(2,128)(2,1)}, u32[]{:S(2)}, u32[]{:S(2)}) async-start(bf16[4,2,18816]{2,1,0:T(2,128)(2,1)} %reshape.521), calls=%async_computation.1 | async-start | bytes 602112 | tf_op jit(solution)/shard_map/all_to_all | solution.py:162
  260.9 53.9 %copy-start.76 = (f32[196]{0:T(256)}, f32[196]{0:T(256)S(1)}, u32[]{:S(2)}) copy-start(f32[196]{0:T(256)S(1)} %fusion.118) | copy-start | bytes 2356
  260.9 53.9 %copy-start.78 = (f32[196]{0:T(256)}, f32[196]{0:T(256)S(1)}, u32[]{:S(2)}) copy-start(f32[196]{0:T(256)S(1)} %fusion.117) | copy-start | bytes 2356
  260.9 31.5 %copy-start.85 = (f32[196]{0:T(256)S(1)}, f32[196]{0:T(256)}, u32[]{:S(2)}) copy-start(f32[196]{0:T(256)} %copy-done.84) | copy-start | bytes 2356
  300.2 8.9 slice-start
  326.5 19.1 %all-to-all-start.6 = ((bf16[4,2,18816]{2,1,0:T(2,128)(2,1)}), bf16[4,2,18816]{2,1,0:T(2,128)(2,1)}, u32[]{:S(2)}, u32[]{:S(2)}) async-start(bf16[4,2,18816]{2,1,0:T(2,128)(2,1)} %reshape.529), calls=%async_computation.6 | async-start | bytes 602112 | tf_op jit(solution)/shard_map/all_to_all | solution.py:204
  330.6 282.7 %reduce-scatter.7.cloned.1.call-start = ((), (), s32[]{:S(2)}) async-start(), calls=%async_computation.17 | async-start | bytes 2433024 | tf_op jit(solution)/shard_map/reduce_scatter | solution.py:248
  333.7 8.1 copy-start.47
  345.6 23.5 %all-to-all-start.4 = ((bf16[4,2,18816]{2,1,0:T(2,128)(2,1)}), bf16[4,2,18816]{2,1,0:T(2,128)(2,1)}, u32[]{:S(2)}, u32[]{:S(2)}) async-start(bf16[4,2,18816]{2,1,0:T(2,128)(2,1)} %reshape.523), calls=%async_computation.4 | async-start | bytes 602112 | tf_op jit(solution)/shard_map/all_to_all | solution.py:204
  408.0 18.5 %copy-start.61 = (bf16[14,14,64,1,1]{2,1,4,3,0:T(8,128)(2,1)S(1)}, bf16[14,14,64,1,1]{2,1,4,3,0:T(8,128)(2,1)}, u32[]{:S(2)}) copy-start(bf16[14,14,64,1,1]{2,1,4,3,0:T(8,128)(2,1)} %fusion.79) | copy-start | bytes 75268
  446.0 26.1 %all-to-all-start.7 = ((bf16[4,2,56448]{2,1,0:T(2,128)(2,1)}), bf16[4,2,56448]{2,1,0:T(2,128)(2,1)}, u32[]{:S(2)}, u32[]{:S(2)}) async-start(bf16[4,2,56448]{2,1,0:T(2,128)(2,1)} %reshape.531), calls=%async_computation.7 | async-start | bytes 1806336 | tf_op jit(solution)/shard_map/all_to_all | solution.py:208
  468.6 7.8 copy-start.74
  468.7 7.9 copy-start.94
  468.7 8.0 copy-start.93
  468.7 8.1 copy-start.29
  468.7 8.1 copy-start.63
  468.7 8.1 copy-start.65
  468.7 8.1 copy-start.81
  468.7 8.1 copy-start.96
  472.2 18.8 %all-to-all-start.5 = ((bf16[4,2,56448]{2,1,0:T(2,128)(2,1)}), bf16[4,2,56448]{2,1,0:T(2,128)(2,1)}, u32[]{:S(2)}, u32[]{:S(2)}) async-start(bf16[4,2,56448]{2,1,0:T(2,128)(2,1)} %reshape.533), calls=%async_computation.5 | async-start | bytes 1806336 | tf_op jit(solution)/shard_map/all_to_all | solution.py:208
  476.4 153.7 %reduce-scatter.5.cloned.1.call-start = ((), (), s32[]{:S(2)}) async-start(), calls=%async_computation.16 | async-start | bytes 7299072 | tf_op jit(solution)/shard_map/reduce_scatter | solution.py:247
  511.6 259.7 %reduce-scatter.9.cloned.1.call-start = ((), (), s32[]{:S(2)}) async-start(), calls=%async_computation.18 | async-start | bytes 9732096 | tf_op jit(solution)/shard_map/reduce_scatter | solution.py:249
  520.7 392.5 %reduce-scatter.11.cloned.1.call-start = ((), (), s32[]{:S(2)}) async-start(), calls=%async_computation.19 | async-start | bytes 9732096 | tf_op jit(solution)/shard_map/reduce_scatter | solution.py:250
  570.1 343.1 %copy-start.1 = (bf16[27,64]{1,0:T(8,128)(2,1)S(1)}, bf16[27,64]{1,0:T(8,128)(2,1)}, u32[]{:S(2)}) copy-start(bf16[27,64]{1,0:T(8,128)(2,1)} %param.24) | copy-start | bytes 10372
  (86 other events, 247.7 us)
Sparse Core Ops, SparseCore 0:
  9.6 72.6 all-gather.4
  83.9 29.0 all-gather.6
  114.6 88.5 all-gather.8
  204.5 87.8 all-gather.10
  345.7 97.9 reduce-scatter.6
  511.7 118.2 reduce-scatter.4
  636.5 134.6 reduce-scatter.8
  778.7 134.3 reduce-scatter.10
where the time goes:
time: 931 us; the launch traced here: 920 us
  waiting for transfers between devices  393 us (42%)
  local copies, waits for them, and re-layouts  242 us (26%)
  matrix products  140 us (15%)
  other arithmetic  53.6 us (6%)
  blocking collectives  41.8 us (4%)
  starting transfers between devices  34.1 us (4%)
  between operations  15.9 us (2%)
    reduce_scatter x1, waiting for transfers between devices, per_device(): lax.psum_scatter(large_sums[3], ('dp', 'seq', 'fsdp'), scatter_dimension=...  142 us
    reduce_scatter x1, waiting for transfers between devices, per_device(): lax.psum_scatter(large_sums[2], ('dp', 'seq', 'fsdp'), scatter_dimension=...  141 us
    all_gather x1, waiting for transfers between devices, per_device(): lax.all_gather(qkv_weight, 'fsdp', axis=0, tiled=True)  67.2 us
    unnamed x256, local copies, waits for them, and re-layouts  64.1 us
    psum x1, blocking collectives, per_device(): small_sums = lax.psum(small_sums, ('dp', 'seq', 'fsdp'))  41.8 us
    convert_element_type x4, local copies, waits for them, and re-layouts, attend_back(): height_grads = jnp.sum(grid_grads, axis=5, dtype=jnp.float32)  31.1 us
    add x4, local copies, waits for them, and re-layouts, scores_of(): height_terms[..., :, None] + width_terms[..., None, :]  30.1 us
    all_gather x1, waiting for transfers between devices, per_device(): lax.all_gather(output_weight, 'fsdp', axis=0, tiled=True)  21.8 us
  transfers between devices with their start and end apart: 16, of which 6 were waited for; matrix products, arithmetic and copies ran while one was open for 42% of the time, Pallas kernels for 0%

commit v1 on v0

v1 whole, which is shorter than its diff:
```python
import functools

import jax
import jax.numpy as jnp
from jax import lax
from jax.experimental import pallas as pl
from jax.experimental.pallas import tpu as pltpu
from jax.sharding import PartitionSpec as P

D = 768
HEADS = 12
HD = 64
FF = 3072
WIN = 14
GRID = 48
NWS = 4
TOK = 49
PAD = 56
ROWS = 4 * PAD
HALF = D // 2
PAIRS = 3
LANES = 128
TAB = 512
NEG = -1e30
BF = jnp.bfloat16
F32 = jnp.float32


def mm(left, right, dims=((1,), (0,))):
    return lax.dot_general(left, right, (dims, ((), ())), preferred_element_type=F32)


def attn_fwd_kernel(packed, table, spot, fold, keys, bias, out, probs):
    lane = lax.broadcasted_iota(jnp.int32, (ROWS, LANES), 1)
    for pair in range(PAIRS):
        q = packed[0, :, pair * LANES : (pair + 1) * LANES]
        k = packed[0, :, HALF + pair * LANES : HALF + (pair + 1) * LANES]
        v = packed[0, :, 2 * HALF + pair * LANES : 2 * HALF + (pair + 1) * LANES]
        right = jnp.concatenate([k, keys[...]], axis=1)
        parts = []
        for e in range(2):
            mine = (lane < HD) if e == 0 else (lane >= HD)
            spread = (mm(q, table[e]) * spot[...]).astype(BF)
            rel = mm(spread, fold[...]).astype(BF)
            scaled = jnp.where(mine, q.astype(F32) * (HD**-0.5), 0.0).astype(BF)
            left = jnp.concatenate([scaled, rel], axis=1)
            s = mm(left, right, ((1,), (1,))) + bias[...]
            p = jnp.exp(s - jnp.max(s, axis=1, keepdims=True))
            p = (p / jnp.sum(p, axis=1, keepdims=True)).astype(BF)
            probs[0, 2 * pair + e] = p
            parts.append(mm(p, v))
        out[0, :, pair * LANES : (pair + 1) * LANES] = jnp.where(
            lane < HD, parts[0], parts[1]
        ).astype(BF)


def attn_bwd_kernel(packed, grads, probs, table, spot, fold, keys, out, tab_grad):
    lane = lax.broadcasted_iota(jnp.int32, (ROWS, LANES), 1)
    lane_t = lax.broadcasted_iota(jnp.int32, (TAB, LANES), 1)

    @pl.when(pl.program_id(0) == 0)
    def _():
        tab_grad[...] = jnp.zeros_like(tab_grad)

    for pair in range(PAIRS):
        q = packed[0, :, pair * LANES : (pair + 1) * LANES]
        k = packed[0, :, HALF + pair * LANES : HALF + (pair + 1) * LANES]
        v = packed[0, :, 2 * HALF + pair * LANES : 2 * HALF + (pair + 1) * LANES]
        go = grads[0, :, pair * LANES : (pair + 1) * LANES]
        right = jnp.concatenate([k, keys[...]], axis=1)
        dq, dk, dv, dt = [], [], [], []
        for e in range(2):
            mine = (lane < HD) if e == 0 else (lane >= HD)
            go_e = jnp.where(mine, go.astype(F32), 0.0).astype(BF)
            p_low = probs[0, 2 * pair + e]
            p = p_low.astype(F32)
            dp = mm(go_e, v, ((1,), (1,)))
            ds = (p * (dp - jnp.sum(dp * p, axis=1, keepdims=True))).astype(BF)
            both = mm(ds, right)
            rel = both[:, LANES:].astype(BF)
            spread = (mm(rel, fold[...], ((1,), (1,))) * spot[...]).astype(BF)
            dq.append((HD**-0.5) * both[:, :LANES] + mm(spread, table[e], ((1,), (1,))))
            dk.append((HD**-0.5) * mm(ds, q, ((0,), (0,))))
            dv.append(mm(p_low, go, ((0,), (0,))))
            dt.append(mm(spread, q, ((0,), (0,))))
        tab_grad[...] += jnp.where(lane_t < HD, dt[0], dt[1])
        for at, two in ((0, dq), (HALF, dk), (2 * HALF, dv)):
            out[0, :, at + pair * LANES : at + (pair + 1) * LANES] = jnp.where(
                lane < HD, two[0], two[1]
            ).astype(BF)


def whole(shape):
    return pl.BlockSpec(shape, lambda w: (0,) * len(shape))


def per_window(shape):
    return pl.BlockSpec((1,) + shape, lambda w: (w,) + (0,) * len(shape))


PARAMS = pltpu.CompilerParams(vmem_limit_bytes=48 * 1024 * 1024)


def attn_fwd(packed, table, spot, fold, keys, bias):
    count = packed.shape[0]
    return pl.pallas_call(
        attn_fwd_kernel,
        grid=(count,),
        in_specs=[
            per_window((ROWS, 3 * HALF)),
            whole((2, LANES, TAB)),
            whole((ROWS, TAB)),
            whole((TAB, LANES)),
            whole((ROWS, LANES)),
            whole((1, ROWS)),
        ],
        out_specs=[per_window((ROWS, HALF)), per_window((2 * PAIRS, ROWS, ROWS))],
        out_shape=[
            jax.ShapeDtypeStruct((count, ROWS, HALF), BF),
            jax.ShapeDtypeStruct((count, 2 * PAIRS, ROWS, ROWS), BF),
        ],
        compiler_params=PARAMS,
        name="attn_fwd",
    )(packed, table, spot, fold, keys, bias)


def attn_bwd(packed, grads, probs, table, spot, fold, keys):
    count = packed.shape[0]
    return pl.pallas_call(
        attn_bwd_kernel,
        grid=(count,),
        in_specs=[
            per_window((ROWS, 3 * HALF)),
            per_window((ROWS, HALF)),
            per_window((2 * PAIRS, ROWS, ROWS)),
            whole((2, LANES, TAB)),
            whole((ROWS, TAB)),
            whole((TAB, LANES)),
            whole((ROWS, LANES)),
        ],
        out_specs=[per_window((ROWS, 3 * HALF)), whole((TAB, LANES))],
        out_shape=[
            jax.ShapeDtypeStruct((count, ROWS, 3 * HALF), BF),
            jax.ShapeDtypeStruct((TAB, LANES), F32),
        ],
        compiler_params=PARAMS,
        name="attn_bwd",
    )(packed, grads, probs, table, spot, fold, keys)


def place_kernel(where, shard, first, second, third, out, sems):
    z, s, a, b, d = where[0], where[1], where[2], where[3], where[4]
    copies = [pltpu.make_async_copy(shard, out.at[z], sems.at[0])]
    for i in range(3):
        zz = lax.rem(z + 3 - i, 4)
        for n, (src, q) in enumerate(
            (
                (first.at[i], s),
                (second.at[i], a),
                (third.at[i], b),
                (third.at[3 + i], d),
            )
        ):
            copies.append(pltpu.make_async_copy(src, out.at[zz, q], sems.at[1 + 4 * i + n]))
    for copy in copies:
        copy.start()
    for copy in copies:
        copy.wait()


def place(where, shard, first, second, third):
    rows, columns = first.shape[1:]
    anyspace = pl.BlockSpec(memory_space=pl.ANY)
    return pl.pallas_call(
        place_kernel,
        in_specs=[pl.BlockSpec(memory_space=pltpu.SMEM)] + [anyspace] * 4,
        out_specs=pl.BlockSpec(memory_space=pltpu.VMEM),
        out_shape=jax.ShapeDtypeStruct((4, 4, rows, columns), BF),
        scratch_shapes=[pltpu.SemaphoreType.DMA((13,))],
        name="place",
    )(where, shard.reshape(4, rows, columns), first, second, third).reshape(16 * rows, columns)


def per_device(
    n_dp,
    image_tokens,
    slot_window,
    first_gain,
    first_bias,
    qkv_weight,
    qkv_bias,
    rel_height,
    rel_width,
    proj_weight,
    proj_bias,
    second_gain,
    second_bias,
    hidden_weight,
    hidden_bias,
    output_weight,
    output_bias,
    cotangent,
):
    images = image_tokens.shape[0]
    own_rows = images * ROWS
    c = lax.axis_index("dp") % 2
    s = lax.axis_index("seq")
    z = lax.axis_index("fsdp")
    a = jnp.where(c == 0, s ^ 1, s ^ 2)
    b = jnp.where(c == 0, s ^ 2, s ^ 1)
    d = s ^ 3

    def plane_perm(step):
        out = []
        for i in range(n_dp):
            hop = (1, 2)[(i + step) % 2]
            out += [(i * 4 + j, i * 4 + (j ^ hop)) for j in range(4)]
        return out

    plane_one, plane_two = plane_perm(0), plane_perm(1)

    def to_core(v):
        return lax.ppermute(v, "dp", [(i, i ^ 1) for i in range(n_dp)])

    def to_seq(v, k):
        return lax.ppermute(v, "seq", [(i, i ^ k) for i in range(4)])

    def to_z(v, k):
        return lax.ppermute(v, "fsdp", [(i, (i + k) % 4) for i in range(4)])

    def to_plane(v, perm):
        return lax.ppermute(v, ("dp", "seq"), perm)

    def pick(v, index, axis=0):
        return lax.dynamic_index_in_dim(v, index, axis, keepdims=False)

    def gather(shard):
        rows = shard.shape[0] // 4
        own = pick(shard.reshape(4, rows, -1), s)
        first = jnp.stack([to_z(own, k) for k in (1, 2, 3)])
        second = to_plane(first, plane_one)
        third = to_plane(jnp.concatenate([first, second]), plane_two)
        where = jnp.stack([z, s, a, b, d]).astype(jnp.int32)
        return place(where, shard, first, second, third)

    def spread_tokens(v):
        own = []
        for k in range(4):
            piece = jnp.pad(pick(v, s ^ k, 1), ((0, 0), (0, PAD - TOK), (0, 0)))
            own.append(to_seq(piece, k) if k else piece)
        other = [to_core(piece) for piece in own]
        return jnp.concatenate(
            [jnp.stack(own, axis=1), jnp.stack(other, axis=1)], axis=0
        ).reshape(2 * own_rows, D)

    def home_tokens(v):
        v = v.reshape(images, 4, PAD, D)
        got = [to_seq(v[:, k], k) if k else v[:, 0] for k in range(4)]
        for bit in (1, 2):
            flip = (s & bit) != 0
            got = [jnp.where(flip, got[k ^ bit], got[k]) for k in range(4)]
        return jnp.stack([piece[:, :TOK] for piece in got], axis=1)

    qp_shard = jnp.concatenate(
        [
            pick(qkv_weight.reshape(-1, 3, 2, HALF), c, 2).reshape(-1, 3 * HALF),
            pick(proj_weight.reshape(-1, 2, HALF), c, 1),
        ],
        axis=1,
    )
    hidden_shard = pick(hidden_weight.reshape(-1, 4, 2, HALF), c, 2).reshape(-1, FF // 2)
    output_shard = pick(output_weight.reshape(2, HALF, D), c)
    x_low = spread_tokens(image_tokens)
    w_qp = gather(qp_shard)
    w_hidden = gather(hidden_shard)
    w_output = gather(output_shard)
    cot = spread_tokens(cotangent)
    w_qkv = w_qp[:, : 3 * HALF]
    proj_cols = w_qp[:, 3 * HALF :].reshape(2, HALF, HALF)
    proj_mine = pick(proj_cols, c)
    proj_other = to_core(pick(proj_cols, 1 - c))
    w_proj = jnp.where(
        c == 0,
        jnp.concatenate([proj_mine, proj_other], axis=1),
        jnp.concatenate([proj_other, proj_mine], axis=1),
    )
    b_qkv = pick(qkv_bias.reshape(3, 2, HALF), c, 1).reshape(-1)
    b_hidden = pick(hidden_bias.reshape(4, 2, HALF), c, 1).reshape(-1)

    row = jnp.arange(ROWS)
    token = (s ^ (row // PAD)) * TOK + row % PAD
    real = row % PAD < TOK
    t_r, t_c = token // WIN, token % WIN
    window = pick(slot_window, s)
    ok = (
        real
        & (window >= 0)
        & (window // NWS * WIN + t_r < GRID)
        & (window % NWS * WIN + t_c < GRID)
    ).astype(F32)
    keep_own = jnp.tile(ok, images)[:, None]
    keep = jnp.tile(ok, 2 * images)[:, None]
    near = jnp.arange(WIN)[:, None] - jnp.arange(WIN)[None, :] + WIN - 1
    height = rel_height[near].reshape(WIN * WIN, HD).T
    width = rel_width[near].reshape(WIN * WIN, HD).T
    gap = jnp.zeros((HD, TAB // 2 - WIN * WIN), BF)
    flat = jnp.concatenate([height, gap, width, gap], axis=1)
    blank = jnp.zeros_like(flat)
    table = jnp.stack([jnp.concatenate([flat, blank]), jnp.concatenate([blank, flat])])
    col = jnp.arange(TAB)
    in_half = col % (TAB // 2)
    col_from = jnp.where(in_half < WIN * WIN, in_half // WIN, -1)
    spot = (
        jnp.where(col[None, :] < TAB // 2, t_r[:, None], t_c[:, None]) == col_from[None, :]
    ).astype(F32)
    col_to = jnp.where(in_half < WIN * WIN, in_half % WIN + WIN * (col // (TAB // 2)), -1)
    fold = (col_to[:, None] == jnp.arange(LANES)[None, :]).astype(BF)
    lanes = jnp.arange(LANES)[None, :]
    keys = (
        real[:, None] & ((lanes == t_r[:, None]) | (lanes == WIN + t_c[:, None]))
    ).astype(BF)
    key_bias = jnp.where(real, 0.0, NEG).astype(F32)[None, :]

    def centre_of(v):
        v = v - jnp.mean(v, axis=-1, keepdims=True)
        rstd = lax.rsqrt(jnp.mean(v * v, axis=-1, keepdims=True) + 1e-06)
        return v * rstd, rstd

    def norm_back(grad, unit, rstd):
        return rstd * (
            grad
            - jnp.mean(grad, axis=-1, keepdims=True)
            - unit * jnp.mean(grad * unit, axis=-1, keepdims=True)
        )

    x = x_low.astype(F32)
    unit_one, rstd_one = centre_of(x)
    normed = ((unit_one * first_gain + first_bias) * keep).astype(BF)
    packed = (mm(normed, w_qkv) + b_qkv).astype(BF).reshape(2 * images, ROWS, 3 * HALF)
    attended, probs = attn_fwd(packed, table, spot, fold, keys, key_bias)
    attended = attended.reshape(2 * own_rows, HALF)
    branch = mm(attended, w_proj)
    branch_there = to_core(jnp.concatenate([branch[own_rows:], branch[:own_rows]]).astype(BF))
    middle = x + (branch + branch_there.astype(F32)) + proj_bias
    unit_two, rstd_two = centre_of(middle)
    second = (unit_two * second_gain + second_bias).astype(BF)
    pre_act = mm(second, w_hidden) + b_hidden
    phi = 0.5 * (1.0 + lax.erf(pre_act * (0.5**0.5)))
    active = (pre_act * phi).astype(BF)
    slope = (phi + pre_act * jnp.exp(-0.5 * pre_act * pre_act) * 0.3989422804014327).astype(BF)

    def blocks(grad):
        keep_two = jnp.stack([pick(grad, s, 1), pick(grad, b, 1)])
        send_two = jnp.stack([pick(grad, a, 1), pick(grad, d, 1)])
        return keep_two, send_two

    def reduce_plane(grad):
        keep_two, send_two = blocks(grad.astype(BF))
        one = keep_two.astype(F32) + to_plane(send_two, plane_one).astype(F32)
        two = one[0] + to_plane(one[1].astype(BF), plane_two).astype(F32)
        heads, rows, width_here = two.shape
        two = two.reshape(heads, 4, rows // 4, width_here)
        total = pick(two, z, 1)
        for k in (1, 2, 3):
            total = total + to_z(pick(two, (z + k) % 4, 1).astype(BF), k).astype(F32)
        return total

    def swap_halves(total):
        mine = pick(total, c)
        there = to_core(pick(total, 1 - c))
        return jnp.where(c == 0, mine, there), jnp.where(c == 0, there, mine)

    def interleave(grad, parts):
        if n_dp == 2:
            low, high = swap_halves(reduce_plane(grad.reshape(2, 4, -1, parts * HALF)))
            rows = low.shape[0]
            return jnp.stack(
                [low.reshape(rows, parts, HALF), high.reshape(rows, parts, HALF)], axis=2
            ).reshape(rows, 2 * parts * HALF)
        grad = grad.reshape(D, parts, HALF)
        zero = jnp.zeros_like(grad)
        full = jnp.where(
            c == 0, jnp.stack([grad, zero], axis=2), jnp.stack([zero, grad], axis=2)
        ).reshape(D, 2 * parts * HALF)
        return lax.psum_scatter(full, ("dp", "seq", "fsdp"), scatter_dimension=0, tiled=True)

    def stacked(grad):
        if n_dp == 2:
            return reduce_plane(grad.reshape(1, 4, -1, D))[0]
        zero = jnp.zeros_like(grad)
        full = jnp.where(c == 0, jnp.concatenate([grad, zero]), jnp.concatenate([zero, grad]))
        return lax.psum_scatter(full, ("dp", "seq", "fsdp"), scatter_dimension=0, tiled=True)

    grad_out = cot.astype(F32) * keep
    grad_feed = grad_out.astype(BF)
    g_output = interleave(mm(grad_feed, active, ((0,), (0,))), 4).T
    grad_pre = (mm(grad_feed, w_output, ((1,), (1,))) * slope.astype(F32)).astype(BF)
    g_hidden = interleave(mm(second, grad_pre, ((0,), (0,))), 4)
    part = mm(grad_pre, w_hidden, ((1,), (1,)))
    part_there = to_core(jnp.concatenate([part[own_rows:], part[:own_rows]]).astype(BF))
    grad_second = part + part_there.astype(F32)
    grad_middle = grad_out + norm_back(grad_second * second_gain, unit_two, rstd_two)
    grad_branch = grad_middle.astype(BF)
    g_proj = stacked(mm(attended, grad_branch, ((0,), (0,))))
    grad_att = mm(grad_branch, w_proj, ((1,), (1,))).astype(BF)

    feed = mm(active, w_output)
    feed_there = to_core(feed[own_rows:].astype(BF))
    block = (
        (middle[:own_rows] + feed[:own_rows] + feed_there.astype(F32) + output_bias) * keep_own
    ).astype(BF)
    block_out = home_tokens(block)

    grad_packed, tab_grad = attn_bwd(
        packed, grad_att.reshape(2 * images, ROWS, HALF), probs, table, spot, fold, keys
    )
    grad_packed = grad_packed.reshape(2 * own_rows, 3 * HALF)
    g_qkv = interleave(mm(normed, grad_packed, ((0,), (0,))), 3)
    back = mm(grad_packed, w_qkv, ((1,), (1,)))
    back_there = to_core(back[own_rows:].astype(BF))
    grad_normed = (back[:own_rows] + back_there.astype(F32)) * keep_own
    unit_own = unit_one[:own_rows]
    tok_grad = norm_back(grad_normed * first_gain, unit_own, rstd_one[:own_rows])
    input_grad = home_tokens((grad_middle[:own_rows] + tok_grad).astype(BF))

    def at_core(v, parts):
        v = v.reshape(parts, HALF)
        zero = jnp.zeros_like(v)
        return jnp.where(
            c == 0, jnp.stack([v, zero], axis=1), jnp.stack([zero, v], axis=1)
        ).reshape(-1)

    tab_sum = (tab_grad[:, :HD] + tab_grad[:, HD:]).reshape(2, TAB // 2, HD)[:, : WIN * WIN]
    to_offset = (near.reshape(-1)[None, :] == jnp.arange(2 * WIN - 1)[:, None]).astype(F32)
    rel_sums = jnp.einsum(
        "jp,apd->ajd", to_offset, tab_sum, precision=lax.Precision.HIGHEST
    )
    terms = [
        jnp.sum(grad_normed * unit_own, axis=0),
        jnp.sum(grad_normed, axis=0),
        at_core(jnp.sum(grad_packed.astype(F32), axis=0), 3),
        rel_sums[0].reshape(-1),
        rel_sums[1].reshape(-1),
        jnp.sum(grad_branch[:own_rows].astype(F32), axis=0),
        jnp.sum(grad_second[:own_rows] * unit_two[:own_rows], axis=0),
        jnp.sum(grad_second[:own_rows], axis=0),
        at_core(jnp.sum(grad_pre.astype(F32), axis=0), 4),
        jnp.sum(grad_feed[:own_rows].astype(F32), axis=0),
    ]
    sizes = [term.shape[0] for term in terms]
    total = jnp.concatenate(terms)
    total = total + to_core(total)
    total = total + to_seq(total, 1)
    total = total + to_seq(total, 2)
    for hop in (1, 2):
        total = total + lax.ppermute(total, "fsdp", [(i, i ^ hop) for i in range(4)])
    if n_dp > 2:
        groups = [list(range(core, n_dp, 2)) for core in range(2)]
        total = lax.psum(total, "dp", axis_index_groups=groups)
    small = []
    at = 0
    for size in sizes:
        small.append(total[at : at + size])
        at += size
    return (
        block_out,
        input_grad,
        small[0],
        small[1],
        g_qkv,
        small[2],
        small[3].reshape(2 * WIN - 1, HD),
        small[4].reshape(2 * WIN - 1, HD),
        g_proj,
        small[5],
        small[6],
        small[7],
        g_hidden,
        small[8],
        g_output,
        small[9],
    )


def solution(mesh):
    tokens = P("dp", "fsdp", "seq", None)
    rows = P("fsdp", None)
    every = P(("dp", "seq", "fsdp"), None)
    return jax.shard_map(
        functools.partial(per_device, mesh.shape["dp"]),
        mesh=mesh,
        in_specs=(
            tokens,
            P("fsdp"),
            P(),
            P(),
            rows,
            P(),
            P(),
            P(),
            rows,
            P(),
            P(),
            P(),
            rows,
            P(),
            rows,
            P(),
            tokens,
        ),
        out_specs=(
            tokens,
            tokens,
            P(),
            P(),
            every,
            P(),
            P(),
            P(),
            every,
            P(),
            P(),
            P(),
            every,
            P(),
            P(None, ("dp", "seq", "fsdp")),
            P(),
        ),
        check_vma=False,
    )
```

time: 931 us -> 380 us (0.41)
  waiting for transfers between devices: 393 us -> 63.2 us
  local copies, waits for them, and re-layouts: 242 us -> 70.6 us
  matrix products: 140 us -> 37.7 us
  starting transfers between devices: 34.1 us -> 82.9 us
  Pallas kernels: 0 us -> 45.3 us
  blocking collectives: 41.8 us -> 0 us
  other arithmetic: 53.6 us -> 69 us
  between operations: 15.9 us -> 5.81 us
    reduce_scatter x4 -> x0, waiting for transfers between devices: 300 us -> none  [the longest x1 142 us: per_device(): lax.psum_scatter(large_sums[3], ('dp', 'seq', 'fsdp'), scatter_dimension=...]
    dot_general x54 -> x13, matrix products: 140 us -> 37.7 us  [the longest x12 37.5 us: mm(): lax.dot_general(left, right, (dims, ((), ())), preferred_element_type=F32)]
    all_gather x4 -> x0, waiting for transfers between devices: 89 us -> none  [the longest x1 67.2 us: per_device(): lax.all_gather(qkv_weight, 'fsdp', axis=0, tiled=True)]
    ppermute x0 -> x68, starting transfers between devices: none -> 82.9 us  [the longest x21 29.6 us: to_z(): return lax.ppermute(v, 'fsdp', [(i, (i + k) % 4) for i in range(4)])]
    ppermute x0 -> x68, waiting for transfers between devices: none -> 63.2 us  [the longest x21 28.2 us: to_z(): return lax.ppermute(v, 'fsdp', [(i, (i + k) % 4) for i in range(4)])]
    unnamed x256 -> x184, local copies, waits for them, and re-layouts: 64.1 us -> 10 us
    all_to_all x14 -> x0, local copies, waits for them, and re-layouts: 47.1 us -> none  [the longest x4 18.6 us: per_device(): lax.all_to_all(grad_packed_h, 'seq', split_axis=1, concat_axis=3, tiled=T...]
    pallas_call x0 -> x5, Pallas kernels: none -> 45.3 us  [the longest x1 17.4 us: attn_bwd(): pl.pallas_call(attn_bwd_kernel, grid=(count,), in_specs=[per_window((ROWS...]
  transfers between devices with their start and end apart: 16 -> 68, of which waited for: 6 -> 21; matrix products, arithmetic and copies ran while one was open for 42% -> 40% of each run, Pallas kernels for 0% -> 12%
where the time goes in v1:
time: 380 us; the launch traced here: 375 us
  starting transfers between devices  82.9 us (22%)
  local copies, waits for them, and re-layouts  70.6 us (19%)
  other arithmetic  69 us (18%)
  waiting for transfers between devices  63.2 us (17%)
  Pallas kernels  45.3 us (12%)
  matrix products  37.7 us (10%)
  between operations  5.81 us (2%)
    dot_general x12, matrix products, mm(): lax.dot_general(left, right, (dims, ((), ())), preferred_element_type=F32)  37.5 us
    ppermute x21, starting transfers between devices, to_z(): return lax.ppermute(v, 'fsdp', [(i, (i + k) % 4) for i in range(4)])  29.6 us
    ppermute x21, waiting for transfers between devices, to_z(): return lax.ppermute(v, 'fsdp', [(i, (i + k) % 4) for i in range(4)])  28.2 us
    ppermute x14, waiting for transfers between devices, to_seq(): return lax.ppermute(v, 'seq', [(i, i ^ k) for i in range(4)])  22.9 us
    ppermute x14, starting transfers between devices, to_plane(): return lax.ppermute(v, ('dp', 'seq'), perm)  17.5 us
    pallas_call x1, Pallas kernels, attn_bwd(): pl.pallas_call(attn_bwd_kernel, grid=(count,), in_specs=[per_window((ROWS...  17.4 us
    ppermute x14, starting transfers between devices, to_seq(): return lax.ppermute(v, 'seq', [(i, i ^ k) for i in range(4)])  17.2 us
    pallas_call x1, Pallas kernels, attn_fwd(): pl.pallas_call(attn_fwd_kernel, grid=(count,), in_specs=[per_window((ROWS...  16.5 us
  transfers between devices with their start and end apart: 68, of which 21 were waited for; matrix products, arithmetic and copies ran while one was open for 40% of the time, Pallas kernels for 12%

profile of v1, /device:TPU:0, one launch (start us, length us, event | category | flops | bytes accessed | tf_op | source)
XLA Modules:
  0.0 374.5 jit_solution(15989349055818461567)
XLA Ops:
  3.5 5.0 %collective-permute-start.21 = (bf16[96,768]{1,0:T(8,128)(2,1)}, bf16[96,768]{1,0:T(8,128)(2,1)S(1)}, u32[]{:S(2)}, u32[]{:S(2)}) collective-permute-start(bf16[96,768]{1,0:T(8,128)(2,1)} %dynamic-slice_bitcast_fusion.20), channel_id=1, source_target_pairs={{0,3},{1,0},{2,1},{3,2},{4,7},{5,4},{6,5},{7,6},{8,11},{9,8},{10,9... | collective-permute-start | bytes 442376 | tf_op jit(solution)/shard_map/ppermute | solution.py:229
  11.1 2.9 dynamic-slice_reduce_fusion.1
  15.1 3.3 collective-permute-start.9
  23.2 3.4 reshape.616
  26.6 3.8 %dynamic-slice_reduce_fusion = bf16[192,4,384]{2,1,0:T(4,128)(2,1)S(1)} fusion(bf16[192,4,2,384]{3,2,1,0:T(2,128)(2,1)S(1)} %reshape.616, s32[]{:T(128)S(6)} %select_n.480), kind=kLoop, calls=%fused_computation.76 | loop fusion | bytes 1179652 | tf_op jit(solution)/shard_map/jit(dynamic_index_in_dim)/dynamic_slice | solution.py:235
  31.3 3.5 constant_dynamic-slice_fusion.3
  39.6 3.8 %collective-permute-start.16 = (bf16[48,1536]{1,0:T(8,128)(2,1)}, bf16[48,1536]{1,0:T(8,128)(2,1)S(1)}, u32[]{:S(2)}, u32[]{:S(2)}) collective-permute-start(bf16[48,1536]{1,0:T(8,128)(2,1)} %dynamic-slice_bitcast_fusion.21), channel_id=1, source_target_pairs={{0,3},{1,0},{2,1},{3,2},{4,7},{5,4},{6,5},{7,6},{8,11},{9,8},{10,9... | collective-permute-start | bytes 442376 | tf_op jit(solution)/shard_map/ppermute | solution.py:229
  55.8 2.7 collective-permute-done.15
  63.6 3.4 fusion.110
  80.1 3.3 fusion.104
  83.4 4.0 %collective-permute-done.11.third = bf16[6,48,1536]{2,1,0:T(8,128)(2,1)} collective-permute-done((bf16[6,48,1536]{2,1,0:T(8,128)(2,1)}, bf16[6,48,1536]{2,1,0:T(8,128)(2,1)}, u32[]{:S(2)}, u32[]{:S(2)}) %collective-permute-start.11) | collective-permute-done | bytes 884768 | tf_op jit(solution)/shard_map/ppermute | solution.py:232
  87.4 3.9 %place.3 = bf16[4,4,48,1536]{3,2,1,0:T(8,128)(2,1)} custom-call(s32[5]{0:T(128)} %stack.269.where, bf16[4,48,1536]{2,1,0:T(8,128)(2,1)} %pad_maximum_fusion.8.shard, bf16[3,48,1536]{2,1,0:T(8,128)(2,1)} %pad_maximum_fusion.12.first, bf16[3,48,1536]{2,1,0:T(8,128)(2,1)} %collective-permute-done.10.second, bf16[6,48,1536]{2,1,0:T(8,128)(2,1)} %collective-permute-done.11.third), custom_call_target="tpu_custom_call" | custom-call | tf_op jit(solution)/shard_map/place/pallas_call | solution.py:174
  93.2 3.9 %fusion.5 = bf16[896,1152]{1,0:T(8,128)(2,1)S(1)} fusion(f32[1152]{0:T(1024)S(1)} %copy-done.78, bf16[768,1536]{1,0:T(8,128)(2,1)S(1)} %bitcast.372, f32[896,768]{1,0:T(8,128)} %get-tuple-element.113, f32[896]{0:T(1024)S(1)} %mul.220, f32[768]{0:T(1024)S(1)} %copy-done.81, f32[768]{0:T(1024)S(1)} %copy-done.66), kind=kOutput, calls=%fused_computation.14 | convolution fusion | flops 1590263808 | bytes 6606848 | tf_op jit(solution)/shard_map/dot_general | solution.py:30
  97.2 16.5 %attn_fwd.1 = (bf16[4,224,384]{2,1,0:T(8,128)(2,1)S(1)}, bf16[4,6,224,224]{3,2,1,0:T(8,128)(2,1)}) custom-call(bf16[4,224,1152]{2,1,0:T(8,128)(2,1)S(1)} %bitcast.362, bf16[2,128,512]{2,1,0:T(8,128)(2,1)S(1)} %pad_maximum_fusion.18.table, f32[224,512]{1,0:T(8,128)S(1)} %fusion.30.spot, bf16[512,128]{1,0:T(8,128)(2,1)S(1)} %copy-done.4, ...), custom_call_target="tpu_custom_call" | custom-call | tf_op jit(solution)/shard_map/attn_fwd/pallas_call | solution.py:106
  131.3 5.6 %collective-permute-done.28 = bf16[2,56,768]{2,1,0:T(8,128)(2,1)} collective-permute-done((bf16[2,56,768]{2,1,0:T(8,128)(2,1)}, bf16[2,56,768]{2,1,0:T(8,128)(2,1)}, u32[]{:S(2)}, u32[]{:S(2)}) %collective-permute-start.28) | collective-permute-done | bytes 172064 | tf_op jit(solution)/shard_map/ppermute | solution.py:226
  137.0 12.5 %collective-permute-start.34 = (bf16[2,56,768]{2,1,0:T(8,128)(2,1)}, bf16[2,56,768]{2,1,0:T(8,128)(2,1)}, u32[]{:S(2)}, u32[]{:S(2)}) collective-permute-start(bf16[2,56,768]{2,1,0:T(8,128)(2,1)} %collective-permute-done.30), channel_id=1, source_target_pairs={{0,16},{16,0},{1,17},{17,1},{2,18},{18,2},{3,19},{19,3},{4,20},{20... | collective-permute-start | bytes 516104 | tf_op jit(solution)/shard_map/ppermute | solution.py:223
  153.5 2.7 copy.213
  156.2 2.9 multiply_convert_fusion.2
  160.3 3.7 place.5
  164.1 3.7 place.4
  167.8 3.6 fusion.108
  174.2 2.7 multiply_convert_fusion.1
  176.9 5.6 %convert_reduce_fusion = (f32[1536]{0:T(1024)}, bf16[896,1536]{1,0:T(8,128)(2,1)S(1)}) fusion(f32[896,1536]{1,0:T(8,128)S(1)} %get-tuple-element.217, f32[1536]{0:T(1024)S(1)} %copy-done.79, bf16[896,768]{1,0:T(8,128)(2,1)S(1)} %bitcast.390, bf16[1536,768]{1,0:T(8,128)(2,1)S(1)} %bitcast.381), kind=kOutput, calls=%fused_computation.8 | convolution fusion | flops 2134571520 | bytes 12005376 | tf_op jit(solution)/shard_map/dot_general | solution.py:30
  182.5 2.9 convolution_convert_fusion.1
  189.2 3.9 %fusion.119 = (bf16[896,768]{1,0:T(8,128)(2,1)S(1)}, f32[896,768]{1,0:T(8,128)}) fusion(bf16[896,1536]{1,0:T(8,128)(2,1)S(1)} %get-tuple-element.219, bf16[768,1536]{1,0:T(8,128)(2,1)S(1)} %bitcast.384), kind=kOutput, calls=%fused_computation.336 | convolution fusion | flops 2114617344 | bytes 9240576 | tf_op jit(solution)/shard_map/dot_general | solution.py:30
  194.6 3.9 %fusion.120 = f32[896,768]{1,0:T(8,128)} fusion(bf16[896,1536]{1,0:T(8,128)(2,1)S(1)} %get-tuple-element.216, bf16[1536,768]{1,0:T(8,128)(2,1)S(1)} %bitcast.382), kind=kOutput, calls=%fused_computation.337 | convolution fusion | flops 2113929216 | bytes 7864320 | tf_op jit(solution)/shard_map/dot_general | solution.py:30
  201.1 3.1 collective-permute-done.56
  208.6 2.7 multiply_reduce_fusion.3
  212.3 5.8 %fusion.107 = (bf16[896,768]{1,0:T(8,128)(2,1)S(1)}, f32[896,768]{1,0:T(8,128)}, bf16[896,768]{1,0:T(8,128)(2,1)}) fusion(f32[896]{0:T(1024)S(1)} %broadcast_multiply_fusion.1, f32[896]{0:T(1024)S(1)} %broadcast_multiply_fusion.2, f32[896,768]{1,0:T(8,128)S(1)} %get-tuple-element.117, f32[768]{0:T(1024)S(1)} %copy-done.70, f32[896]{0:T(1024)S(1)} %add_rsqrt_fusion.1, ...), kind=kLoop, calls=%fused_computation.325 | loop fusion | flops 15482880 | bytes 12407296 | tf_op jit(solution)/shard_map/convert_element_type | solution.py:403
  220.6 17.4 %attn_bwd.1 = (bf16[4,224,1152]{2,1,0:T(8,128)(2,1)S(1)}, f32[512,128]{1,0:T(8,128)S(1)}) custom-call(bf16[4,224,1152]{2,1,0:T(8,128)(2,1)S(1)} %bitcast.363, bf16[4,224,384]{2,1,0:T(8,128)(2,1)S(1)} %bitcast.368, bf16[4,6,224,224]{3,2,1,0:T(8,128)(2,1)} %get-tuple-element.21.probs, bf16[2,128,512]{2,1,0:T(8,128)(2,1)S(1)} %pad_maximum_fusion.18.table, ...), custom_call_target="tpu_custom_call" | custom-call | tf_op jit(solution)/shard_map/attn_bwd/pallas_call | solution.py:129
  244.1 3.6 fusion.10
  253.5 4.8 %convolution_convert_fusion = bf16[2,4,96,1536]{3,2,1,0:T(8,128)(2,1)S(1)} fusion(bf16[2,4,96,896]{3,2,1,0:T(8,128)(2,1)} %bitcast.391, bf16[896,1536]{1,0:T(8,128)(2,1)} %copy-done.86), kind=kOutput, calls=%fused_computation.15 | convolution fusion | flops 2115108864 | bytes 6488064 | tf_op jit(solution)/shard_map/dot_general | solution.py:30
  265.2 3.7 collective-permute-start.60
  269.0 4.5 %collective-permute-done.58 = bf16[2,24,1536]{2,1,0:T(8,128)(2,1)S(1)} collective-permute-done((bf16[2,24,1536]{2,1,0:T(8,128)(2,1)S(1)}, bf16[2,24,1536]{2,1,0:T(8,128)(2,1)S(1)}, u32[]{:S(2)}, u32[]{:S(2)}) %collective-permute-start.58) | collective-permute-done | bytes 147488 | tf_op jit(solution)/shard_map/ppermute | solution.py:229
  274.6 3.0 collective-permute-start.55
  277.6 4.5 %collective-permute-done.59 = bf16[2,24,1536]{2,1,0:T(8,128)(2,1)S(1)} collective-permute-done((bf16[2,24,1536]{2,1,0:T(8,128)(2,1)S(1)}, bf16[2,24,1536]{2,1,0:T(8,128)(2,1)S(1)}, u32[]{:S(2)}, u32[]{:S(2)}) %collective-permute-start.59) | collective-permute-done | bytes 147488 | tf_op jit(solution)/shard_map/ppermute | solution.py:229
  284.2 2.7 collective-permute-done.54
  289.9 4.6 %multiply_reduce_fusion.4 = (f32[768]{0:T(1024)S(1)}, f32[448]{0:T(512)S(1)}, f32[448]{0:T(512)S(1)}, f32[768]{0:T(1024)S(1)}, f32[448,768]{1,0:T(8,128)}, /*index=5*/bf16[448,768]{1,0:T(8,128)(2,1)S(1)}) fusion(f32[896,768]{1,0:T(8,128)} %get-tuple-element.113, f32[768]{0:T(1024)S(1)} %copy-done.67, f32[448]{0:T(512)} %mul.234, ...), kind=kLoop, calls=%fused_computation.62 | loop fusion | flops 5502592 | bytes 8963328 | tf_op jit(solution)/shard_map/reduce_sum | solution.py:439
  294.8 2.5 fusion.15
  301.3 9.9 %collective-permute-done.41 = f32[13440]{0:T(1024)S(1)} collective-permute-done((f32[13440]{0:T(1024)S(1)}, f32[13440]{0:T(1024)S(1)}, u32[]{:S(2)}, u32[]{:S(2)}) %collective-permute-start.41) | collective-permute-done | bytes 53792 | tf_op jit(solution)/shard_map/ppermute | solution.py:226
  312.8 2.7 collective-permute-done.42
  318.5 4.1 %collective-permute-done.39 = bf16[2,56,768]{2,0,1:T(2,128)(2,1)S(1)} collective-permute-done((bf16[2,56,768]{2,0,1:T(2,128)(2,1)S(1)}, bf16[2,56,768]{2,0,1:T(2,128)(2,1)S(1)}, u32[]{:S(2)}, u32[]{:S(2)}) %collective-permute-start.39) | collective-permute-done | bytes 172064 | tf_op jit(solution)/shard_map/ppermute | solution.py:226
  333.4 3.0 collective-permute-start.44
  345.8 3.7 collective-permute-start.49
  352.9 3.2 collective-permute-done.48
  358.5 3.8 %collective-permute-start.66 = (bf16[2,24,1536]{2,1,0:T(8,128)(2,1)S(1)}, bf16[2,24,1536]{2,1,0:T(8,128)(2,1)S(1)}, u32[]{:S(2)}, u32[]{:S(2)}) collective-permute-start(bf16[2,24,1536]{2,1,0:T(8,128)(2,1)S(1)} %get-tuple-element.140), channel_id=1, source_target_pairs={{0,3},{1,0},{2,1},{3,2},{4,7},{5,4},{6,5},{7,6},{8,11},{9,8},{10,9... | collective-permute-start | bytes 442376 | tf_op jit(solution)/shard_map/ppermute | solution.py:229
  362.4 3.3 collective-permute-done.64
  365.8 5.4 %collective-permute-done.65 = bf16[2,24,1536]{2,1,0:T(8,128)(2,1)S(1)} collective-permute-done((bf16[2,24,1536]{2,1,0:T(8,128)(2,1)S(1)}, bf16[2,24,1536]{2,1,0:T(8,128)(2,1)S(1)}, u32[]{:S(2)}, u32[]{:S(2)}) %collective-permute-start.65) | collective-permute-done | bytes 147488 | tf_op jit(solution)/shard_map/ppermute | solution.py:229
  (486 shorter events, 149.8 us)
Async XLA Ops:
  3.5 36.0 %collective-permute-start.21 = (bf16[96,768]{1,0:T(8,128)(2,1)}, bf16[96,768]{1,0:T(8,128)(2,1)S(1)}, u32[]{:S(2)}, u32[]{:S(2)}) collective-permute-start(bf16[96,768]{1,0:T(8,128)(2,1)} %dynamic-slice_bitcast_fusion.20), channel_id=1, source_target_pairs={{0,3},{1,0},{2,1},{3,2},{4,7},{5,4},{6,5},{7,6},{8,11},{9,8},{10,9... | collective-permute-start | bytes 442376 | tf_op jit(solution)/shard_map/ppermute | solution.py:229
  8.5 31.1 %collective-permute-start.20 = (bf16[96,768]{1,0:T(8,128)(2,1)}, bf16[96,768]{1,0:T(8,128)(2,1)}, u32[]{:S(2)}, u32[]{:S(2)}) collective-permute-start(bf16[96,768]{1,0:T(8,128)(2,1)} %dynamic-slice_bitcast_fusion.20), channel_id=1, source_target_pairs={{0,2},{1,3},{2,0},{3,1},{4,6},{5,7},{6,4},{7,5},{8,10},{9,11},{10,... | collective-permute-start | bytes 442376 | tf_op jit(solution)/shard_map/ppermute | solution.py:229
  8.5 39.5 %collective-permute-start.19 = (bf16[96,768]{1,0:T(8,128)(2,1)}, bf16[96,768]{1,0:T(8,128)(2,1)}, u32[]{:S(2)}, u32[]{:S(2)}) collective-permute-start(bf16[96,768]{1,0:T(8,128)(2,1)} %dynamic-slice_bitcast_fusion.20), channel_id=1, source_target_pairs={{0,1},{1,2},{2,3},{3,0},{4,5},{5,6},{6,7},{7,4},{8,9},{9,10},{10,1... | collective-permute-start | bytes 442376 | tf_op jit(solution)/shard_map/ppermute | solution.py:229
  15.1 33.0 %collective-permute-start.9 = (bf16[48,1536]{1,0:T(8,128)(2,1)}, bf16[48,1536]{1,0:T(8,128)(2,1)}, u32[]{:S(2)}, u32[]{:S(2)}) collective-permute-start(bf16[48,1536]{1,0:T(8,128)(2,1)} %fusion.58), channel_id=1, source_target_pairs={{0,3},{1,0},{2,1},{3,2},{4,7},{5,4},{6,5},{7,6},{8,11},{9,8},{10,9... | collective-permute-start | bytes 442376 | tf_op jit(solution)/shard_map/ppermute | solution.py:229
  18.4 30.3 %collective-permute-start.8 = (bf16[48,1536]{1,0:T(8,128)(2,1)}, bf16[48,1536]{1,0:T(8,128)(2,1)}, u32[]{:S(2)}, u32[]{:S(2)}) collective-permute-start(bf16[48,1536]{1,0:T(8,128)(2,1)} %fusion.58), channel_id=1, source_target_pairs={{0,2},{1,3},{2,0},{3,1},{4,6},{5,7},{6,4},{7,5},{8,10},{9,11},{10,... | collective-permute-start | bytes 442376 | tf_op jit(solution)/shard_map/ppermute | solution.py:229
  39.5 10.7 %collective-permute-start.7 = (bf16[48,1536]{1,0:T(8,128)(2,1)}, bf16[48,1536]{1,0:T(8,128)(2,1)S(1)}, u32[]{:S(2)}, u32[]{:S(2)}) collective-permute-start(bf16[48,1536]{1,0:T(8,128)(2,1)} %fusion.58), channel_id=1, source_target_pairs={{0,1},{1,2},{2,3},{3,0},{4,5},{5,6},{6,7},{7,4},{8,9},{9,10},{10,1... | collective-permute-start | bytes 442376 | tf_op jit(solution)/shard_map/ppermute | solution.py:229
  39.6 12.1 %collective-permute-start.16 = (bf16[48,1536]{1,0:T(8,128)(2,1)}, bf16[48,1536]{1,0:T(8,128)(2,1)S(1)}, u32[]{:S(2)}, u32[]{:S(2)}) collective-permute-start(bf16[48,1536]{1,0:T(8,128)(2,1)} %dynamic-slice_bitcast_fusion.21), channel_id=1, source_target_pairs={{0,3},{1,0},{2,1},{3,2},{4,7},{5,4},{6,5},{7,6},{8,11},{9,8},{10,9... | collective-permute-start | bytes 442376 | tf_op jit(solution)/shard_map/ppermute | solution.py:229
  48.0 10.4 %collective-permute-start.15 = (bf16[48,1536]{1,0:T(8,128)(2,1)}, bf16[48,1536]{1,0:T(8,128)(2,1)S(1)}, u32[]{:S(2)}, u32[]{:S(2)}) collective-permute-start(bf16[48,1536]{1,0:T(8,128)(2,1)} %dynamic-slice_bitcast_fusion.21), channel_id=1, source_target_pairs={{0,2},{1,3},{2,0},{3,1},{4,6},{5,7},{6,4},{7,5},{8,10},{9,11},{10,... | collective-permute-start | bytes 442376 | tf_op jit(solution)/shard_map/ppermute | solution.py:229
  48.1 10.3 %collective-permute-start.14 = (bf16[48,1536]{1,0:T(8,128)(2,1)}, bf16[48,1536]{1,0:T(8,128)(2,1)S(1)}, u32[]{:S(2)}, u32[]{:S(2)}) collective-permute-start(bf16[48,1536]{1,0:T(8,128)(2,1)} %dynamic-slice_bitcast_fusion.21), channel_id=1, source_target_pairs={{0,1},{1,2},{2,3},{3,0},{4,5},{5,6},{6,7},{7,4},{8,9},{9,10},{10,1... | collective-permute-start | bytes 442376 | tf_op jit(solution)/shard_map/ppermute | solution.py:229
  48.7 11.4 %collective-permute-start = (bf16[2,56,768]{2,0,1:T(2,128)(2,1)S(1)}, bf16[2,56,768]{2,0,1:T(2,128)(2,1)S(1)}, u32[]{:S(2)}, u32[]{:S(2)}) collective-permute-start(bf16[2,56,768]{2,0,1:T(2,128)(2,1)S(1)} %pad.32), channel_id=1, source_target_pairs={{0,4},{4,0},{8,12},{12,8},{1,5},{5,1},{9,13},{13,9},{2,6},{6,2},{1... | collective-permute-start | bytes 516104 | tf_op jit(solution)/shard_map/ppermute | solution.py:226
  50.2 10.0 %collective-permute-start.2 = (bf16[2,56,768]{2,0,1:T(2,128)(2,1)S(1)}, bf16[2,56,768]{2,0,1:T(2,128)(2,1)S(1)}, u32[]{:S(2)}, u32[]{:S(2)}) collective-permute-start(bf16[2,56,768]{2,0,1:T(2,128)(2,1)S(1)} %pad.34), channel_id=1, source_target_pairs={{0,12},{4,8},{8,4},{12,0},{1,13},{5,9},{9,5},{13,1},{2,14},{6,10},... | collective-permute-start | bytes 516104 | tf_op jit(solution)/shard_map/ppermute | solution.py:226
  51.7 8.9 %collective-permute-start.1 = (bf16[2,56,768]{2,0,1:T(2,128)(2,1)S(1)}, bf16[2,56,768]{2,0,1:T(2,128)(2,1)S(1)}, u32[]{:S(2)}, u32[]{:S(2)}) collective-permute-start(bf16[2,56,768]{2,0,1:T(2,128)(2,1)S(1)} %pad.33), channel_id=1, source_target_pairs={{0,8},{4,12},{8,0},{12,4},{1,9},{5,13},{9,1},{13,5},{2,10},{6,14},... | collective-permute-start | bytes 516104 | tf_op jit(solution)/shard_map/ppermute | solution.py:226
  58.5 62.2 %collective-permute-start.22 = (bf16[3,96,768]{2,1,0:T(8,128)(2,1)}, bf16[3,96,768]{2,1,0:T(8,128)(2,1)}, u32[]{:S(2)}, u32[]{:S(2)}) collective-permute-start(bf16[3,96,768]{2,1,0:T(8,128)(2,1)} %pad_maximum_fusion.14.first), channel_id=1, source_target_pairs={{0,4},{4,0},{8,12},{12,8},{16,24},{20,28},{24,16},{28,20},{1,5},{5... | collective-permute-start | bytes 1327112 | tf_op jit(solution)/shard_map/ppermute | solution.py:232
  61.6 10.3 %collective-permute-start.10 = (bf16[3,48,1536]{2,1,0:T(8,128)(2,1)}, bf16[3,48,1536]{2,1,0:T(8,128)(2,1)}, u32[]{:S(2)}, u32[]{:S(2)}) collective-permute-start(bf16[3,48,1536]{2,1,0:T(8,128)(2,1)} %pad_maximum_fusion.12.first), channel_id=1, source_target_pairs={{0,4},{4,0},{8,12},{12,8},{16,24},{20,28},{24,16},{28,20},{1,5},{5... | collective-permute-start | bytes 1327112 | tf_op jit(solution)/shard_map/ppermute | solution.py:232
  63.1 61.2 %collective-permute-start.17 = (bf16[3,48,1536]{2,1,0:T(8,128)(2,1)}, bf16[3,48,1536]{2,1,0:T(8,128)(2,1)}, u32[]{:S(2)}, u32[]{:S(2)}) collective-permute-start(bf16[3,48,1536]{2,1,0:T(8,128)(2,1)} %pad_maximum_fusion.13.first), channel_id=1, source_target_pairs={{0,4},{4,0},{8,12},{12,8},{16,24},{20,28},{24,16},{28,20},{1,5},{5... | collective-permute-start | bytes 1327112 | tf_op jit(solution)/shard_map/ppermute | solution.py:232
  74.1 13.4 %collective-permute-start.11 = (bf16[6,48,1536]{2,1,0:T(8,128)(2,1)}, bf16[6,48,1536]{2,1,0:T(8,128)(2,1)}, u32[]{:S(2)}, u32[]{:S(2)}) collective-permute-start(bf16[6,48,1536]{2,1,0:T(8,128)(2,1)} %pad_maximum_fusion.4), channel_id=1, source_target_pairs={{0,8},{4,12},{8,0},{12,4},{16,20},{20,16},{24,28},{28,24},{1,9},{5... | collective-permute-start | bytes 2654216 | tf_op jit(solution)/shard_map/ppermute | solution.py:232
  92.8 20.9 %collective-permute-start.12 = (bf16[384,384]{1,0:T(8,128)(2,1)S(1)}, bf16[384,384]{1,0:T(8,128)(2,1)S(1)}, u32[]{:S(2)}, u32[]{:S(2)}) collective-permute-start(bf16[384,384]{1,0:T(8,128)(2,1)S(1)} %get-tuple-element.169), channel_id=1, source_target_pairs={{0,16},{16,0},{1,17},{17,1},{2,18},{18,2},{3,19},{19,3},{4,20},{20... | collective-permute-start | bytes 884744 | tf_op jit(solution)/shard_map/ppermute | solution.py:223
  117.4 50.4 %collective-permute-start.13 = (bf16[896,768]{1,0:T(8,128)(2,1)}, bf16[896,768]{1,0:T(8,128)(2,1)}, u32[]{:S(2)}, u32[]{:S(2)}) collective-permute-start(bf16[896,768]{1,0:T(8,128)(2,1)} %pad_maximum_fusion), channel_id=1, source_target_pairs={{0,16},{16,0},{1,17},{17,1},{2,18},{18,2},{3,19},{19,3},{4,20},{20... | collective-permute-start | bytes 4128776 | tf_op jit(solution)/shard_map/ppermute | solution.py:223
  118.3 9.7 %collective-permute-start.31 = (bf16[2,56,768]{2,1,0:T(8,128)(2,1)S(1)}, bf16[2,56,768]{2,1,0:T(8,128)(2,1)S(1)}, u32[]{:S(2)}, u32[]{:S(2)}) collective-permute-start(bf16[2,56,768]{2,1,0:T(8,128)(2,1)S(1)} %get-tuple-element.196), channel_id=1, source_target_pairs={{0,16},{16,0},{1,17},{17,1},{2,18},{18,2},{3,19},{19,3},{4,20},{20... | collective-permute-start | bytes 516104 | tf_op jit(solution)/shard_map/ppermute | solution.py:223
  118.9 10.5 %collective-permute-start.29 = (bf16[2,56,768]{2,1,0:T(8,128)(2,1)S(1)}, bf16[2,56,768]{2,1,0:T(8,128)(2,1)}, u32[]{:S(2)}, u32[]{:S(2)}) collective-permute-start(bf16[2,56,768]{2,1,0:T(8,128)(2,1)S(1)} %pad.37), channel_id=1, source_target_pairs={{0,8},{4,12},{8,0},{12,4},{1,9},{5,13},{9,1},{13,5},{2,10},{6,14},... | collective-permute-start | bytes 516104 | tf_op jit(solution)/shard_map/ppermute | solution.py:226
  120.7 9.9 %collective-permute-start.30 = (bf16[2,56,768]{2,1,0:T(8,128)(2,1)S(1)}, bf16[2,56,768]{2,1,0:T(8,128)(2,1)}, u32[]{:S(2)}, u32[]{:S(2)}) collective-permute-start(bf16[2,56,768]{2,1,0:T(8,128)(2,1)S(1)} %pad.38), channel_id=1, source_target_pairs={{0,12},{4,8},{8,4},{12,0},{1,13},{5,9},{9,5},{13,1},{2,14},{6,10},... | collective-permute-start | bytes 516104 | tf_op jit(solution)/shard_map/ppermute | solution.py:226
  124.3 36.0 %collective-permute-start.23 = (bf16[6,96,768]{2,1,0:T(8,128)(2,1)}, bf16[6,96,768]{2,1,0:T(8,128)(2,1)}, u32[]{:S(2)}, u32[]{:S(2)}) collective-permute-start(bf16[6,96,768]{2,1,0:T(8,128)(2,1)} %pad_maximum_fusion.6), channel_id=1, source_target_pairs={{0,8},{4,12},{8,0},{12,4},{16,20},{20,16},{24,28},{28,24},{1,9},{5... | collective-permute-start | bytes 2654216 | tf_op jit(solution)/shard_map/ppermute | solution.py:232
  127.9 36.1 %collective-permute-start.18 = (bf16[6,48,1536]{2,1,0:T(8,128)(2,1)}, bf16[6,48,1536]{2,1,0:T(8,128)(2,1)}, u32[]{:S(2)}, u32[]{:S(2)}) collective-permute-start(bf16[6,48,1536]{2,1,0:T(8,128)(2,1)} %pad_maximum_fusion.5), channel_id=1, source_target_pairs={{0,8},{4,12},{8,0},{12,4},{16,20},{20,16},{24,28},{28,24},{1,9},{5... | collective-permute-start | bytes 2654216 | tf_op jit(solution)/shard_map/ppermute | solution.py:232
  129.3 7.6 %collective-permute-start.28 = (bf16[2,56,768]{2,1,0:T(8,128)(2,1)}, bf16[2,56,768]{2,1,0:T(8,128)(2,1)}, u32[]{:S(2)}, u32[]{:S(2)}) collective-permute-start(bf16[2,56,768]{2,1,0:T(8,128)(2,1)} %pad.36), channel_id=1, source_target_pairs={{0,4},{4,0},{8,12},{12,8},{1,5},{5,1},{9,13},{13,9},{2,6},{6,2},{1... | collective-permute-start | bytes 516104 | tf_op jit(solution)/shard_map/ppermute | solution.py:226
  130.6 18.8 %collective-permute-start.33 = (bf16[2,56,768]{2,1,0:T(8,128)(2,1)}, bf16[2,56,768]{2,1,0:T(8,128)(2,1)}, u32[]{:S(2)}, u32[]{:S(2)}) collective-permute-start(bf16[2,56,768]{2,1,0:T(8,128)(2,1)} %collective-permute-done.29), channel_id=1, source_target_pairs={{0,16},{16,0},{1,17},{17,1},{2,18},{18,2},{3,19},{19,3},{4,20},{20... | collective-permute-start | bytes 516104 | tf_op jit(solution)/shard_map/ppermute | solution.py:223
  137.0 19.3 %collective-permute-start.34 = (bf16[2,56,768]{2,1,0:T(8,128)(2,1)}, bf16[2,56,768]{2,1,0:T(8,128)(2,1)}, u32[]{:S(2)}, u32[]{:S(2)}) collective-permute-start(bf16[2,56,768]{2,1,0:T(8,128)(2,1)} %collective-permute-done.30), channel_id=1, source_target_pairs={{0,16},{16,0},{1,17},{17,1},{2,18},{18,2},{3,19},{19,3},{4,20},{20... | collective-permute-start | bytes 516104 | tf_op jit(solution)/shard_map/ppermute | solution.py:223
  187.7 16.5 %collective-permute-start.56 = (bf16[2,2,96,1536]{3,2,1,0:T(8,128)(2,1)}, bf16[2,2,96,1536]{3,2,1,0:T(8,128)(2,1)}, u32[]{:S(2)}, u32[]{:S(2)}) collective-permute-start(bf16[2,2,96,1536]{3,2,1,0:T(8,128)(2,1)} %pad_maximum_fusion.2), channel_id=1, source_target_pairs={{0,4},{4,0},{8,12},{12,8},{16,24},{20,28},{24,16},{28,20},{1,5},{5... | collective-permute-start | bytes 3538952 | tf_op jit(solution)/shard_map/ppermute | solution.py:232
  194.4 14.2 %collective-permute-start.35 = (bf16[896,768]{1,0:T(8,128)(2,1)}, bf16[896,768]{1,0:T(8,128)(2,1)}, u32[]{:S(2)}, u32[]{:S(2)}) collective-permute-start(bf16[896,768]{1,0:T(8,128)(2,1)} %pad_maximum_fusion.1), channel_id=1, source_target_pairs={{0,16},{16,0},{1,17},{17,1},{2,18},{18,2},{3,19},{19,3},{4,20},{20... | collective-permute-start | bytes 4128776 | tf_op jit(solution)/shard_map/ppermute | solution.py:223
  200.9 89.0 %collective-permute-start.24 = (bf16[448,768]{1,0:T(8,128)(2,1)}, bf16[448,768]{1,0:T(8,128)(2,1)}, u32[]{:S(2)}, u32[]{:S(2)}) collective-permute-start(bf16[448,768]{1,0:T(8,128)(2,1)} %slice.406), channel_id=1, source_target_pairs={{0,16},{16,0},{1,17},{17,1},{2,18},{18,2},{3,19},{19,3},{4,20},{20... | collective-permute-start | bytes 2064392 | tf_op jit(solution)/shard_map/ppermute | solution.py:223
  207.0 56.6 %collective-permute-start.57 = (bf16[2,96,1536]{2,1,0:T(8,128)(2,1)}, bf16[2,96,1536]{2,1,0:T(8,128)(2,1)}, u32[]{:S(2)}, u32[]{:S(2)}) collective-permute-start(bf16[2,96,1536]{2,1,0:T(8,128)(2,1)} %fusion.28), channel_id=1, source_target_pairs={{0,8},{4,12},{8,0},{12,4},{16,20},{20,16},{24,28},{28,24},{1,9},{5... | collective-permute-start | bytes 1769480 | tf_op jit(solution)/shard_map/ppermute | solution.py:232
  242.6 20.0 %collective-permute-start.51 = (bf16[2,1,96,768]{3,2,1,0:T(8,128)(2,1)S(1)}, bf16[2,1,96,768]{3,2,1,0:T(8,128)(2,1)S(1)}, u32[]{:S(2)}, u32[]{:S(2)}) collective-permute-start(bf16[2,1,96,768]{3,2,1,0:T(8,128)(2,1)S(1)} %pad_maximum_fusion.15), channel_id=1, source_target_pairs={{0,4},{4,0},{8,12},{12,8},{16,24},{20,28},{24,16},{28,20},{1,5},{5... | collective-permute-start | bytes 884744 | tf_op jit(solution)/shard_map/ppermute | solution.py:232
  251.9 38.0 %collective-permute-start.36 = (bf16[448,768]{1,0:T(8,128)(2,1)}, bf16[448,768]{1,0:T(8,128)(2,1)}, u32[]{:S(2)}, u32[]{:S(2)}) collective-permute-start(bf16[448,768]{1,0:T(8,128)(2,1)} %slice.405), channel_id=1, source_target_pairs={{0,16},{16,0},{1,17},{17,1},{2,18},{18,2},{3,19},{19,3},{4,20},{20... | collective-permute-start | bytes 2064392 | tf_op jit(solution)/shard_map/ppermute | solution.py:223
  264.9 8.6 %collective-permute-start.58 = (bf16[2,24,1536]{2,1,0:T(8,128)(2,1)S(1)}, bf16[2,24,1536]{2,1,0:T(8,128)(2,1)S(1)}, u32[]{:S(2)}, u32[]{:S(2)}) collective-permute-start(bf16[2,24,1536]{2,1,0:T(8,128)(2,1)S(1)} %get-tuple-element.142), channel_id=1, source_target_pairs={{0,1},{1,2},{2,3},{3,0},{4,5},{5,6},{6,7},{7,4},{8,9},{9,10},{10,1... | collective-permute-start | bytes 442376 | tf_op jit(solution)/shard_map/ppermute | solution.py:229
  265.2 9.4 %collective-permute-start.60 = (bf16[2,24,1536]{2,1,0:T(8,128)(2,1)S(1)}, bf16[2,24,1536]{2,1,0:T(8,128)(2,1)S(1)}, u32[]{:S(2)}, u32[]{:S(2)}) collective-permute-start(bf16[2,24,1536]{2,1,0:T(8,128)(2,1)S(1)} %get-tuple-element.143), channel_id=1, source_target_pairs={{0,3},{1,0},{2,1},{3,2},{4,7},{5,4},{6,5},{7,6},{8,11},{9,8},{10,9... | collective-permute-start | bytes 442376 | tf_op jit(solution)/shard_map/ppermute | solution.py:229
  269.0 13.1 %collective-permute-start.59 = (bf16[2,24,1536]{2,1,0:T(8,128)(2,1)S(1)}, bf16[2,24,1536]{2,1,0:T(8,128)(2,1)S(1)}, u32[]{:S(2)}, u32[]{:S(2)}) collective-permute-start(bf16[2,24,1536]{2,1,0:T(8,128)(2,1)S(1)} %get-tuple-element.144), channel_id=1, source_target_pairs={{0,2},{1,3},{2,0},{3,1},{4,6},{5,7},{6,4},{7,5},{8,10},{9,11},{10,... | collective-permute-start | bytes 442376 | tf_op jit(solution)/shard_map/ppermute | solution.py:229
  273.5 8.6 %collective-permute-start.53 = (bf16[1,24,768]{2,1,0:T(8,128)(2,1)S(1)}, bf16[1,24,768]{2,1,0:T(8,128)(2,1)S(1)}, u32[]{:S(2)}, u32[]{:S(2)}) collective-permute-start(bf16[1,24,768]{2,1,0:T(8,128)(2,1)S(1)} %get-tuple-element.192), channel_id=1, source_target_pairs={{0,1},{1,2},{2,3},{3,0},{4,5},{5,6},{6,7},{7,4},{8,9},{9,10},{10,1... | collective-permute-start | bytes 110600 | tf_op jit(solution)/shard_map/ppermute | solution.py:229
  274.6 9.0 %collective-permute-start.55 = (bf16[1,24,768]{2,1,0:T(8,128)(2,1)S(1)}, bf16[1,24,768]{2,1,0:T(8,128)(2,1)S(1)}, u32[]{:S(2)}, u32[]{:S(2)}) collective-permute-start(bf16[1,24,768]{2,1,0:T(8,128)(2,1)S(1)} %get-tuple-element.193), channel_id=1, source_target_pairs={{0,3},{1,0},{2,1},{3,2},{4,7},{5,4},{6,5},{7,6},{8,11},{9,8},{10,9... | collective-permute-start | bytes 110600 | tf_op jit(solution)/shard_map/ppermute | solution.py:229
  282.1 49.8 %collective-permute-start.45 = (bf16[2,2,96,1152]{3,2,1,0:T(8,128)(2,1)}, bf16[2,2,96,1152]{3,2,1,0:T(8,128)(2,1)}, u32[]{:S(2)}, u32[]{:S(2)}) collective-permute-start(bf16[2,2,96,1152]{3,2,1,0:T(8,128)(2,1)} %pad_maximum_fusion.7), channel_id=1, source_target_pairs={{0,4},{4,0},{8,12},{12,8},{16,24},{20,28},{24,16},{28,20},{1,5},{5... | collective-permute-start | bytes 2654216 | tf_op jit(solution)/shard_map/ppermute | solution.py:232
  283.6 55.6 %collective-permute-start.62 = (bf16[2,2,96,1536]{3,2,1,0:T(8,128)(2,1)}, bf16[2,2,96,1536]{3,2,1,0:T(8,128)(2,1)}, u32[]{:S(2)}, u32[]{:S(2)}) collective-permute-start(bf16[2,2,96,1536]{3,2,1,0:T(8,128)(2,1)} %pad_maximum_fusion.3), channel_id=1, source_target_pairs={{0,4},{4,0},{8,12},{12,8},{16,24},{20,28},{24,16},{28,20},{1,5},{5... | collective-permute-start | bytes 3538952 | tf_op jit(solution)/shard_map/ppermute | solution.py:232
  297.3 13.8 %collective-permute-start.41 = (f32[13440]{0:T(1024)S(1)}, f32[13440]{0:T(1024)S(1)}, u32[]{:S(2)}, u32[]{:S(2)}) collective-permute-start(f32[13440]{0:T(1024)S(1)} %add.649), channel_id=1, source_target_pairs={{0,4},{4,0},{8,12},{12,8},{1,5},{5,1},{9,13},{13,9},{2,6},{6,2},{1... | collective-permute-start | bytes 161288 | tf_op jit(solution)/shard_map/ppermute | solution.py:226
  299.2 17.7 %collective-permute-start.38 = (bf16[2,56,768]{2,0,1:T(2,128)(2,1)S(1)}, bf16[2,56,768]{2,0,1:T(2,128)(2,1)S(1)}, u32[]{:S(2)}, u32[]{:S(2)}) collective-permute-start(bf16[2,56,768]{2,0,1:T(2,128)(2,1)S(1)} %bitcast.437), channel_id=1, source_target_pairs={{0,8},{4,12},{8,0},{12,4},{1,9},{5,13},{9,1},{13,5},{2,10},{6,14},... | collective-permute-start | bytes 516104 | tf_op jit(solution)/shard_map/ppermute | solution.py:226
  300.2 17.7 %collective-permute-start.37 = (bf16[2,56,768]{2,0,1:T(2,128)(2,1)S(1)}, bf16[2,56,768]{2,0,1:T(2,128)(2,1)S(1)}, u32[]{:S(2)}, u32[]{:S(2)}) collective-permute-start(bf16[2,56,768]{2,0,1:T(2,128)(2,1)S(1)} %bitcast.436), channel_id=1, source_target_pairs={{0,12},{4,8},{8,4},{12,0},{1,13},{5,9},{9,5},{13,1},{2,14},{6,10},... | collective-permute-start | bytes 516104 | tf_op jit(solution)/shard_map/ppermute | solution.py:226
  316.9 10.5 %collective-permute-start.26 = (bf16[2,56,768]{2,0,1:T(2,128)(2,1)S(1)}, bf16[2,56,768]{2,0,1:T(2,128)(2,1)S(1)}, u32[]{:S(2)}, u32[]{:S(2)}) collective-permute-start(bf16[2,56,768]{2,0,1:T(2,128)(2,1)S(1)} %bitcast.432), channel_id=1, source_target_pairs={{0,8},{4,12},{8,0},{12,4},{1,9},{5,13},{9,1},{13,5},{2,10},{6,14},... | collective-permute-start | bytes 516104 | tf_op jit(solution)/shard_map/ppermute | solution.py:226
  317.9 11.0 %collective-permute-start.27 = (bf16[2,56,768]{2,0,1:T(2,128)(2,1)S(1)}, bf16[2,56,768]{2,0,1:T(2,128)(2,1)S(1)}, u32[]{:S(2)}, u32[]{:S(2)}) collective-permute-start(bf16[2,56,768]{2,0,1:T(2,128)(2,1)S(1)} %bitcast.430), channel_id=1, source_target_pairs={{0,4},{4,0},{8,12},{12,8},{1,5},{5,1},{9,13},{13,9},{2,6},{6,2},{1... | collective-permute-start | bytes 516104 | tf_op jit(solution)/shard_map/ppermute | solution.py:226
  336.5 8.4 %collective-permute-start.46 = (bf16[2,96,1152]{2,1,0:T(8,128)(2,1)S(1)}, bf16[2,96,1152]{2,1,0:T(8,128)(2,1)S(1)}, u32[]{:S(2)}, u32[]{:S(2)}) collective-permute-start(bf16[2,96,1152]{2,1,0:T(8,128)(2,1)S(1)} %fusion.31), channel_id=1, source_target_pairs={{0,8},{4,12},{8,0},{12,4},{16,20},{20,16},{24,28},{28,24},{1,9},{5... | collective-permute-start | bytes 1327112 | tf_op jit(solution)/shard_map/ppermute | solution.py:232
  341.8 15.4 %collective-permute-start.63 = (bf16[2,96,1536]{2,1,0:T(8,128)(2,1)}, bf16[2,96,1536]{2,1,0:T(8,128)(2,1)}, u32[]{:S(2)}, u32[]{:S(2)}) collective-permute-start(bf16[2,96,1536]{2,1,0:T(8,128)(2,1)} %fusion.29), channel_id=1, source_target_pairs={{0,8},{4,12},{8,0},{12,4},{16,20},{20,16},{24,28},{28,24},{1,9},{5... | collective-permute-start | bytes 1769480 | tf_op jit(solution)/shard_map/ppermute | solution.py:232
  362.3 8.9 %collective-permute-start.65 = (bf16[2,24,1536]{2,1,0:T(8,128)(2,1)S(1)}, bf16[2,24,1536]{2,1,0:T(8,128)(2,1)S(1)}, u32[]{:S(2)}, u32[]{:S(2)}) collective-permute-start(bf16[2,24,1536]{2,1,0:T(8,128)(2,1)S(1)} %get-tuple-element.141), channel_id=1, source_target_pairs={{0,2},{1,3},{2,0},{3,1},{4,6},{5,7},{6,4},{7,5},{8,10},{9,11},{10,... | collective-permute-start | bytes 442376 | tf_op jit(solution)/shard_map/ppermute | solution.py:229
  362.3 9.0 %collective-permute-start.50 = (f32[24,1152]{1,0:T(8,128)S(1)}, f32[24,1152]{1,0:T(8,128)S(1)}, u32[]{:S(2)}, u32[]{:S(2)}) collective-permute-start(f32[24,1152]{1,0:T(8,128)S(1)} %dynamic-slice_bitcast_fusion.22), channel_id=1, source_target_pairs={{0,16},{16,0},{1,17},{17,1},{2,18},{18,2},{3,19},{19,3},{4,20},{20... | collective-permute-start | bytes 331784 | tf_op jit(solution)/shard_map/ppermute | solution.py:223
  (107 other events, 625.4 us)

commit v2 on v1

v2 whole, which is shorter than its diff:
```python
import functools

import jax
import jax.numpy as jnp
from jax import lax
from jax.experimental import pallas as pl
from jax.experimental.pallas import tpu as pltpu
from jax.sharding import PartitionSpec as P

D = 768
HD = 64
FF = 3072
WIN = 14
GRID = 48
NWS = 4
TOK = 49
PAD = 56
ROWS = 4 * PAD
SPLIT = 4 * TOK
HALF = D // 2
QKV = 3 * HALF
WIDE = 4 * HALF
PIECE = 48
PAIRS = 3
LANES = 128
TAB = 512
NEG = -1e30
EPS = 1e-06
SCALE = HD**-0.5
BF = jnp.bfloat16
F32 = jnp.float32
ANY = pl.BlockSpec(memory_space=pl.ANY)
HBM = pl.BlockSpec(memory_space=pltpu.HBM)
SMEM = pl.BlockSpec(memory_space=pltpu.SMEM)


def mm(left, right, dims=((1,), (0,))):
    return lax.dot_general(left, right, (dims, ((), ())), preferred_element_type=F32)


def array(shape, dtype=BF):
    return jax.ShapeDtypeStruct(shape, dtype)


def whole(shape):
    return pl.BlockSpec(shape, lambda *at: (0,) * len(shape))


def window(shape, index=None):
    index = index or (lambda w: w)
    return pl.BlockSpec((1,) + shape, lambda w: (index(w),) + (0,) * len(shape))


TIMES = dict(cut=0.3, join=0.3, pair_up=0.3, weld=0.3, norm_one=0.3, place_qp=0.3)


def call(kernel, name, ins, outs, grid=(), scratch=(), after=(), vmem=8, alias=()):
    count = len(ins)
    extra = len(after)

    def held(v):
        mode = pl.Buffered(1) if grid else None
        return pl.BlockSpec(v.shape, lambda *at: (0,) * len(v.shape), pipeline_mode=mode)

    def body(*refs):
        return kernel(*refs[:count], *refs[count + extra :])

    return pl.pallas_call(
        body,
        grid=grid,
        in_specs=[spec or held(v) for v, spec in ins] + [ANY] * extra,
        out_specs=[spec or whole(v.shape) for v, spec in outs],
        out_shape=[v for v, _ in outs],
        scratch_shapes=list(scratch),
        compiler_params=pltpu.CompilerParams(vmem_limit_bytes=vmem * 1024 * 1024),
        input_output_aliases=dict(alias),
        cost_estimate=pl.CostEstimate(
            flops=int(1.15e9 * TIMES.get(name, 87.0)),
            bytes_accessed=int(1.15e6 * TIMES.get(name, 87.0)),
            transcendentals=0,
        ),
        name=name,
    )(*[v for v, _ in ins], *after)


def pieces_kernel(where, qkv, proj, hidden, output, out, qp_out, sems):
    s, c = where[1], where[5]
    rows = pl.ds(pl.multiple_of(s * PIECE, PIECE), PIECE)
    start = pl.multiple_of(c * HALF + s * 2 * PIECE, 2 * PIECE)
    copies = [(output.at[pl.ds(start, 2 * PIECE)], out.at[: 2 * PIECE])]
    for i in range(4):
        cols = pl.ds(pl.multiple_of(i * D + c * HALF, LANES), HALF)
        at = (2 + i // 2) * PIECE
        half = slice(i % 2 * HALF, (i % 2 + 1) * HALF)
        copies.append((hidden.at[rows, cols], out.at[at : at + PIECE, half]))
    for i in range(3):
        cols = pl.ds(pl.multiple_of(i * D + c * HALF, LANES), HALF)
        copies.append((qkv.at[rows, cols], qp_out.at[:, i * HALF : (i + 1) * HALF]))
    cols = pl.ds(pl.multiple_of(c * HALF, LANES), HALF)
    copies.append((proj.at[rows, cols], qp_out.at[:, QKV:]))
    run_copies(copies, sems)


def run_copies(pairs, sems):
    copies = [
        pltpu.make_async_copy(src, dst, sems.at[n]) for n, (src, dst) in enumerate(pairs)
    ]
    for copy in copies:
        copy.start()
    for copy in copies:
        copy.wait()


def pieces(where, qkv, proj, hidden, output):
    return call(
        pieces_kernel,
        "pieces",
        [(where, SMEM), (qkv, HBM), (proj, HBM), (hidden, HBM), (output, HBM)],
        [(array((4 * PIECE, D)), None), (array((PIECE, WIDE)), None)],
        scratch=[pltpu.SemaphoreType.DMA((9,))],
        vmem=60,
    )


def output_part(w, first=0, count=16):
    return w[first : first + count, : 2 * PIECE, :].reshape(count * 2 * PIECE, D)


def hidden_part(w, half):
    at = (2 + half) * PIECE
    return w[:, at : at + PIECE, :].reshape(D, D)


def join_kernel(one, two, three, out):
    out[0] = one[...]
    out[1] = two[...]
    out[2] = three[...]


def join(parts, after=()):
    return call(
        join_kernel,
        "join",
        [(part, None) for part in parts],
        [(array((3,) + parts[0].shape), None)],
        after=after,
    )[0]


def place_qp_kernel(where, qkv, proj, first, second, third, fourth, out, send, sems):
    z, c = where[0], where[5]
    copies = []

    def add(src, dst):
        copies.append(pltpu.make_async_copy(src, dst, sems.at[len(copies)]))

    for i in range(3):
        for q in range(4):
            cols = pl.ds(pl.multiple_of(i * D + c * HALF, LANES), HALF)
            add(
                qkv.at[q * PIECE : (q + 1) * PIECE, cols],
                out.at[z, q, :, i * HALF : (i + 1) * HALF],
            )
    for q in range(4):
        cols = pl.ds(pl.multiple_of(c * HALF, LANES), HALF)
        add(proj.at[q * PIECE : (q + 1) * PIECE, cols], out.at[z, q, :, QKV:])
    for i in range(3):
        zz = lax.rem(z + 3 - i, 4)
        for n, src in enumerate((first, second, third, fourth)):
            add(src.at[i], out.at[zz, where[1 + n]])
    for copy in copies:
        copy.start()
    for copy in copies:
        copy.wait()
    send[...] = out[pl.ds(2 * (1 - c), 2), :, :, QKV:]


def place_ho_kernel(where, hidden, output, first, second, third, fourth, out, sems):
    z, c = where[0], where[5]
    copies = []
    for q in range(4):
        start = pl.multiple_of(c * HALF + q * 2 * PIECE, 2 * PIECE)
        copies.append((output.at[pl.ds(start, 2 * PIECE)], out.at[z, q, : 2 * PIECE]))
        for i in range(4):
            cols = pl.ds(pl.multiple_of(i * D + c * HALF, LANES), HALF)
            at = (2 + i // 2) * PIECE
            half = slice(i % 2 * HALF, (i % 2 + 1) * HALF)
            copies.append(
                (
                    hidden.at[q * PIECE : (q + 1) * PIECE, cols],
                    out.at[z, q, at : at + PIECE, half],
                )
            )
    for i in range(3):
        zz = lax.rem(z + 3 - i, 4)
        for n, src in enumerate((first, second, third, fourth)):
            copies.append((src.at[i], out.at[zz, where[1 + n]]))
    run_copies(copies, sems)


def hand_out(c, rows, i, outs):
    near, both, far = outs

    def piece(k):
        return rows[pl.ds(pl.multiple_of(k * PAD, 8), PAD), :].astype(BF)

    near[i] = piece(0)
    both[0, i] = piece(1 + c)
    both[1, i] = piece(3)
    far[i] = piece(2 - c)


def handed(images):
    shape = (images, PAD, D)
    return [(array(shape), None), (array((2,) + shape), None), (array(shape), None)]


ROWS_F32 = pltpu.VMEM((ROWS, D), F32)


def gathered_rows(c, near, one, two, i):
    first, second = one[0, i].astype(F32), two[0, i].astype(F32)
    parts = [near[i].astype(F32)]
    parts += [jnp.where(c == 0, first, second), jnp.where(c == 0, second, first)]
    return jnp.concatenate(parts + [two[1, i].astype(F32)])


def pair_kernel(far, one, out):
    out[0] = far[...]
    out[1] = one[1]


def pair_up(far, one, after=()):
    return call(
        pair_kernel,
        "pair_up",
        [(far, None), (one, None)],
        [(array((2,) + far.shape), None)],
        after=after,
    )[0]


def cut_kernel(where, tokens, cotangent, *rest):
    s, c = where[1], where[5]
    images = tokens.shape[0]
    outs, rows = rest[:3], rest[3]
    row = lax.broadcasted_iota(jnp.int32, (ROWS, SPLIT), 0)
    col = lax.broadcasted_iota(jnp.int32, (ROWS, SPLIT), 1)
    token = row % PAD
    take = ((token < TOK) & (col == token * 4 + (s ^ (row // PAD)))).astype(F32).astype(BF)
    for i in range(2 * images):
        rows[...] = mm(take, tokens[i] if i < images else cotangent[i - images])
        hand_out(c, rows, i, outs)


def cut(where, tokens, cotangent, after=()):
    images = tokens.shape[0]
    flat = [jnp.transpose(v, (0, 2, 1, 3)).reshape(images, SPLIT, D) for v in (tokens, cotangent)]
    return call(
        cut_kernel,
        "cut",
        [(where, SMEM)] + [(v, None) for v in flat],
        handed(2 * images),
        scratch=[ROWS_F32],
        after=after,
        vmem=12,
    )


def weld_kernel(where, ok, near, one, two, out):
    count = out.shape[0]
    for i in range(count):
        rows = gathered_rows(where[5], near, one, two, i)
        out[i] = (rows if i < count // 2 else rows * ok[...]).astype(BF)


def weld(where, ok, near, one, two, after=()):
    return call(
        weld_kernel,
        "weld",
        [(where, SMEM), (ok, None)] + [(part, None) for part in (near, one, two)],
        [(array((near.shape[0], ROWS, D)), None)],
        after=after,
    )[0]


def home_kernel(where, near, one, two, *outs):
    s = where[1]
    row = lax.broadcasted_iota(jnp.int32, (SPLIT, ROWS), 0)
    col = lax.broadcasted_iota(jnp.int32, (SPLIT, ROWS), 1)
    token = col % PAD
    take = ((token < TOK) & (row == token * 4 + (s ^ (col // PAD)))).astype(F32).astype(BF)
    images = outs[0].shape[0]
    for i in range(2 * images):
        rows = gathered_rows(where[5], near, one, two, i).astype(BF)
        outs[i // images][i % images] = mm(take, rows).astype(BF)


def home(where, near, one, two, after=()):
    images = near.shape[0] // 2
    flat = call(
        home_kernel,
        "home",
        [(where, SMEM)] + [(part, None) for part in (near, one, two)],
        [(array((images, SPLIT, D)), None)] * 2,
        after=after,
        vmem=12,
    )
    return [jnp.transpose(v.reshape(images, TOK, 4, D), (0, 2, 1, 3)) for v in flat]


def unit_of(v):
    v = v - jnp.mean(v, axis=-1, keepdims=True)
    rstd = lax.rsqrt(jnp.mean(v * v, axis=-1, keepdims=True) + EPS)
    return v * rstd, rstd


def norm_back(grad, unit, rstd):
    return rstd * (
        grad
        - jnp.mean(grad, axis=-1, keepdims=True)
        - unit * jnp.mean(grad * unit, axis=-1, keepdims=True)
    )


def norm_one_kernel(ok, own, other, gain, shift, out):
    images = own.shape[0] // 2
    for w in range(2 * images):
        x = own[w] if w < images else other[w - images]
        unit, _ = unit_of(x.astype(F32))
        out[w] = ((unit * gain[...] + shift[...]) * ok[...]).astype(BF)


def norm_one(ok, own, other, gain, shift, after=()):
    return call(
        norm_one_kernel,
        "norm_one",
        [(v, None) for v in (ok, own, other, gain, shift)],
        [(array(own.shape), None)],
        after=after,
        vmem=12,
    )[0]


def norm_two_kernel(
    own, other, branch, branch_other, there, bias, gain, shift, middle, second
):
    images = own.shape[0] // 2
    for w in range(2 * images):
        x, mine = (own, branch) if w < images else (other, branch_other)
        at = w % images
        value = x[at].astype(F32) + (mine[at] + there[w].astype(F32)) + bias[...]
        middle[w] = value
        unit, _ = unit_of(value)
        second[w] = (unit * gain[...] + shift[...]).astype(BF)


def norm_two(own, other, branch, branch_other, there, bias, gain, shift, after=()):
    shape = own.shape
    ins = (own, other, branch, branch_other, there, bias, gain, shift)
    return call(
        norm_two_kernel,
        "norm_two",
        [(v, None) for v in ins],
        [(array(shape, F32), None), (array(shape), None)],
        after=after,
        vmem=14,
    )


def norm_two_back_kernel(
    images, part, there, middle, gain, feed, feed_other, grad_middle, grad_branch, sums
):
    sums[...] = jnp.zeros_like(sums)
    for w in range(2 * images):
        grad = part[w] + there[w].astype(F32)
        unit, rstd = unit_of(middle[w])
        feed_w = (feed[images + w] if w < images else feed_other[w]).astype(F32)
        total = feed_w + norm_back(grad * gain[...], unit, rstd)
        low = total.astype(BF)
        grad_branch[w] = low
        if w < images:
            grad_middle[w] = total
            sums[0:1] += jnp.sum(grad * unit, axis=0, keepdims=True)
            sums[1:2] += jnp.sum(grad, axis=0, keepdims=True)
            sums[2:3] += jnp.sum(low.astype(F32), axis=0, keepdims=True)
            sums[3:4] += jnp.sum(feed_w, axis=0, keepdims=True)


def norm_two_back(part, there, middle, gain, feed, feed_other, after=()):
    count = part.shape[0]
    return call(
        functools.partial(norm_two_back_kernel, count // 2),
        "norm_two_back",
        [(v, None) for v in (part, there, middle, gain, feed, feed_other)],
        [
            (array((count // 2, ROWS, D), F32), None),
            (array((count, ROWS, D)), None),
            (array((8, D), F32), None),
        ],
        after=after,
        vmem=16,
    )


def last_kernel(
    where, ok, back, back_there, own, gain, grad_middle, middle, feed, feed_there, bias, *rest
):
    outs, sums, rows = rest[:3], rest[3], rest[4]
    images = back.shape[0]
    sums[...] = jnp.zeros_like(sums)
    for w in range(images):
        grad = (back[w] + back_there[w].astype(F32)) * ok[...]
        unit, rstd = unit_of(own[w].astype(F32))
        sums[0:1] += jnp.sum(grad * unit, axis=0, keepdims=True)
        sums[1:2] += jnp.sum(grad, axis=0, keepdims=True)
        rows[...] = grad_middle[w] + norm_back(grad * gain[...], unit, rstd)
        hand_out(where[5], rows, w, outs)
        rows[...] = (middle[w] + feed[w] + feed_there[w].astype(F32) + bias[...]) * ok[...]
        hand_out(where[5], rows, images + w, outs)


def last(where, ok, back, back_there, own, gain, grad_middle, middle, feed, feed_there, bias, after=()):
    ins = (ok, back, back_there, own, gain, grad_middle, middle, feed, feed_there, bias)
    return call(
        last_kernel,
        "last",
        [(where, SMEM)] + [(v, None) for v in ins],
        handed(own.shape[0]) + [(array((8, D), F32), None)],
        scratch=[ROWS_F32],
        after=after,
        vmem=20,
    )


def attn_fwd_kernel(
    where, normed, w_qp, other, b_qkv, table, spot, fold, keys, bias, *rest
):
    packed, out, probs, low, branch = rest[-5:]
    c = where[5]
    lane = lax.broadcasted_iota(jnp.int32, (ROWS, LANES), 1)
    packed[0] = (mm(normed[0], w_qp[:, :QKV]) + b_qkv[...]).astype(BF)
    for pair in range(PAIRS):
        q = packed[0, :, pair * LANES : (pair + 1) * LANES]
        k = packed[0, :, HALF + pair * LANES : HALF + (pair + 1) * LANES]
        v = packed[0, :, 2 * HALF + pair * LANES : 2 * HALF + (pair + 1) * LANES]
        right = jnp.concatenate([k, keys[...]], axis=1)
        parts = []
        for e in range(2):
            mine = (lane < HD) if e == 0 else (lane >= HD)
            spread = (mm(q, table[e]) * spot[...]).astype(BF)
            rel = mm(spread, fold[...]).astype(BF)
            scaled = jnp.where(mine, q.astype(F32) * SCALE, 0.0).astype(BF)
            left = jnp.concatenate([scaled, rel], axis=1)
            s = mm(left, right, ((1,), (1,))) + bias[...]
            p = jnp.exp(s - jnp.max(s, axis=1, keepdims=True))
            p = (p * (1.0 / jnp.sum(p, axis=1, keepdims=True))).astype(BF)
            probs[0, 2 * pair + e] = p
            parts.append(mm(p, v))
        out[0, :, pair * LANES : (pair + 1) * LANES] = jnp.where(
            lane < HD, parts[0], parts[1]
        ).astype(BF)
    att = out[0]
    own_cols = pl.ds(pl.multiple_of(c * HALF, LANES), HALF)
    other_cols = pl.ds(pl.multiple_of((1 - c) * HALF, LANES), HALF)
    own_rows = pl.ds(pl.multiple_of(c * HALF, HALF), HALF)
    mine = mm(att, w_qp[own_rows, QKV:])
    theirs = mm(att, other[...])
    branch[0, :, own_cols] = mine
    branch[0, :, other_cols] = theirs
    low[0, :, own_cols] = mine.astype(BF)
    low[0, :, other_cols] = theirs.astype(BF)


def attn_fwd(where, group, normed, w_qp, other, b_qkv, tables, before=(), after=()):
    table, spot, fold, keys, bias = tables
    count = normed.shape[0]
    half = count // 2
    start = group * half
    ins = [(where, SMEM), (normed, window((ROWS, D), lambda w: w + start))]
    ins += [(v, None) for v in (w_qp, other, b_qkv, table, spot, fold, keys, bias)]
    kept = ((ROWS, QKV), (ROWS, HALF), (2 * PAIRS, ROWS, ROWS))
    outs = [(array((count,) + shape), window(shape, lambda w: w + start)) for shape in kept]
    outs += [
        (array((count, ROWS, D)), window((ROWS, D), lambda w: (w + start + half) % count)),
        (array((half, ROWS, D), F32), window((ROWS, D))),
    ]
    return call(
        attn_fwd_kernel,
        "attn_fwd",
        ins + [(v, ANY) for v in before],
        outs,
        grid=(half,),
        after=after,
        alias=[(len(ins) + n, n) for n in range(len(before))],
        vmem=18,
    )


def attn_bwd_kernel(
    where, packed, grad_branch, probs, w_qp, other, table, spot, fold, keys, *rest
):
    out, tab_grad, sums, att = rest[-4:]
    c = where[5]
    lane = lax.broadcasted_iota(jnp.int32, (ROWS, LANES), 1)
    lane_t = lax.broadcasted_iota(jnp.int32, (TAB, LANES), 1)

    @pl.when(pl.program_id(0) == 0)
    def _():
        tab_grad[...] = jnp.zeros_like(tab_grad)
        sums[...] = jnp.zeros_like(sums)

    own_cols = pl.ds(pl.multiple_of(c * HALF, LANES), HALF)
    other_cols = pl.ds(pl.multiple_of((1 - c) * HALF, LANES), HALF)
    own_rows = pl.ds(pl.multiple_of(c * HALF, HALF), HALF)
    att[...] = (
        mm(grad_branch[0, :, own_cols], w_qp[own_rows, QKV:], ((1,), (1,)))
        + mm(grad_branch[0, :, other_cols], other[...], ((1,), (1,)))
    ).astype(BF)
    for pair in range(PAIRS):
        q = packed[0, :, pair * LANES : (pair + 1) * LANES]
        k = packed[0, :, HALF + pair * LANES : HALF + (pair + 1) * LANES]
        v = packed[0, :, 2 * HALF + pair * LANES : 2 * HALF + (pair + 1) * LANES]
        go = att[:, pair * LANES : (pair + 1) * LANES]
        right = jnp.concatenate([k, keys[...]], axis=1)
        dq, dk, dv, dt = [], [], [], []
        for e in range(2):
            mine = (lane < HD) if e == 0 else (lane >= HD)
            go_e = jnp.where(mine, go.astype(F32), 0.0).astype(BF)
            p_low = probs[0, 2 * pair + e]
            p = p_low.astype(F32)
            dp = mm(go_e, v, ((1,), (1,)))
            ds = (p * (dp - jnp.sum(dp * p, axis=1, keepdims=True))).astype(BF)
            both = mm(ds, right)
            rel = both[:, LANES:].astype(BF)
            spread = (mm(rel, fold[...], ((1,), (1,))) * spot[...]).astype(BF)
            dq.append(SCALE * both[:, :LANES] + mm(spread, table[e], ((1,), (1,))))
            dk.append(SCALE * mm(ds, q, ((0,), (0,))))
            dv.append(mm(p_low, go, ((0,), (0,))))
            dt.append(mm(spread, q, ((0,), (0,))))
        tab_grad[...] += jnp.where(lane_t < HD, dt[0], dt[1])
        for at, two in ((0, dq), (HALF, dk), (2 * HALF, dv)):
            low = jnp.where(lane < HD, two[0], two[1]).astype(BF)
            cols = slice(at + pair * LANES, at + (pair + 1) * LANES)
            out[0, :, cols] = low
            sums[0:1, cols] += jnp.sum(low.astype(F32), axis=0, keepdims=True)


def attn_bwd(where, group, packed, grad_branch, probs, w_qp, other, tables, before=(), after=()):
    table, spot, fold, keys, _ = tables
    count = packed.shape[0]
    half = count // 2
    start = group * half
    ins = [
        (where, SMEM),
        (packed, window((ROWS, QKV), lambda w: w + start)),
        (grad_branch, window((ROWS, D), lambda w: w + start)),
        (probs, window((2 * PAIRS, ROWS, ROWS), lambda w: w + start)),
    ]
    ins += [(v, None) for v in (w_qp, other, table, spot, fold, keys)]
    return call(
        attn_bwd_kernel,
        "attn_bwd",
        ins + [(v, ANY) for v in before],
        [
            (array((count, ROWS, QKV)), window((ROWS, QKV), lambda w: w + start)),
            (array((TAB, LANES), F32), None),
            (array((8, QKV), F32), None),
        ],
        grid=(half,),
        scratch=[pltpu.VMEM((ROWS, HALF), BF)],
        after=after,
        alias=[(len(ins) + n, n) for n in range(len(before))],
        vmem=18,
    )


def hidden_kernel(second, w, bias, active, slope):
    for half in range(2):
        cols = slice(half * D, (half + 1) * D)
        v = mm(second[0], hidden_part(w, half)) + bias[:, cols]
        phi = 0.5 * (1.0 + lax.erf(v * (0.5**0.5)))
        active[0, :, cols] = (v * phi).astype(BF)
        slope[0, :, cols] = (phi + v * (jnp.exp(-0.5 * v * v) * 0.3989422804014327)).astype(BF)


def hidden_layer(second, w_hidden, bias, after=()):
    count = second.shape[0]
    return call(
        hidden_kernel,
        "hidden",
        [(second, window((ROWS, D))), (w_hidden, None), (bias, None)],
        [(array((count, ROWS, WIDE)), window((ROWS, WIDE)))] * 2,
        grid=(count,),
        after=after,
        vmem=14,
    )


def product_kernel(of, count, left, right, own, low):
    w = pl.program_id(0)
    value = of(left[0], right)

    @pl.when(w < count // 2)
    def _():
        low[w] = value.astype(BF)

    @pl.when(w >= count // 2)
    def _():
        own[w - count // 2] = value


def product(name, left, right, right_spec, of, after=()):
    count = left.shape[0]
    shape = (count // 2, ROWS, D)
    return call(
        functools.partial(product_kernel, of, count),
        name,
        [(left, window(left.shape[1:], lambda w: (w + count // 2) % count)), (right, right_spec)],
        [(array(shape, F32), None), (array(shape), None)],
        grid=(count,),
        after=after,
        vmem=14,
    )


def grad_pre_kernel(count, own, other, slope, w, out, part, low, sums):
    feed = jnp.where(pl.program_id(0) < count // 2, own[0].astype(F32), other[0].astype(F32))
    feed = feed.astype(BF)

    @pl.when(pl.program_id(0) == 0)
    def _():
        sums[...] = jnp.zeros_like(sums)

    for half in range(2):
        cols = slice(half * D, (half + 1) * D)
        value = mm(feed, output_part(w, 8 * half, 8), ((1,), (1,))) * slope[0, :, cols].astype(F32)
        value = value.astype(BF)
        out[0, :, cols] = value
        sums[0:1, cols] += jnp.sum(value.astype(F32), axis=0, keepdims=True)
    value = mm(out[0, :, :D], hidden_part(w, 0), ((1,), (1,)))
    value = value + mm(out[0, :, D:], hidden_part(w, 1), ((1,), (1,)))
    part[0] = value
    low[0] = value.astype(BF)


def grad_pre_of(own, other, slope, w, after=()):
    count = slope.shape[0]
    half = count // 2
    return call(
        functools.partial(grad_pre_kernel, count),
        "grad_pre",
        [
            (own, window((ROWS, D), lambda w: half + jnp.minimum(w, half - 1))),
            (other, window((ROWS, D), lambda w: half + jnp.maximum(w - half, 0))),
            (slope, window((ROWS, WIDE))),
            (w, None),
        ],
        [
            (array((count, ROWS, WIDE)), window((ROWS, WIDE))),
            (array((count, ROWS, D), F32), window((ROWS, D))),
            (array((count, ROWS, D)), window((ROWS, D), lambda w: (w + count // 2) % count)),
            (array((8, WIDE), F32), None),
        ],
        grid=(count,),
        after=after,
        vmem=18,
    )


def deal(where, total, keep, send, cols):
    for n, out in enumerate((keep, keep, send, send)):
        q = where[(1, 3, 2, 4)[n]]
        for h in range(2):
            rows = pl.ds(pl.multiple_of(h * HALF + q * 96, 8), 96)
            out[n % 2, h, :, cols] = total[rows, :].astype(BF)


def weight_grad_kernel(count, where, *refs):
    lefts, (right, keep, send, flip, total) = refs[:count], refs[count:]
    rows = right.shape[0] // count
    for n, left in enumerate(lefts):
        flip[:, n * rows : (n + 1) * rows] = left[left.shape[0] - rows :, :].T
    for at in range(0, WIDE, TAB):
        cols = slice(at, at + TAB)
        total[...] = mm(flip[...], right[:, cols])
        deal(where, total, keep, send, cols)


def weight_grad(where, lefts, right, after=()):
    rows = right.shape[0] * right.shape[1]
    shape = (2, 2, 96, WIDE)
    return call(
        functools.partial(weight_grad_kernel, len(lefts)),
        "weight_grad",
        [(where, SMEM)]
        + [(left.reshape(-1, D), None) for left in lefts]
        + [(right.reshape(rows, WIDE), None)],
        [(array(shape), None), (array(shape), None)],
        scratch=[pltpu.VMEM((D, rows), BF), pltpu.VMEM((D, TAB), F32)],
        after=after,
        vmem=16,
    )


def weight_grad_qp_kernel(
    where, normed, packed, att, branch, keep, send, flip, total, flip_att, total_att
):
    flip[...] = normed[...].T
    for at in range(0, QKV, HALF):
        cols = slice(at, at + HALF)
        total[...] = mm(flip[...], packed[:, cols])
        deal(where, total, keep, send, cols)
    flip_att[...] = att[...].T
    total_att[...] = mm(flip_att[...], branch[...])
    for n, out in enumerate((keep, keep, send, send)):
        q = where[(1, 3, 2, 4)[n]]
        rows = pl.ds(pl.multiple_of(q * 96, 8), 96)
        for h in range(2):
            out[n % 2, h, :, QKV:] = total_att[rows, h * HALF : (h + 1) * HALF].astype(BF)


def weight_grad_qp(where, normed, packed, att, branch, after=()):
    rows = normed.shape[0] * normed.shape[1]
    shape = (2, 2, 96, WIDE)
    return call(
        weight_grad_qp_kernel,
        "weight_grad_qp",
        [(where, SMEM)]
        + [(v.reshape(rows, v.shape[-1]), None) for v in (normed, packed, att, branch)],
        [(array(shape), None), (array(shape), None)],
        scratch=[
            pltpu.VMEM((D, rows), BF),
            pltpu.VMEM((D, HALF), F32),
            pltpu.VMEM((HALF, rows), BF),
            pltpu.VMEM((HALF, D), F32),
        ],
        after=after,
        vmem=16,
    )


def add_one_kernel(keep, got, stay, send):
    for h in range(2):
        for q in range(4):
            rows = slice(q * 24, (q + 1) * 24)
            stay[h, q] = keep[0, h, rows].astype(F32) + got[0, h, rows].astype(F32)
            send[h, q] = (keep[1, h, rows].astype(F32) + got[1, h, rows].astype(F32)).astype(BF)


def add_one(keep, got, after=()):
    shape = (2, 4, 24, WIDE)
    return call(
        add_one_kernel,
        "add_one",
        [(keep, None), (got, None)],
        [(array(shape, F32), None), (array(shape), None)],
        after=after,
    )


def add_two_kernel(where, *refs):
    z = where[0]
    keep, send = refs[-2:]
    for i in range(len(refs) // 2 - 1):
        stay, got = refs[2 * i], refs[2 * i + 1]
        for n in range(2):
            mine, theirs = z ^ (2 * n), z ^ (2 * n + 1)
            for h in range(2):
                keep[n, i, h] = stay[h, mine] + got[h, mine].astype(F32)
                send[n, i, h] = (stay[h, theirs] + got[h, theirs].astype(F32)).astype(BF)


def add_two(where, parts, after=()):
    shape = (2, len(parts), 2, 24, WIDE)
    return call(
        add_two_kernel,
        "add_two",
        [(where, SMEM)] + [(v, None) for part in parts for v in part],
        [(array(shape, F32), None), (array(shape), None)],
        after=after,
        vmem=12,
    )


def add_three_kernel(keep, got, stay, send):
    for i in range(stay.shape[0]):
        for h in range(2):
            stay[i, h] = keep[0, i, h] + got[0, i, h].astype(F32)
            send[i, h] = (keep[1, i, h] + got[1, i, h].astype(F32)).astype(BF)


def add_three(keep, got, after=()):
    shape = keep.shape[1:]
    return call(
        add_three_kernel,
        "add_three",
        [(keep, None), (got, None)],
        [(array(shape, F32), None), (array(shape), None)],
        after=after,
    )


def add_four_kernel(where, stay, got, total, send):
    for i in range(stay.shape[0]):
        for h in range(2):
            total[i, h] = stay[i, h] + got[i, h].astype(F32)
        send[i] = total[i, 1 - where[5]]


def add_four(where, stay, got, after=()):
    shape = (stay.shape[0],) + stay.shape[2:]
    return call(
        add_four_kernel,
        "add_four",
        [(where, SMEM), (stay, None), (got, None)],
        [(array(stay.shape, F32), None), (array(shape, F32), None)],
        after=after,
    )


def finish_kernel(where, two, two_there, total, there, output, hidden, qkv, proj):
    c = where[5]

    def lay(out, blocks, mine, theirs):
        for i in range(blocks):
            cols = slice(i * HALF, (i + 1) * HALF)
            out[:, pl.ds(pl.multiple_of(i * D + c * HALF, LANES), HALF)] = mine[:, cols]
            out[:, pl.ds(pl.multiple_of(i * D + (1 - c) * HALF, LANES), HALF)] = theirs[:, cols]

    lay(output, 4, two.at[0, c], two_there.at[0])
    lay(hidden, 4, two.at[1, c], two_there.at[1])
    lay(qkv, 3, total.at[0, c], there.at[0])
    for h in range(2):
        proj[:, h * HALF : (h + 1) * HALF] = total[0, h, :, QKV:]


def finish(where, two, two_there, total, there, after=()):
    return call(
        finish_kernel,
        "finish",
        [(where, SMEM)] + [(v, None) for v in (two, two_there, total, there)],
        [(array((24, blocks * D), F32), None) for blocks in (4, 4, 3, 1)],
        after=after,
    )


def small_kernel(where, two, one, hidden, qkv, qkv_b, tab, tab_b, to_offset, out):
    c = where[5]
    out[...] = jnp.zeros_like(out)
    cols = pl.ds(pl.multiple_of(c * HALF, LANES), HALF)
    for i in range(3):
        part = slice(i * HALF, (i + 1) * HALF)
        out[i : i + 1, cols] = qkv[0:1, part] + qkv_b[0:1, part]
    for i in range(4):
        out[3 + i : 4 + i, cols] = hidden[0:1, i * HALF : (i + 1) * HALF]
    for i in range(4):
        out[7 + i : 8 + i, :] = two[i : i + 1, :]
    for i in range(2):
        out[11 + i : 12 + i, :] = one[i : i + 1, :]
        half = slice(i * (TAB // 2), (i + 1) * (TAB // 2))
        rel = lax.dot_general(
            to_offset[...],
            tab[half, :] + tab_b[half, :],
            (((1,), (0,)), ((), ())),
            preferred_element_type=F32,
            precision=lax.Precision.HIGHEST,
        )
        for k in range(4):
            out[16 + 8 * i : 24 + 8 * i, k * LANES : (k + 1) * LANES] = rel[8 * k : 8 * k + 8]


def tally_kernel(one, two, out):
    out[...] = one[...] + two[...]


def tally(one, two, after=()):
    return call(
        tally_kernel,
        "tally",
        [(one, None), (two, None)],
        [(array(one.shape, F32), None)],
        after=after,
    )[0]


def unpack_kernel(total, *outs):
    qkv, height, width, proj, gain_two, bias_two, hidden, output, gain_one, bias_one = outs
    for i in range(3):
        qkv[i * D : (i + 1) * D] = total[i, :]
    for i in range(4):
        hidden[i * D : (i + 1) * D] = total[3 + i, :]
    rows = (gain_two, bias_two, proj, output, gain_one, bias_one)
    for i, out in enumerate(rows):
        out[...] = total[7 + i, :]
    for i, out in enumerate((height, width)):
        at = slice(16 + 8 * i, 24 + 8 * i)
        rel = jnp.concatenate([total[at, k * LANES : (k + 1) * LANES] for k in range(4)])
        out[...] = (rel + pltpu.roll(rel, HD, 1))[: 2 * WIN - 1, :HD]


def unpack(total):
    rel = (2 * WIN - 1, HD)
    shapes = [(2 * QKV,), rel, rel] + [(D,)] * 3 + [(FF,)] + [(D,)] * 3
    return call(
        unpack_kernel, "unpack", [(total, None)], [(array(shape, F32), None) for shape in shapes]
    )


def per_device(
    n_dp,
    image_tokens,
    slot_window,
    first_gain,
    first_bias,
    qkv_weight,
    qkv_bias,
    rel_height,
    rel_width,
    proj_weight,
    proj_bias,
    second_gain,
    second_bias,
    hidden_weight,
    hidden_bias,
    output_weight,
    output_bias,
    cotangent,
):
    images = image_tokens.shape[0]
    count = 2 * images
    c = lax.axis_index("dp") % 2
    s = lax.axis_index("seq")
    z = lax.axis_index("fsdp")
    a = jnp.where(c == 0, s ^ 1, s ^ 2)
    b = jnp.where(c == 0, s ^ 2, s ^ 1)
    where = jnp.stack([z, s, a, b, s ^ 3, c]).astype(jnp.int32)

    def plane_perm(step):
        out = []
        for i in range(n_dp):
            hop = (1, 2)[(i + step) % 2]
            out += [(i * 4 + j, i * 4 + (j ^ hop)) for j in range(4)]
        return out

    plane_one, plane_two = plane_perm(0), plane_perm(1)

    def to_core(v):
        return lax.ppermute(v, "dp", [(i, i ^ 1) for i in range(n_dp)])

    def to_seq(v, k):
        return lax.ppermute(v, "seq", [(i, i ^ k) for i in range(4)])

    def to_z(v, k):
        return lax.ppermute(v, "fsdp", [(i, (i + k) % 4) for i in range(4)])

    def swap_z(v, hop):
        return lax.ppermute(v, "fsdp", [(i, i ^ hop) for i in range(4)])

    def to_plane(v, perm):
        return lax.ppermute(v, ("dp", "seq"), perm)

    def pick(v, index, axis=0):
        return lax.dynamic_index_in_dim(v, index, axis, keepdims=False)

    row = jnp.arange(ROWS)
    token = (s ^ (row // PAD)) * TOK + row % PAD
    real = row % PAD < TOK
    t_r, t_c = token // WIN, token % WIN
    slot = pick(slot_window, s)
    ok = (
        real
        & (slot >= 0)
        & (slot // NWS * WIN + t_r < GRID)
        & (slot % NWS * WIN + t_c < GRID)
    ).astype(F32)[:, None]
    ones = jnp.ones((ROWS, 1), F32)
    near_offset = jnp.arange(WIN)[:, None] - jnp.arange(WIN)[None, :] + WIN - 1
    height = rel_height[near_offset].reshape(WIN * WIN, HD).T
    width = rel_width[near_offset].reshape(WIN * WIN, HD).T
    gap = jnp.zeros((HD, TAB // 2 - WIN * WIN), BF)
    flat = jnp.concatenate([height, gap, width, gap], axis=1)
    blank = jnp.zeros_like(flat)
    table = jnp.stack([jnp.concatenate([flat, blank]), jnp.concatenate([blank, flat])])
    col = jnp.arange(TAB)
    in_half = col % (TAB // 2)
    col_from = jnp.where(in_half < WIN * WIN, in_half // WIN, -1)
    spot = (
        jnp.where(col[None, :] < TAB // 2, t_r[:, None], t_c[:, None]) == col_from[None, :]
    ).astype(F32)
    col_to = jnp.where(in_half < WIN * WIN, in_half % WIN + WIN * (col // (TAB // 2)), -1)
    fold = (col_to[:, None] == jnp.arange(LANES)[None, :]).astype(BF)
    lanes = jnp.arange(LANES)[None, :]
    keys = (
        real[:, None] & ((lanes == t_r[:, None]) | (lanes == WIN + t_c[:, None]))
    ).astype(BF)
    key_bias = jnp.where(real, 0.0, NEG).astype(F32)[None, :]
    tables = (table, spot, fold, keys, key_bias)
    gain_one, bias_one = first_gain[None], first_bias[None]
    gain_two, bias_two = second_gain[None], second_bias[None]

    def mine_of(v, parts):
        v = v.reshape(parts, 2, HALF)
        return jnp.where(c == 0, v[:, 0], v[:, 1]).reshape(1, -1)

    b_qkv, b_hidden = mine_of(qkv_bias, 3), mine_of(hidden_bias, 4)

    def along_z(piece):
        return [to_z(piece, k) for k in (1, 2, 3)]

    def in_plane(first):
        second = to_plane(first, plane_one)
        third = to_plane(first, plane_two)
        fourth = to_plane(second, plane_two)
        return first, second, third, fourth

    def exchange(parts, after=()):
        near, both, far = parts
        one = to_plane(both, plane_one)
        send = pair_up(far, one, after)
        return near, one, to_plane(send, plane_two), send

    ho_piece, qp_piece = pieces(where, qkv_weight, proj_weight, hidden_weight, output_weight)
    z_qp = along_z(qp_piece)
    tokens_cut = cut(where, image_tokens, cotangent, after=[qp_piece])
    z_ho = along_z(ho_piece)
    first_qp = join(z_qp, after=[tokens_cut[0]])
    got_qp = in_plane(first_qp)
    near, one, two, _ = exchange(tokens_cut, after=[got_qp[1]])
    own = weld(where, ok, near, one, two, after=got_qp[1:])
    other = to_core(own)
    w_qp, proj_send = call(
        place_qp_kernel,
        "place_qp",
        [(where, SMEM), (qkv_weight, HBM), (proj_weight, HBM)] + [(v, ANY) for v in got_qp],
        [
            (array((4, 4, PIECE, WIDE)), None),
            (array((2, 4, PIECE, HALF)), None),
        ],
        scratch=[pltpu.SemaphoreType.DMA((28,))],
        after=[own],
    )
    w_qp = w_qp.reshape(D, WIDE)
    proj_other = to_core(proj_send.reshape(HALF, HALF))
    normed = norm_one(ok, own, other, gain_one, bias_one, after=[w_qp])
    got_ho = in_plane(join(z_ho, after=[normed]))
    packed, attended, probs, low, branch_other = attn_fwd(
        where, 1, normed, w_qp, proj_other, b_qkv, tables, after=[got_ho[0]]
    )
    packed, attended, probs, low, branch = attn_fwd(
        where, 0, normed, w_qp, proj_other, b_qkv, tables,
        before=(packed, attended, probs, low), after=[got_ho[1]],
    )
    there = to_core(low)
    w_ho = call(
        place_ho_kernel,
        "place_ho",
        [(where, SMEM), (hidden_weight, HBM), (output_weight, HBM)] + [(v, ANY) for v in got_ho],
        [(array((4, 4, 4 * PIECE, D)), None)],
        scratch=[pltpu.SemaphoreType.DMA((32,))],
        after=[packed],
    )[0].reshape(16, 4 * PIECE, D)
    middle, second = norm_two(
        own, other, branch, branch_other, there, proj_bias[None], gain_two, bias_two, after=[w_ho]
    )
    active, slope = hidden_layer(second, w_ho, b_hidden)

    def natural(keep_two, send_two):
        out = jnp.zeros((2, 4, 96, WIDE), BF)
        for q, part in ((s, keep_two[0]), (b, keep_two[1]), (a, send_two[0]), (s ^ 3, send_two[1])):
            out = lax.dynamic_update_index_in_dim(out, part, q, 1)
        return out.astype(F32)

    def sum_rows(full):
        return lax.psum_scatter(full, ("dp", "seq", "fsdp"), scatter_dimension=0, tiled=True)

    def spread_cols(grad, parts):
        grad = grad.reshape(D, parts, HALF)
        zero = jnp.zeros_like(grad)
        return jnp.where(
            c == 0, jnp.stack([grad, zero], axis=2), jnp.stack([zero, grad], axis=2)
        ).reshape(D, 2 * parts * HALF)

    def larger_wide(keep_two, send_two):
        return sum_rows(spread_cols(natural(keep_two, send_two).reshape(D, WIDE), 4))

    def larger_qp(keep_two, send_two):
        grad = natural(keep_two, send_two)
        qkv = sum_rows(spread_cols(grad[..., :QKV].reshape(D, QKV), 3))
        proj = jnp.concatenate(list(grad[..., QKV:].reshape(2, HALF, HALF)), axis=1)
        zero = jnp.zeros_like(proj)
        proj = jnp.where(c == 0, jnp.concatenate([proj, zero]), jnp.concatenate([zero, proj]))
        return qkv, sum_rows(proj)

    def step_one(send):
        return to_plane(send, plane_one)

    def step_two(keep, got, after=()):
        stay, send = add_one(keep, got, after)
        return stay, to_plane(send, plane_two), send

    def step_three(parts, after=()):
        keep, send = add_two(where, parts, after)
        return keep, swap_z(send, 1), send

    def step_four(keep, got, after=()):
        stay, send = add_three(keep, got, after)
        return stay, swap_z(send, 2), send

    def step_five(stay, got, after=()):
        total, send = add_four(where, stay, got, after)
        return total, to_core(send), send

    pair = n_dp == 2

    o_keep, o_send = weight_grad(where, [own, other], active)
    o_got = step_one(o_send) if pair else o_send
    grad_pre, part, part_low, hidden_sums = grad_pre_of(own, other, slope, w_ho, after=[o_send])
    part_there = to_core(part_low)
    h_keep, h_send = weight_grad(where, [second], grad_pre)
    h_got = step_one(h_send) if pair else h_send
    held = [h_send]
    if pair:
        o_stay, o_got, mid = step_two(o_keep, o_got, after=held)
        held = [mid]
    grad_middle, grad_branch, sums_two = norm_two_back(
        part, part_there, middle, gain_two, own, other, after=held
    )
    grad_packed, tab_grad, qkv_sums = attn_bwd(
        where, 0, packed, grad_branch, probs, w_qp, proj_other, tables
    )
    held = [grad_packed]
    if pair:
        h_stay, h_got, mid = step_two(h_keep, h_got, after=held)
        held = [mid, o_got]
    grad_packed, tab_grad_b, qkv_sums_b = attn_bwd(
        where, 1, packed, grad_branch, probs, w_qp, proj_other, tables,
        before=(grad_packed,), after=held,
    )
    q_keep, q_send = weight_grad_qp(where, normed, grad_packed, attended, grad_branch)
    held = [q_send]
    if pair:
        q_got = step_one(q_send)
        oh_keep, oh_got, mid = step_three([(o_stay, o_got), (h_stay, h_got)], after=held)
        held = [mid]
    back, back_low = product(
        "back", grad_packed, w_qp, pl.BlockSpec((D, QKV), lambda w: (0, 0)),
        lambda left, right: mm(left, right[...], ((1,), (1,))), after=held,
    )
    back_there = to_core(back_low)
    feed, feed_low = product(
        "feed", active, w_ho, None, lambda left, right: mm(left, output_part(right)),
        after=[back_low],
    )
    feed_there = to_core(feed_low)
    held = [feed_low]
    if pair:
        q_stay, q_got, mid = step_two(q_keep, q_got, after=held)
        oh_stay, oh_got, mid = step_four(oh_keep, oh_got, after=[mid])
        held = [mid]
    *parts, sums_one = last(
        where, ok, back, back_there, own, gain_one, grad_middle, middle, feed, feed_there,
        output_bias[None], after=held,
    )
    to_offset = jnp.pad(
        (near_offset.reshape(-1)[None, :] == jnp.arange(2 * WIN - 1)[:, None]).astype(F32),
        ((0, 32 - (2 * WIN - 1)), (0, TAB // 2 - WIN * WIN)),
    )
    ins = (sums_two, sums_one, hidden_sums, qkv_sums, qkv_sums_b, tab_grad, tab_grad_b, to_offset)
    small = call(
        small_kernel,
        "small",
        [(where, SMEM)] + [(v, None) for v in ins],
        [(array((32, D), F32), None)],
    )[0]
    small_got = to_core(small)
    held = [small]
    if pair:
        q_keep, q_got, mid = step_three([(q_stay, q_got)], after=held)
        held = [mid]
    *parts, mid = exchange(parts, after=held)
    small = tally(small, small_got, after=[mid])
    small_got = to_seq(small, 1)
    held = [small]
    if pair:
        q_stay, q_got, mid = step_four(q_keep, q_got, after=held)
        oh_total, oh_there, mid = step_five(oh_stay, oh_got, after=[mid])
        held = [mid]
    small = tally(small, small_got, after=held)
    small_got = to_seq(small, 2)
    input_grad, block_out = home(where, *parts, after=[small])
    held = [input_grad]
    if pair:
        q_total, q_there, mid = step_five(q_stay, q_got, after=held)
        held = [mid]
    small = tally(small, small_got, after=held)
    small_got = swap_z(small, 1)
    if pair:
        g_output, g_hidden, g_qkv, g_proj = finish(
            where, oh_total, oh_there, q_total, q_there, after=[small]
        )
        g_output = g_output.T
    else:
        g_output = larger_wide(o_keep, o_send).T
        g_hidden = larger_wide(h_keep, h_send)
        g_qkv, g_proj = larger_qp(q_keep, q_send)
    small = tally(small, small_got, after=[g_qkv])
    small_got = swap_z(small, 2)
    small = tally(small, small_got)
    if n_dp > 2:
        groups = [list(range(core, n_dp, 2)) for core in range(2)]
        small = lax.psum(small, "dp", axis_index_groups=groups)
    (
        d_qkv_bias, d_height, d_width, d_proj_bias, d_gain_two, d_bias_two, d_hidden_bias,
        d_output_bias, d_gain_one, d_bias_one,
    ) = unpack(small)
    return (
        block_out,
        input_grad,
        d_gain_one,
        d_bias_one,
        g_qkv,
        d_qkv_bias,
        d_height,
        d_width,
        g_proj,
        d_proj_bias,
        d_gain_two,
        d_bias_two,
        g_hidden,
        d_hidden_bias,
        g_output,
        d_output_bias,
    )


def solution(mesh):
    tokens = P("dp", "fsdp", "seq", None)
    rows = P("fsdp", None)
    every = P(("dp", "seq", "fsdp"), None)
    args = (tokens, P("fsdp"), P(), P(), rows, P(), P(), P(), rows)
    args += (P(), P(), P(), rows, P(), rows, P(), tokens)
    outs = (tokens, tokens, P(), P(), every, P(), P(), P(), every)
    outs += (P(), P(), P(), every, P(), P(None, ("dp", "seq", "fsdp")), P())
    return jax.shard_map(
        functools.partial(per_device, mesh.shape["dp"]),
        mesh=mesh,
        in_specs=args,
        out_specs=outs,
        check_vma=False,
    )
```

time: 380 us -> 251 us (0.66)
  Pallas kernels: 45.3 us -> 122 us
  other arithmetic: 69 us -> 0.95 us
  local copies, waits for them, and re-layouts: 70.6 us -> 11.3 us
  matrix products: 37.7 us -> 0 us
  starting transfers between devices: 82.9 us -> 48.5 us
    pallas_call x5 -> x42, Pallas kernels: 45.3 us -> 122 us  [call(): pl.pallas_call(body, grid=grid, in_specs=[spec or held(v) for v, spec in...]
    dot_general x13 -> x0, matrix products: 37.7 us -> none  [the longest x12 37.5 us: mm(): lax.dot_general(left, right, (dims, ((), ())), preferred_element_type=F32)]
    ppermute x14 -> x16, waiting for transfers between devices: 10.2 us -> 43.5 us  [to_plane(): return lax.ppermute(v, ('dp', 'seq'), perm)]
    ppermute x14 -> x2, waiting for transfers between devices: 22.9 us -> 0.01 us  [to_seq(): return lax.ppermute(v, 'seq', [(i, i ^ k) for i in range(4)])]
    ppermute x21 -> x6, waiting for transfers between devices: 28.2 us -> 7.73 us  [to_z(): return lax.ppermute(v, 'fsdp', [(i, (i + k) % 4) for i in range(4)])]
    reduce_sum x10 -> x0, other arithmetic: 19.9 us -> none  [the longest x2 6.97 us: centre_of(): v = v - jnp.mean(v, axis=-1, keepdims=True)]
    ppermute x21 -> x6, starting transfers between devices: 29.6 us -> 11.4 us  [to_z(): return lax.ppermute(v, 'fsdp', [(i, (i + k) % 4) for i in range(4)])]
    ppermute x14 -> x2, starting transfers between devices: 17.2 us -> 2.57 us  [to_seq(): return lax.ppermute(v, 'seq', [(i, i ^ k) for i in range(4)])]
  transfers between devices with their start and end apart: 68 -> 39, of which waited for: 21 -> 13; matrix products, arithmetic and copies ran while one was open for 40% -> 3% of each run, Pallas kernels for 12% -> 44%
where the time goes in v2:
time: 251 us; the launch traced here: 247 us
  Pallas kernels  122 us (49%)
  waiting for transfers between devices  59.5 us (24%)
  starting transfers between devices  48.5 us (19%)
  local copies, waits for them, and re-layouts  11.3 us (5%)
  between operations  5.22 us (2%)
    pallas_call x42, Pallas kernels, call(): pl.pallas_call(body, grid=grid, in_specs=[spec or held(v) for v, spec in...  122 us
    ppermute x16, waiting for transfers between devices, to_plane(): return lax.ppermute(v, ('dp', 'seq'), perm)  43.5 us
    ppermute x16, starting transfers between devices, to_plane(): return lax.ppermute(v, ('dp', 'seq'), perm)  17.7 us
    ppermute x6, starting transfers between devices, swap_z(): return lax.ppermute(v, 'fsdp', [(i, i ^ hop) for i in range(4)])  14.8 us
    ppermute x6, starting transfers between devices, to_z(): return lax.ppermute(v, 'fsdp', [(i, (i + k) % 4) for i in range(4)])  11.4 us
    ppermute x6, waiting for transfers between devices, swap_z(): return lax.ppermute(v, 'fsdp', [(i, i ^ hop) for i in range(4)])  8.28 us
    ppermute x6, waiting for transfers between devices, to_z(): return lax.ppermute(v, 'fsdp', [(i, (i + k) % 4) for i in range(4)])  7.73 us
    unnamed x106, local copies, waits for them, and re-layouts  6.04 us
  transfers between devices with their start and end apart: 39, of which 13 were waited for; matrix products, arithmetic and copies ran while one was open for 3% of the time, Pallas kernels for 44%

profile of v2, /device:TPU:0, one launch (start us, length us, event | category | flops | bytes accessed | tf_op | source)
XLA Modules:
  0.0 247.2 jit_solution(951954308129371306)
XLA Ops:
  1.3 2.6 %pieces.1 = (bf16[192,768]{1,0:T(8,128)(2,1)}, bf16[48,1536]{1,0:T(8,128)(2,1)}) custom-call(s32[6]{0:T(128)} %stack.36.refs_0_, bf16[192,2304]{1,0:T(8,128)(2,1)} %refs_1_.4, bf16[192,768]{1,0:T(8,128)(2,1)} %refs_2_.4, bf16[192,3072]{1,0:T(8,128)(2,1)} %refs_1_.5, bf16[768,768]{1,0:T(8,128)(2,1)} %refs_2_.5), custom_call_target="tpu_custom_call" | custom-call | flops 100050001920 | bytes 100050000 | tf_op jit(solution)/shard_map/pieces/pallas_call | solution.py:68
  3.9 3.1 %collective-permute-start.1 = (bf16[48,1536]{1,0:T(8,128)(2,1)}, bf16[48,1536]{1,0:T(8,128)(2,1)S(1)}, u32[]{:S(2)}, u32[]{:S(2)}) collective-permute-start(bf16[48,1536]{1,0:T(8,128)(2,1)} %get-tuple-element.98.refs_3_), channel_id=1, source_target_pairs={{0,1},{1,2},{2,3},{3,0},{4,5},{5,6},{6,7},{7,4},{8,9},{9,10},{10,1... | collective-permute-start | bytes 442376 | tf_op jit(solution)/shard_map/ppermute | solution.py:955
  7.0 2.6 %collective-permute-start.2 = (bf16[48,1536]{1,0:T(8,128)(2,1)}, bf16[48,1536]{1,0:T(8,128)(2,1)S(1)}, u32[]{:S(2)}, u32[]{:S(2)}) collective-permute-start(bf16[48,1536]{1,0:T(8,128)(2,1)} %get-tuple-element.98.refs_3_), channel_id=1, source_target_pairs={{0,2},{1,3},{2,0},{3,1},{4,6},{5,7},{6,4},{7,5},{8,10},{9,11},{10,... | collective-permute-start | bytes 442376 | tf_op jit(solution)/shard_map/ppermute | solution.py:955
  13.6 1.6 collective-permute-start
  22.9 7.6 %collective-permute-done.4.refs_2_.refs_5_.refs_4_ = bf16[3,48,1536]{2,1,0:T(8,128)(2,1)S(1)} collective-permute-done((bf16[3,48,1536]{2,1,0:T(8,128)(2,1)S(1)}, bf16[3,48,1536]{2,1,0:T(8,128)(2,1)S(1)}, u32[]{:S(2)}, u32[]{:S(2)}) %collective-permute-start.4) | collective-permute-done | bytes 442400 | tf_op jit(solution)/shard_map/ppermute | solution.py:961
  30.6 1.6 collective-permute-start.5
  32.9 1.5 collective-permute-start.7
  34.8 11.6 %collective-permute-done.6.refs_6_.refs_5_ = bf16[3,48,1536]{2,1,0:T(8,128)(2,1)S(1)} collective-permute-done((bf16[3,48,1536]{2,1,0:T(8,128)(2,1)S(1)}, bf16[3,48,1536]{2,1,0:T(8,128)(2,1)S(1)}, u32[]{:S(2)}, u32[]{:S(2)}) %collective-permute-start.6) | collective-permute-done | bytes 442400 | tf_op jit(solution)/shard_map/ppermute | solution.py:961
  46.4 3.4 %collective-permute-start.12 = (bf16[192,768]{1,0:T(8,128)(2,1)S(1)}, bf16[192,768]{1,0:T(8,128)(2,1)S(1)}, u32[]{:S(2)}, u32[]{:S(2)}) collective-permute-start(bf16[192,768]{1,0:T(8,128)(2,1)S(1)} %copy-done.50), channel_id=1, source_target_pairs={{0,3},{1,0},{2,1},{3,2},{4,7},{5,4},{6,5},{7,6},{8,11},{9,8},{10,9... | collective-permute-start | bytes 884744 | tf_op jit(solution)/shard_map/ppermute | solution.py:955
  52.5 3.3 %place_qp.1 = (bf16[4,4,48,1536]{3,2,1,0:T(8,128)(2,1)S(1)}, bf16[2,4,48,384]{3,2,1,0:T(8,128)(2,1)S(1)}) custom-call(s32[6]{0:T(128)S(1)} %copy-done.25, bf16[192,2304]{1,0:T(8,128)(2,1)S(1)} %copy-done.14, bf16[192,768]{1,0:T(8,128)(2,1)S(1)} %copy-done.17, bf16[3,48,1536]{2,1,0:T(8,128)(2,1)S(1)} %join.2.refs_3_, ...), custom_call_target="tpu_custom_call" | custom-call | flops 345000000 | bytes 345000 | tf_op jit(solution)/shard_map/place_qp/pallas_call | solution.py:68
  57.9 7.7 %collective-permute-done.12.refs_2_ = bf16[192,768]{1,0:T(8,128)(2,1)S(1)} collective-permute-done((bf16[192,768]{1,0:T(8,128)(2,1)S(1)}, bf16[192,768]{1,0:T(8,128)(2,1)S(1)}, u32[]{:S(2)}, u32[]{:S(2)}) %collective-permute-start.12) | collective-permute-done | bytes 294944 | tf_op jit(solution)/shard_map/ppermute | solution.py:955
  66.6 1.5 collective-permute-start.13
  68.1 1.5 collective-permute-start.15
  69.6 10.0 %attn_fwd.2 = (bf16[4,224,1152]{2,1,0:T(8,128)(2,1)S(1)}, bf16[4,224,384]{2,1,0:T(8,128)(2,1)S(1)}, bf16[4,6,224,224]{3,2,1,0:T(8,128)(2,1)S(1)}, bf16[4,224,768]{2,1,0:T(8,128)(2,1)S(1)}, f32[2,224,768]{2,1,0:T(8,128)S(1)}) custom-call(s32[6]{0:T(128)S(1)} %copy-done.25, bf16[4,224,768]{2,1,0:T(8,128)(2,1)S(1)} %norm_one.1.refs_3_.refs_1_, ...), custom_call_target="tpu_custom_call" | custom-call | flops 100050001920 | bytes 100050000 | tf_op jit(solution)/shard_map/attn_fwd/pallas_call | solution.py:68
  79.5 9.8 %collective-permute-done.13.refs_14_.refs_4_ = bf16[3,192,768]{2,1,0:T(8,128)(2,1)S(1)} collective-permute-done((bf16[3,192,768]{2,1,0:T(8,128)(2,1)}, bf16[3,192,768]{2,1,0:T(8,128)(2,1)S(1)}, u32[]{:S(2)}, u32[]{:S(2)}) %collective-permute-start.13) | collective-permute-done | bytes 884768 | tf_op jit(solution)/shard_map/ppermute | solution.py:961
  89.4 10.0 %attn_fwd.3 = (bf16[4,224,1152]{2,1,0:T(8,128)(2,1)S(1)}, bf16[4,224,384]{2,1,0:T(8,128)(2,1)S(1)}, bf16[4,6,224,224]{3,2,1,0:T(8,128)(2,1)S(1)}, bf16[4,224,768]{2,1,0:T(8,128)(2,1)S(1)}, f32[2,224,768]{2,1,0:T(8,128)S(1)}) custom-call(s32[6]{0:T(128)S(1)} %copy-done.25, ...), custom_call_target="tpu_custom_call", output_to_operand_aliasing={{0}: (10, {}), {1}: (11, {}), {2}: (12, {}), {3}: (13, {})} | custom-call | flops 100050001920 | bytes 100050000 | tf_op jit(solution)/shard_map/attn_fwd/pallas_call | solution.py:68
  100.3 1.5 copy-done.35
  102.4 3.2 %place_ho.1 = bf16[4,4,192,768]{3,2,1,0:T(8,128)(2,1)S(1)} custom-call(s32[6]{0:T(128)S(1)} %copy-done.25, bf16[192,3072]{1,0:T(8,128)(2,1)S(1)} %copy-done.26, bf16[768,768]{1,0:T(8,128)(2,1)S(1)} %copy-done.27, bf16[3,192,768]{2,1,0:T(8,128)(2,1)} %join.3.refs_10_.refs_3_, bf16[3,192,768]{2,1,0:T(8,128)(2,1)S(1)} %collective-permute-done.13.refs_14_.refs_4_, ...), custom_call_target="tpu_custom_call" | custom-call | flops 100050001920 | bytes 100050000 | tf_op jit(solution)/shard_map/place_ho/pallas_call | solution.py:68
  107.0 4.4 %hidden.1 = (bf16[4,224,1536]{2,1,0:T(8,128)(2,1)S(1)}, bf16[4,224,1536]{2,1,0:T(8,128)(2,1)S(1)}) custom-call(bf16[4,224,768]{2,1,0:T(8,128)(2,1)S(1)} %get-tuple-element.113.refs_0_, bf16[16,192,768]{2,1,0:T(8,128)(2,1)S(1)} %bitcast.57, f32[1,1536]{1,0:T(1,128)S(1)} %bitcast.52), custom_call_target="tpu_custom_call" | custom-call | flops 100050001920 | bytes 100050000 | tf_op jit(solution)/shard_map/hidden/pallas_call | solution.py:68
  111.4 4.5 %weight_grad.2 = (bf16[2,2,96,1536]{3,2,1,0:T(8,128)(2,1)S(1)}, bf16[2,2,96,1536]{3,2,1,0:T(8,128)(2,1)}) custom-call(s32[6]{0:T(128)S(1)} %copy-done.25, bf16[896,768]{1,0:T(8,128)(2,1)S(1)} %bitcast.41, bf16[896,768]{1,0:T(8,128)(2,1)S(1)} %bitcast.51, bf16[896,1536]{1,0:T(8,128)(2,1)S(1)} %bitcast.60), custom_call_target="tpu_custom_call" | custom-call | flops 100050001920 | bytes 100050000 | tf_op jit(solution)/shard_map/weight_grad/pallas_call | solution.py:68
  117.4 8.3 %grad_pre.1 = (bf16[4,224,1536]{2,1,0:T(8,128)(2,1)S(1)}, f32[4,224,768]{2,1,0:T(8,128)S(1)}, bf16[4,224,768]{2,1,0:T(8,128)(2,1)}, f32[8,1536]{1,0:T(8,128)S(1)}) custom-call(bf16[4,224,768]{2,1,0:T(8,128)(2,1)S(1)} %copy-done.3, bf16[4,224,768]{2,1,0:T(8,128)(2,1)S(1)} %copy-done.11, bf16[4,224,1536]{2,1,0:T(8,128)(2,1)S(1)} %get-tuple-element.114.refs_2_, ...), custom_call_target="tpu_custom_call" | custom-call | flops 100050001920 | bytes 100050000 | tf_op jit(solution)/shard_map/grad_pre/pallas_call | solution.py:68
  125.9 4.3 %weight_grad.3 = (bf16[2,2,96,1536]{3,2,1,0:T(8,128)(2,1)S(1)}, bf16[2,2,96,1536]{3,2,1,0:T(8,128)(2,1)}) custom-call(s32[6]{0:T(128)S(1)} %copy-done.25, bf16[896,768]{1,0:T(8,128)(2,1)S(1)} %bitcast.64, bf16[896,1536]{1,0:T(8,128)(2,1)S(1)} %bitcast.61), custom_call_target="tpu_custom_call" | custom-call | flops 100050001920 | bytes 100050000 | tf_op jit(solution)/shard_map/weight_grad/pallas_call | solution.py:68
  132.4 2.3 add_one.3
  134.7 1.6 collective-permute-start.20
  136.4 3.7 %norm_two_back.1 = (f32[2,224,768]{2,1,0:T(8,128)S(1)}, bf16[4,224,768]{2,1,0:T(8,128)(2,1)S(1)}, f32[8,768]{1,0:T(8,128)S(1)}) custom-call(f32[4,224,768]{2,1,0:T(8,128)S(1)} %get-tuple-element.117.refs_0_, bf16[4,224,768]{2,1,0:T(8,128)(2,1)} %collective-permute-done.17.refs_1_, f32[4,224,768]{2,1,0:T(8,128)S(1)} %get-tuple-element.119.refs_2_.refs_7_, ...), custom_call_target="tpu_custom_call" | custom-call | flops 100050001920 | bytes 100050000 | tf_op jit(solution)/shard_map/norm_two_back/pallas_call | solution.py:68
  140.2 9.3 %attn_bwd.2 = (bf16[4,224,1152]{2,1,0:T(8,128)(2,1)S(1)}, f32[512,128]{1,0:T(8,128)S(1)}, f32[8,1152]{1,0:T(8,128)S(1)}) custom-call(s32[6]{0:T(128)S(1)} %copy-done.25, bf16[4,224,1152]{2,1,0:T(8,128)(2,1)S(1)} %copy-done.38, bf16[4,224,768]{2,1,0:T(8,128)(2,1)S(1)} %get-tuple-element.124.refs_2_, bf16[4,6,224,224]{3,2,1,0:T(8,128)(2,1)S(1)} %copy-done.36, ...), custom_call_target="tpu_custom_call" | custom-call | flops 100050001920 | bytes 100050000 | tf_op jit(solution)/shard_map/attn_bwd/pallas_call | solution.py:68
  149.5 3.6 %collective-permute-done.19.refs_1_ = bf16[2,2,96,1536]{3,2,1,0:T(8,128)(2,1)} collective-permute-done((bf16[2,2,96,1536]{3,2,1,0:T(8,128)(2,1)}, bf16[2,2,96,1536]{3,2,1,0:T(8,128)(2,1)}, u32[]{:S(2)}, u32[]{:S(2)}) %collective-permute-start.19) | collective-permute-done | bytes 1179680 | tf_op jit(solution)/shard_map/ppermute | solution.py:961
  153.0 2.3 add_one.4
  156.7 9.7 %attn_bwd.3 = (bf16[4,224,1152]{2,1,0:T(8,128)(2,1)S(1)}, f32[512,128]{1,0:T(8,128)S(1)}, f32[8,1152]{1,0:T(8,128)S(1)}) custom-call(s32[6]{0:T(128)S(1)} %copy-done.25, bf16[4,224,1152]{2,1,0:T(8,128)(2,1)S(1)} %copy-done.38, bf16[4,224,768]{2,1,0:T(8,128)(2,1)S(1)} %get-tuple-element.124.refs_2_, ...), custom_call_target="tpu_custom_call", output_to_operand_aliasing={{0}: (10, {})} | custom-call | flops 100050001920 | bytes 100050000 | tf_op jit(solution)/shard_map/attn_bwd/pallas_call | solution.py:68
  166.4 4.8 %weight_grad_qp.1 = (bf16[2,2,96,1536]{3,2,1,0:T(8,128)(2,1)S(1)}, bf16[2,2,96,1536]{3,2,1,0:T(8,128)(2,1)}) custom-call(s32[6]{0:T(128)S(1)} %copy-done.25, bf16[896,768]{1,0:T(8,128)(2,1)S(1)} %bitcast.42, bf16[896,1152]{1,0:T(8,128)(2,1)S(1)} %bitcast.62, bf16[896,384]{1,0:T(8,128)(2,1)S(1)} %bitcast.65, bf16[896,768]{1,0:T(8,128)(2,1)S(1)} %bitcast.63), custom_call_target="tpu_custom_call" | custom-call | flops 100050001920 | bytes 100050000 | tf_op jit(solution)/shard_map/weight_grad_qp/pallas_call | solution.py:68
  171.7 2.3 add_two.2
  174.0 4.0 %back.1 = (f32[2,224,768]{2,1,0:T(8,128)S(1)}, bf16[2,224,768]{2,1,0:T(8,128)(2,1)}) custom-call(bf16[4,224,1152]{2,1,0:T(8,128)(2,1)S(1)} %get-tuple-element.129.refs_0_, bf16[768,1536]{1,0:T(8,128)(2,1)S(1)} %bitcast.50, bf16[2,2,2,24,1536]{4,3,2,1,0:T(8,128)(2,1)} %get-tuple-element.134.refs_2_), custom_call_target="tpu_custom_call" | custom-call | flops 100050001920 | bytes 100050000 | tf_op jit(solution)/shard_map/back/pallas_call | solution.py:68
  178.0 6.6 %collective-permute-start.24 = (bf16[2,2,2,24,1536]{4,3,2,1,0:T(8,128)(2,1)}, bf16[2,2,2,24,1536]{4,3,2,1,0:T(8,128)(2,1)}, u32[]{:S(2)}, u32[]{:S(2)}) collective-permute-start(bf16[2,2,2,24,1536]{4,3,2,1,0:T(8,128)(2,1)} %get-tuple-element.134.refs_2_), channel_id=1, source_target_pairs={{0,1},{1,0},{2,3},{3,2},{4,5},{5,4},{6,7},{7,6},{8,9},{9,8},{10,11... | collective-permute-start | bytes 1769480 | tf_op jit(solution)/shard_map/ppermute | solution.py:958
  184.7 4.0 %feed.1 = (f32[2,224,768]{2,1,0:T(8,128)S(1)}, bf16[2,224,768]{2,1,0:T(8,128)(2,1)}) custom-call(bf16[4,224,1536]{2,1,0:T(8,128)(2,1)S(1)} %get-tuple-element.115.refs_0_, bf16[16,192,768]{2,1,0:T(8,128)(2,1)S(1)} %bitcast.59, bf16[2,224,768]{2,1,0:T(8,128)(2,1)} %get-tuple-element.136.refs_2_), custom_call_target="tpu_custom_call" | custom-call | flops 100050001920 | bytes 100050000 | tf_op jit(solution)/shard_map/feed/pallas_call | solution.py:68
  189.2 2.3 add_one.5
  192.0 5.0 %collective-permute-done.24.refs_1_ = bf16[2,2,2,24,1536]{4,3,2,1,0:T(8,128)(2,1)} collective-permute-done((bf16[2,2,2,24,1536]{4,3,2,1,0:T(8,128)(2,1)}, bf16[2,2,2,24,1536]{4,3,2,1,0:T(8,128)(2,1)}, u32[]{:S(2)}, u32[]{:S(2)}) %collective-permute-start.24) | collective-permute-done | bytes 589856 | tf_op jit(solution)/shard_map/ppermute | solution.py:958
  197.1 1.9 add_three.2
  199.8 3.9 %last.1 = (bf16[4,56,768]{2,1,0:T(8,128)(2,1)S(1)}, bf16[2,4,56,768]{3,2,1,0:T(8,128)(2,1)}, bf16[4,56,768]{2,1,0:T(8,128)(2,1)S(1)}, f32[8,768]{1,0:T(8,128)S(1)}) custom-call(s32[6]{0:T(128)S(1)} %copy-done.25, f32[224,1]{1,0:T(8,128)S(1)} %copy-done.13, f32[2,224,768]{2,1,0:T(8,128)S(1)} %get-tuple-element.135.refs_2_, ...), custom_call_target="tpu_custom_call" | custom-call | flops 100050001920 | bytes 100050000 | tf_op jit(solution)/shard_map/last/pallas_call | solution.py:68
  207.7 7.3 %collective-permute-done.26.refs_1_.refs_2_ = bf16[2,4,56,768]{3,2,1,0:T(8,128)(2,1)} collective-permute-done((bf16[2,4,56,768]{3,2,1,0:T(8,128)(2,1)}, bf16[2,4,56,768]{3,2,1,0:T(8,128)(2,1)}, u32[]{:S(2)}, u32[]{:S(2)}) %collective-permute-start.26) | collective-permute-done | bytes 688160 | tf_op jit(solution)/shard_map/ppermute | solution.py:961
  215.0 2.0 pair_up.3.refs_2_
  220.8 2.1 collective-permute-start.34
  222.9 1.8 add_four.2
  224.7 1.6 tally.6.refs_4_.refs_0_
  228.3 1.9 home.1
  233.3 1.9 collective-permute-start.35
  235.3 1.9 finish.1
  239.2 2.3 collective-permute-start.38
  244.1 2.2 collective-permute-done.38.refs_1_
  (223 shorter events, 44.4 us)
Async XLA Ops:
  0.6 19.2 %copy-start = (bf16[27,64]{1,0:T(8,128)(2,1)S(1)}, bf16[27,64]{1,0:T(8,128)(2,1)}, u32[]{:S(2)}) copy-start(bf16[27,64]{1,0:T(8,128)(2,1)} %param.23) | copy-start | bytes 10372
  3.9 17.8 %collective-permute-start.1 = (bf16[48,1536]{1,0:T(8,128)(2,1)}, bf16[48,1536]{1,0:T(8,128)(2,1)S(1)}, u32[]{:S(2)}, u32[]{:S(2)}) collective-permute-start(bf16[48,1536]{1,0:T(8,128)(2,1)} %get-tuple-element.98.refs_3_), channel_id=1, source_target_pairs={{0,1},{1,2},{2,3},{3,0},{4,5},{5,6},{6,7},{7,4},{8,9},{9,10},{10,1... | collective-permute-start | bytes 442376 | tf_op jit(solution)/shard_map/ppermute | solution.py:955
  7.0 15.2 %collective-permute-start.2 = (bf16[48,1536]{1,0:T(8,128)(2,1)}, bf16[48,1536]{1,0:T(8,128)(2,1)S(1)}, u32[]{:S(2)}, u32[]{:S(2)}) collective-permute-start(bf16[48,1536]{1,0:T(8,128)(2,1)} %get-tuple-element.98.refs_3_), channel_id=1, source_target_pairs={{0,2},{1,3},{2,0},{3,1},{4,6},{5,7},{6,4},{7,5},{8,10},{9,11},{10,... | collective-permute-start | bytes 442376 | tf_op jit(solution)/shard_map/ppermute | solution.py:955
  9.6 12.6 %collective-permute-start.3 = (bf16[48,1536]{1,0:T(8,128)(2,1)}, bf16[48,1536]{1,0:T(8,128)(2,1)S(1)}, u32[]{:S(2)}, u32[]{:S(2)}) collective-permute-start(bf16[48,1536]{1,0:T(8,128)(2,1)} %get-tuple-element.98.refs_3_), channel_id=1, source_target_pairs={{0,3},{1,0},{2,1},{3,2},{4,7},{5,4},{6,5},{7,6},{8,11},{9,8},{10,9... | collective-permute-start | bytes 442376 | tf_op jit(solution)/shard_map/ppermute | solution.py:955
  13.6 17.0 %collective-permute-start = (bf16[2,4,56,768]{3,2,1,0:T(8,128)(2,1)S(1)}, bf16[2,4,56,768]{3,2,1,0:T(8,128)(2,1)S(1)}, u32[]{:S(2)}, u32[]{:S(2)}) collective-permute-start(bf16[2,4,56,768]{3,2,1,0:T(8,128)(2,1)S(1)} %get-tuple-element.100), channel_id=1, source_target_pairs={{0,4},{4,0},{8,12},{12,8},{16,24},{20,28},{24,16},{28,20},{1,5},{5... | collective-permute-start | bytes 2064392 | tf_op jit(solution)/shard_map/ppermute | solution.py:961
  15.1 42.7 %collective-permute-start.10 = (bf16[192,768]{1,0:T(8,128)(2,1)S(1)}, bf16[192,768]{1,0:T(8,128)(2,1)S(1)}, u32[]{:S(2)}, u32[]{:S(2)}) collective-permute-start(bf16[192,768]{1,0:T(8,128)(2,1)S(1)} %copy-done.50), channel_id=1, source_target_pairs={{0,1},{1,2},{2,3},{3,0},{4,5},{5,6},{6,7},{7,4},{8,9},{9,10},{10,1... | collective-permute-start | bytes 884744 | tf_op jit(solution)/shard_map/ppermute | solution.py:955
  21.8 36.1 %collective-permute-start.11 = (bf16[192,768]{1,0:T(8,128)(2,1)S(1)}, bf16[192,768]{1,0:T(8,128)(2,1)S(1)}, u32[]{:S(2)}, u32[]{:S(2)}) collective-permute-start(bf16[192,768]{1,0:T(8,128)(2,1)S(1)} %copy-done.50), channel_id=1, source_target_pairs={{0,2},{1,3},{2,0},{3,1},{4,6},{5,7},{6,4},{7,5},{8,10},{9,11},{10,... | collective-permute-start | bytes 884744 | tf_op jit(solution)/shard_map/ppermute | solution.py:955
  22.2 8.4 %collective-permute-start.4 = (bf16[3,48,1536]{2,1,0:T(8,128)(2,1)S(1)}, bf16[3,48,1536]{2,1,0:T(8,128)(2,1)S(1)}, u32[]{:S(2)}, u32[]{:S(2)}) collective-permute-start(bf16[3,48,1536]{2,1,0:T(8,128)(2,1)S(1)} %join.2.refs_3_), channel_id=1, source_target_pairs={{0,4},{4,0},{8,12},{12,8},{16,24},{20,28},{24,16},{28,20},{1,5},{5... | collective-permute-start | bytes 1327112 | tf_op jit(solution)/shard_map/ppermute | solution.py:961
  30.6 20.5 %collective-permute-start.5 = (bf16[2,4,56,768]{3,2,1,0:T(8,128)(2,1)S(1)}, bf16[2,4,56,768]{3,2,1,0:T(8,128)(2,1)S(1)}, u32[]{:S(2)}, u32[]{:S(2)}) collective-permute-start(bf16[2,4,56,768]{3,2,1,0:T(8,128)(2,1)S(1)} %pair_up.2), channel_id=1, source_target_pairs={{0,8},{4,12},{8,0},{12,4},{16,20},{20,16},{24,28},{28,24},{1,9},{5... | collective-permute-start | bytes 2064392 | tf_op jit(solution)/shard_map/ppermute | solution.py:961
  32.3 14.0 %collective-permute-start.6 = (bf16[3,48,1536]{2,1,0:T(8,128)(2,1)S(1)}, bf16[3,48,1536]{2,1,0:T(8,128)(2,1)S(1)}, u32[]{:S(2)}, u32[]{:S(2)}) collective-permute-start(bf16[3,48,1536]{2,1,0:T(8,128)(2,1)S(1)} %join.2.refs_3_), channel_id=1, source_target_pairs={{0,8},{4,12},{8,0},{12,4},{16,20},{20,16},{24,28},{28,24},{1,9},{5... | collective-permute-start | bytes 1327112 | tf_op jit(solution)/shard_map/ppermute | solution.py:961
  32.9 18.2 %collective-permute-start.7 = (bf16[3,48,1536]{2,1,0:T(8,128)(2,1)S(1)}, bf16[3,48,1536]{2,1,0:T(8,128)(2,1)S(1)}, u32[]{:S(2)}, u32[]{:S(2)}) collective-permute-start(bf16[3,48,1536]{2,1,0:T(8,128)(2,1)S(1)} %collective-permute-done.4.refs_2_.refs_5_.refs_4_), channel_id=1, source_target_pairs={{0,8},{4,12},{8,0},{12,4},{16,20},{20,16},{24,28},{28,24},{1,9},{5... | collective-permute-start | bytes 1327112 | tf_op jit(solution)/shard_map/ppermute | solution.py:961
  34.7 22.0 %copy-start.12 = (f32[224,1]{1,0:T(8,128)}, f32[224,1]{1,0:T(8,128)S(1)}, u32[]{:S(2)}) copy-start(f32[224,1]{1,0:T(8,128)S(1)} %fusion.18.refs_1_.refs_0_) | copy-start | bytes 2692
  34.7 54.6 %copy-start.18 = (bf16[2,128,512]{2,1,0:T(8,128)(2,1)}, bf16[2,128,512]{2,1,0:T(8,128)(2,1)S(1)}, u32[]{:S(2)}) copy-start(bf16[2,128,512]{2,1,0:T(8,128)(2,1)S(1)} %pad_maximum_fusion.refs_5_.refs_6_) | copy-start | bytes 786436
  46.4 19.2 %collective-permute-start.12 = (bf16[192,768]{1,0:T(8,128)(2,1)S(1)}, bf16[192,768]{1,0:T(8,128)(2,1)S(1)}, u32[]{:S(2)}, u32[]{:S(2)}) collective-permute-start(bf16[192,768]{1,0:T(8,128)(2,1)S(1)} %copy-done.50), channel_id=1, source_target_pairs={{0,3},{1,0},{2,1},{3,2},{4,7},{5,4},{6,5},{7,6},{8,11},{9,8},{10,9... | collective-permute-start | bytes 884744 | tf_op jit(solution)/shard_map/ppermute | solution.py:955
  52.0 4.7 %collective-permute-start.8 = (bf16[4,224,768]{2,1,0:T(8,128)(2,1)S(1)}, bf16[4,224,768]{2,1,0:T(8,128)(2,1)S(1)}, u32[]{:S(2)}, u32[]{:S(2)}) collective-permute-start(bf16[4,224,768]{2,1,0:T(8,128)(2,1)S(1)} %weld.1.refs_7_.refs_1_.refs_0_.refs_4_), channel_id=1, source_target_pairs={{0,16},{16,0},{1,17},{17,1},{2,18},{18,2},{3,19},{19,3},{4,20},{20... | collective-permute-start | bytes 4128776 | tf_op jit(solution)/shard_map/ppermute | solution.py:949
  52.3 37.1 %copy-start.23 = (bf16[224,128]{1,0:T(8,128)(2,1)}, bf16[224,128]{1,0:T(8,128)(2,1)S(1)}, u32[]{:S(2)}) copy-start(bf16[224,128]{1,0:T(8,128)(2,1)S(1)} %fusion.22.refs_8_.refs_9_) | copy-start | bytes 172036
  52.4 36.9 %copy-start.15 = (f32[224,512]{1,0:T(8,128)}, f32[224,512]{1,0:T(8,128)S(1)}, u32[]{:S(2)}) copy-start(f32[224,512]{1,0:T(8,128)S(1)} %fusion.refs_6_.refs_7_) | copy-start | bytes 1376260
  55.8 33.6 %copy-start.8 = (bf16[4,4,48,1536]{3,2,1,0:T(8,128)(2,1)}, bf16[4,4,48,1536]{3,2,1,0:T(8,128)(2,1)S(1)}, u32[]{:S(2)}) copy-start(bf16[4,4,48,1536]{3,2,1,0:T(8,128)(2,1)S(1)} %get-tuple-element.102) | copy-start | bytes 7077892
  55.8 13.8 %collective-permute-start.9 = (bf16[384,384]{1,0:T(8,128)(2,1)S(1)}, bf16[384,384]{1,0:T(8,128)(2,1)S(1)}, u32[]{:S(2)}, u32[]{:S(2)}) collective-permute-start(bf16[384,384]{1,0:T(8,128)(2,1)S(1)} %bitcast.55), channel_id=1, source_target_pairs={{0,16},{16,0},{1,17},{17,1},{2,18},{18,2},{3,19},{19,3},{4,20},{20... | collective-permute-start | bytes 884744 | tf_op jit(solution)/shard_map/ppermute | solution.py:949
  56.6 32.7 %copy-start.21 = (bf16[512,128]{1,0:T(8,128)(2,1)}, bf16[512,128]{1,0:T(8,128)(2,1)S(1)}, u32[]{:S(2)}) copy-start(bf16[512,128]{1,0:T(8,128)(2,1)S(1)} %fusion.1.refs_7_.refs_8_) | copy-start | bytes 393220
  57.8 31.6 %copy-start.4 = (bf16[4,224,768]{2,1,0:T(8,128)(2,1)}, bf16[4,224,768]{2,1,0:T(8,128)(2,1)S(1)}, u32[]{:S(2)}) copy-start(bf16[4,224,768]{2,1,0:T(8,128)(2,1)S(1)} %norm_one.1.refs_3_.refs_1_) | copy-start | bytes 4128772
  66.6 22.8 %collective-permute-start.13 = (bf16[3,192,768]{2,1,0:T(8,128)(2,1)}, bf16[3,192,768]{2,1,0:T(8,128)(2,1)S(1)}, u32[]{:S(2)}, u32[]{:S(2)}) collective-permute-start(bf16[3,192,768]{2,1,0:T(8,128)(2,1)} %join.3.refs_10_.refs_3_), channel_id=1, source_target_pairs={{0,4},{4,0},{8,12},{12,8},{16,24},{20,28},{24,16},{28,20},{1,5},{5... | collective-permute-start | bytes 2654216 | tf_op jit(solution)/shard_map/ppermute | solution.py:961
  68.1 33.8 %collective-permute-start.15 = (bf16[3,192,768]{2,1,0:T(8,128)(2,1)}, bf16[3,192,768]{2,1,0:T(8,128)(2,1)}, u32[]{:S(2)}, u32[]{:S(2)}) collective-permute-start(bf16[3,192,768]{2,1,0:T(8,128)(2,1)} %join.3.refs_10_.refs_3_), channel_id=1, source_target_pairs={{0,8},{4,12},{8,0},{12,4},{16,20},{20,16},{24,28},{28,24},{1,9},{5... | collective-permute-start | bytes 2654216 | tf_op jit(solution)/shard_map/ppermute | solution.py:961
  69.6 19.8 %copy-start.28 = (bf16[384,384]{1,0:T(8,128)(2,1)}, bf16[384,384]{1,0:T(8,128)(2,1)S(1)}, u32[]{:S(2)}) copy-start(bf16[384,384]{1,0:T(8,128)(2,1)S(1)} %collective-permute-done.9.refs_3_.refs_5_) | copy-start | bytes 884740
  89.4 13.0 %collective-permute-start.16 = (bf16[3,192,768]{2,1,0:T(8,128)(2,1)S(1)}, bf16[3,192,768]{2,1,0:T(8,128)(2,1)S(1)}, u32[]{:S(2)}, u32[]{:S(2)}) collective-permute-start(bf16[3,192,768]{2,1,0:T(8,128)(2,1)S(1)} %collective-permute-done.13.refs_14_.refs_4_), channel_id=1, source_target_pairs={{0,8},{4,12},{8,0},{12,4},{16,20},{20,16},{24,28},{28,24},{1,9},{5... | collective-permute-start | bytes 2654216 | tf_op jit(solution)/shard_map/ppermute | solution.py:961
  101.8 3.8 %collective-permute-start.14 = (bf16[4,224,768]{2,1,0:T(8,128)(2,1)S(1)}, bf16[4,224,768]{2,1,0:T(8,128)(2,1)S(1)}, u32[]{:S(2)}, u32[]{:S(2)}) collective-permute-start(bf16[4,224,768]{2,1,0:T(8,128)(2,1)S(1)} %get-tuple-element.112), channel_id=1, source_target_pairs={{0,16},{16,0},{1,17},{17,1},{2,18},{18,2},{3,19},{19,3},{4,20},{20... | collective-permute-start | bytes 4128776 | tf_op jit(solution)/shard_map/ppermute | solution.py:949
  115.9 16.5 %collective-permute-start.18 = (bf16[2,2,96,1536]{3,2,1,0:T(8,128)(2,1)}, bf16[2,2,96,1536]{3,2,1,0:T(8,128)(2,1)}, u32[]{:S(2)}, u32[]{:S(2)}) collective-permute-start(bf16[2,2,96,1536]{3,2,1,0:T(8,128)(2,1)} %get-tuple-element.116.refs_4_), channel_id=1, source_target_pairs={{0,4},{4,0},{8,12},{12,8},{16,24},{20,28},{24,16},{28,20},{1,5},{5... | collective-permute-start | bytes 3538952 | tf_op jit(solution)/shard_map/ppermute | solution.py:961
  125.7 10.6 %collective-permute-start.17 = (bf16[4,224,768]{2,1,0:T(8,128)(2,1)}, bf16[4,224,768]{2,1,0:T(8,128)(2,1)}, u32[]{:S(2)}, u32[]{:S(2)}) collective-permute-start(bf16[4,224,768]{2,1,0:T(8,128)(2,1)} %get-tuple-element.118), channel_id=1, source_target_pairs={{0,16},{16,0},{1,17},{17,1},{2,18},{18,2},{3,19},{19,3},{4,20},{20... | collective-permute-start | bytes 4128776 | tf_op jit(solution)/shard_map/ppermute | solution.py:949
  130.2 22.8 %collective-permute-start.19 = (bf16[2,2,96,1536]{3,2,1,0:T(8,128)(2,1)}, bf16[2,2,96,1536]{3,2,1,0:T(8,128)(2,1)}, u32[]{:S(2)}, u32[]{:S(2)}) collective-permute-start(bf16[2,2,96,1536]{3,2,1,0:T(8,128)(2,1)} %get-tuple-element.122.refs_2_), channel_id=1, source_target_pairs={{0,4},{4,0},{8,12},{12,8},{16,24},{20,28},{24,16},{28,20},{1,5},{5... | collective-permute-start | bytes 3538952 | tf_op jit(solution)/shard_map/ppermute | solution.py:961
  134.7 22.0 %collective-permute-start.20 = (bf16[2,4,24,1536]{3,2,1,0:T(8,128)(2,1)}, bf16[2,4,24,1536]{3,2,1,0:T(8,128)(2,1)}, u32[]{:S(2)}, u32[]{:S(2)}) collective-permute-start(bf16[2,4,24,1536]{3,2,1,0:T(8,128)(2,1)} %get-tuple-element.123.refs_6_), channel_id=1, source_target_pairs={{0,8},{4,12},{8,0},{12,4},{16,20},{20,16},{24,28},{28,24},{1,9},{5... | collective-permute-start | bytes 1769480 | tf_op jit(solution)/shard_map/ppermute | solution.py:961
  155.3 16.4 %collective-permute-start.21 = (bf16[2,4,24,1536]{3,2,1,0:T(8,128)(2,1)}, bf16[2,4,24,1536]{3,2,1,0:T(8,128)(2,1)}, u32[]{:S(2)}, u32[]{:S(2)}) collective-permute-start(bf16[2,4,24,1536]{3,2,1,0:T(8,128)(2,1)} %get-tuple-element.128.refs_11_), channel_id=1, source_target_pairs={{0,8},{4,12},{8,0},{12,4},{16,20},{20,16},{24,28},{28,24},{1,9},{5... | collective-permute-start | bytes 1769480 | tf_op jit(solution)/shard_map/ppermute | solution.py:961
  171.2 18.0 %collective-permute-start.25 = (bf16[2,2,96,1536]{3,2,1,0:T(8,128)(2,1)}, bf16[2,2,96,1536]{3,2,1,0:T(8,128)(2,1)}, u32[]{:S(2)}, u32[]{:S(2)}) collective-permute-start(bf16[2,2,96,1536]{3,2,1,0:T(8,128)(2,1)} %get-tuple-element.133.refs_5_), channel_id=1, source_target_pairs={{0,4},{4,0},{8,12},{12,8},{16,24},{20,28},{24,16},{28,20},{1,5},{5... | collective-permute-start | bytes 3538952 | tf_op jit(solution)/shard_map/ppermute | solution.py:961
  178.0 19.0 %collective-permute-start.24 = (bf16[2,2,2,24,1536]{4,3,2,1,0:T(8,128)(2,1)}, bf16[2,2,2,24,1536]{4,3,2,1,0:T(8,128)(2,1)}, u32[]{:S(2)}, u32[]{:S(2)}) collective-permute-start(bf16[2,2,2,24,1536]{4,3,2,1,0:T(8,128)(2,1)} %get-tuple-element.134.refs_2_), channel_id=1, source_target_pairs={{0,1},{1,0},{2,3},{3,2},{4,5},{5,4},{6,7},{7,6},{8,9},{9,8},{10,11... | collective-permute-start | bytes 1769480 | tf_op jit(solution)/shard_map/ppermute | solution.py:958
  188.7 11.2 %collective-permute-start.22 = (bf16[2,224,768]{2,1,0:T(8,128)(2,1)}, bf16[2,224,768]{2,1,0:T(8,128)(2,1)}, u32[]{:S(2)}, u32[]{:S(2)}) collective-permute-start(bf16[2,224,768]{2,1,0:T(8,128)(2,1)} %get-tuple-element.136.refs_2_), channel_id=1, source_target_pairs={{0,16},{16,0},{1,17},{17,1},{2,18},{18,2},{3,19},{19,3},{4,20},{20... | collective-permute-start | bytes 2064392 | tf_op jit(solution)/shard_map/ppermute | solution.py:949
  188.7 11.1 %collective-permute-start.23 = (bf16[2,224,768]{2,1,0:T(8,128)(2,1)}, bf16[2,224,768]{2,1,0:T(8,128)(2,1)}, u32[]{:S(2)}, u32[]{:S(2)}) collective-permute-start(bf16[2,224,768]{2,1,0:T(8,128)(2,1)} %get-tuple-element.139.refs_2_), channel_id=1, source_target_pairs={{0,16},{16,0},{1,17},{17,1},{2,18},{18,2},{3,19},{19,3},{4,20},{20... | collective-permute-start | bytes 2064392 | tf_op jit(solution)/shard_map/ppermute | solution.py:949
  191.5 14.0 %collective-permute-start.27 = (bf16[2,4,24,1536]{3,2,1,0:T(8,128)(2,1)}, bf16[2,4,24,1536]{3,2,1,0:T(8,128)(2,1)}, u32[]{:S(2)}, u32[]{:S(2)}) collective-permute-start(bf16[2,4,24,1536]{3,2,1,0:T(8,128)(2,1)} %get-tuple-element.142.refs_2_), channel_id=1, source_target_pairs={{0,8},{4,12},{8,0},{12,4},{16,20},{20,16},{24,28},{28,24},{1,9},{5... | collective-permute-start | bytes 1769480 | tf_op jit(solution)/shard_map/ppermute | solution.py:961
  199.0 23.9 %collective-permute-start.31 = (bf16[2,2,24,1536]{3,2,1,0:T(8,128)(2,1)}, bf16[2,2,24,1536]{3,2,1,0:T(8,128)(2,1)}, u32[]{:S(2)}, u32[]{:S(2)}) collective-permute-start(bf16[2,2,24,1536]{3,2,1,0:T(8,128)(2,1)} %get-tuple-element.143.refs_11_), channel_id=1, source_target_pairs={{0,2},{1,3},{2,0},{3,1},{4,6},{5,7},{6,4},{7,5},{8,10},{9,11},{10,... | collective-permute-start | bytes 884744 | tf_op jit(solution)/shard_map/ppermute | solution.py:958
  203.8 11.3 %collective-permute-start.26 = (bf16[2,4,56,768]{3,2,1,0:T(8,128)(2,1)}, bf16[2,4,56,768]{3,2,1,0:T(8,128)(2,1)}, u32[]{:S(2)}, u32[]{:S(2)}) collective-permute-start(bf16[2,4,56,768]{3,2,1,0:T(8,128)(2,1)} %get-tuple-element.145), channel_id=1, source_target_pairs={{0,4},{4,0},{8,12},{12,8},{16,24},{20,28},{24,16},{28,20},{1,5},{5... | collective-permute-start | bytes 2064392 | tf_op jit(solution)/shard_map/ppermute | solution.py:961
  205.4 12.5 %collective-permute-start.29 = (f32[32,768]{1,0:T(8,128)S(1)}, f32[32,768]{1,0:T(8,128)S(1)}, u32[]{:S(2)}, u32[]{:S(2)}) collective-permute-start(f32[32,768]{1,0:T(8,128)S(1)} %small.1.refs_3_.refs_0_), channel_id=1, source_target_pairs={{0,16},{16,0},{1,17},{17,1},{2,18},{18,2},{3,19},{19,3},{4,20},{20... | collective-permute-start | bytes 294920 | tf_op jit(solution)/shard_map/ppermute | solution.py:949
  206.7 13.3 %collective-permute-start.32 = (bf16[2,1,2,24,1536]{4,3,2,1,0:T(8,128)(2,1)S(1)}, bf16[2,1,2,24,1536]{4,3,2,1,0:T(8,128)(2,1)S(1)}, u32[]{:S(2)}, u32[]{:S(2)}) collective-permute-start(bf16[2,1,2,24,1536]{4,3,2,1,0:T(8,128)(2,1)S(1)} %get-tuple-element.155.refs_2_), channel_id=1, source_target_pairs={{0,1},{1,0},{2,3},{3,2},{4,5},{5,4},{6,7},{7,6},{8,9},{9,8},{10,11... | collective-permute-start | bytes 884744 | tf_op jit(solution)/shard_map/ppermute | solution.py:958
  217.0 11.3 %collective-permute-start.28 = (bf16[2,4,56,768]{3,2,1,0:T(8,128)(2,1)}, bf16[2,4,56,768]{3,2,1,0:T(8,128)(2,1)}, u32[]{:S(2)}, u32[]{:S(2)}) collective-permute-start(bf16[2,4,56,768]{3,2,1,0:T(8,128)(2,1)} %pair_up.3.refs_2_), channel_id=1, source_target_pairs={{0,8},{4,12},{8,0},{12,4},{16,20},{20,16},{24,28},{28,24},{1,9},{5... | collective-permute-start | bytes 2064392 | tf_op jit(solution)/shard_map/ppermute | solution.py:961
  218.6 6.1 %collective-permute-start.30 = (f32[32,768]{1,0:T(8,128)}, f32[32,768]{1,0:T(8,128)}, u32[]{:S(2)}, u32[]{:S(2)}) collective-permute-start(f32[32,768]{1,0:T(8,128)} %tally.5.refs_2_.refs_0_), channel_id=1, source_target_pairs={{0,4},{4,0},{8,12},{12,8},{1,5},{5,1},{9,13},{13,9},{2,6},{6,2},{1... | collective-permute-start | bytes 294920 | tf_op jit(solution)/shard_map/ppermute | solution.py:952
  220.8 9.9 %collective-permute-start.34 = (bf16[1,2,24,1536]{3,2,1,0:T(8,128)(2,1)}, bf16[1,2,24,1536]{3,2,1,0:T(8,128)(2,1)}, u32[]{:S(2)}, u32[]{:S(2)}) collective-permute-start(bf16[1,2,24,1536]{3,2,1,0:T(8,128)(2,1)} %get-tuple-element.158.refs_3_), channel_id=1, source_target_pairs={{0,2},{1,3},{2,0},{3,1},{4,6},{5,7},{6,4},{7,5},{8,10},{9,11},{10,... | collective-permute-start | bytes 442376 | tf_op jit(solution)/shard_map/ppermute | solution.py:958
  224.7 10.6 %collective-permute-start.36 = (f32[2,24,1536]{2,1,0:T(8,128)}, f32[2,24,1536]{2,1,0:T(8,128)}, u32[]{:S(2)}, u32[]{:S(2)}) collective-permute-start(f32[2,24,1536]{2,1,0:T(8,128)} %get-tuple-element.159.refs_2_), channel_id=1, source_target_pairs={{0,16},{16,0},{1,17},{17,1},{2,18},{18,2},{3,19},{19,3},{4,20},{20... | collective-permute-start | bytes 884744 | tf_op jit(solution)/shard_map/ppermute | solution.py:949
  226.3 6.1 %collective-permute-start.33 = (f32[32,768]{1,0:T(8,128)}, f32[32,768]{1,0:T(8,128)}, u32[]{:S(2)}, u32[]{:S(2)}) collective-permute-start(f32[32,768]{1,0:T(8,128)} %tally.6.refs_4_.refs_0_), channel_id=1, source_target_pairs={{0,8},{4,12},{8,0},{12,4},{1,9},{5,13},{9,1},{13,5},{2,10},{6,14},... | collective-permute-start | bytes 294920 | tf_op jit(solution)/shard_map/ppermute | solution.py:952
  231.9 3.4 %collective-permute-start.37 = (f32[1,24,1536]{2,1,0:T(8,128)S(1)}, f32[1,24,1536]{2,1,0:T(8,128)S(1)}, u32[]{:S(2)}, u32[]{:S(2)}) collective-permute-start(f32[1,24,1536]{2,1,0:T(8,128)S(1)} %get-tuple-element.163.refs_2_), channel_id=1, source_target_pairs={{0,16},{16,0},{1,17},{17,1},{2,18},{18,2},{3,19},{19,3},{4,20},{20... | collective-permute-start | bytes 442376 | tf_op jit(solution)/shard_map/ppermute | solution.py:949
  233.3 4.9 %collective-permute-start.35 = (f32[32,768]{1,0:T(8,128)S(1)}, f32[32,768]{1,0:T(8,128)S(1)}, u32[]{:S(2)}, u32[]{:S(2)}) collective-permute-start(f32[32,768]{1,0:T(8,128)S(1)} %tally.7.refs_5_.refs_0_), channel_id=1, source_target_pairs={{0,1},{1,0},{2,3},{3,2},{4,5},{5,4},{6,7},{7,6},{8,9},{9,8},{10,11... | collective-permute-start | bytes 294920 | tf_op jit(solution)/shard_map/ppermute | solution.py:958
  239.2 7.1 %collective-permute-start.38 = (f32[32,768]{1,0:T(8,128)S(1)}, f32[32,768]{1,0:T(8,128)S(1)}, u32[]{:S(2)}, u32[]{:S(2)}) collective-permute-start(f32[32,768]{1,0:T(8,128)S(1)} %tally.8.refs_0_), channel_id=1, source_target_pairs={{0,2},{1,3},{2,0},{3,1},{4,6},{5,7},{6,4},{7,5},{8,10},{9,11},{10,... | collective-permute-start | bytes 294920 | tf_op jit(solution)/shard_map/ppermute | solution.py:958
  (43 other events, 228.6 us)
